TPU v7x, 512 devices: a whole 4x4x16 slice. The times are simulated.
512 devices in a mesh: seq: 32 (over z, core), head: 16 (over y, x).
Axes of the slice: x: 4, y: 4, z: 16, core: 2. Of those that a mesh axis runs over, the one named last changes fastest.
Arguments:
- light_query: bfloat16 [8192, 8192], P('seq', 'head'), may hold values from -6 to 6
- light_keys: bfloat16 [8192, 8192], P('seq', 'head'), may hold values from -6 to 6
- light_values: bfloat16 [8192, 8192], P('seq', 'head'), may hold values from -6 to 6
- log_decay: float32 [64, 8192], P('head', 'seq'), may hold values from -1.45 to 0, as said below
- light_gain: float32 [8192], P('head'), may hold values from 0.25 to 1.75
- query2: bfloat16 [8192, 8192], P('seq', 'head'), may hold values from -80 to 80
- keys2: bfloat16 [8192, 1024], P('seq'), may hold values from -4 to 4
- values2: bfloat16 [8192, 1024], P('seq'), may hold values from -6 to 6
Outputs:
- light_out: bfloat16 [8192, 8192], P('seq', 'head')
- soft_out: bfloat16 [8192, 8192], P('seq', 'head')
Inputs may be any that keep to these rules, and one draw needn't show every extreme that they name: `log_decay`: strictly negative.
All inputs are finite; a program needn't handle non-finite values.
Results may differ from a plain program's by a relative error of at most 0.0095.
Values may be sent and summed in bfloat16 or wider, within the bound.
No kernel may reach another device: no remote copies, remote signals or barrier semaphores. Data moves between devices by JAX's collectives and lax.ppermute only.
A program may use at most 64 MiB of HBM per device.

v0:
```python
import jax
import jax.numpy as jnp
from jax import lax
from jax.sharding import PartitionSpec as P

HEADS = 64
HD = 128
KVH = 8
BLOCK = 256


def carried_in(value, axis, combine, identity):
    size, index = (lax.axis_size(axis), lax.axis_index(axis))
    everything = jax.tree.map(
        lambda part, kind: lax.all_gather(part.astype(kind), axis),
        value,
        (jnp.bfloat16, jnp.bfloat16),
    )
    start = jax.tree.map(
        lambda part, zero: jnp.broadcast_to(jnp.asarray(zero, part.dtype), part.shape),
        value,
        identity,
    )

    def step(k, before):
        reached = k < index
        new = combine(
            before, jax.tree.map(lambda part, own: part[k].astype(own.dtype), everything, value)
        )
        return jax.tree.map(lambda a, b: jnp.where(reached, a, b), new, before)

    return lax.fori_loop(0, size, step, start)


def prefix_combine(earlier, later):
    return (earlier[0] + later[0], jnp.exp(later[0])[:, None, None] * earlier[1] + later[1])


def local(light_query, light_keys, light_values, log_decay, light_gain, query2, keys2, values2):
    highest = lax.Precision.HIGHEST
    local_rows = light_query.shape[0]
    heads_here = log_decay.shape[0]
    nblocks = local_rows // BLOCK
    queries = light_query.reshape(nblocks, BLOCK, heads_here, HD)
    keys_here = light_keys.reshape(nblocks, BLOCK, heads_here, HD)
    values_here = light_values.reshape(nblocks, BLOCK, heads_here, HD)
    decays = log_decay.reshape(heads_here, nblocks, BLOCK).transpose(1, 0, 2)
    running = jnp.cumsum(decays, axis=2)
    lower = jnp.tril(jnp.ones((BLOCK, BLOCK), dtype=bool))
    scores = jnp.einsum("bihd,bjhd->bhij", queries, keys_here, preferred_element_type=jnp.float32)
    spread = jnp.where(lower, running[:, :, :, None] - running[:, :, None, :], 0.0)
    weighted = jnp.where(lower, scores * jnp.exp(spread), 0.0).astype(jnp.bfloat16)
    within = jnp.einsum(
        "bhij,bjhd->bihd", weighted, values_here, preferred_element_type=jnp.float32
    )
    tail = jnp.exp(running[:, :, -1:] - running)
    scaled_keys = (keys_here.astype(jnp.float32) * tail.transpose(0, 2, 1)[:, :, :, None]).astype(
        jnp.bfloat16
    )
    block_state = jnp.einsum(
        "bjhd,bjhe->bhde", scaled_keys, values_here, preferred_element_type=jnp.float32
    )
    block_decay = running[:, :, -1]
    total_decay = jnp.sum(block_decay, axis=0)
    suffix = total_decay[None, :] - jnp.cumsum(block_decay, axis=0)
    total_state = jnp.einsum("bh,bhde->hde", jnp.exp(suffix), block_state, precision=highest)
    identity = (jnp.zeros_like(total_decay), jnp.zeros_like(total_state))
    earlier_decay, start_state = carried_in(
        (total_decay, total_state), "seq", prefix_combine, identity
    )

    def advance(state, item):
        decay_one, state_one = item
        return (jnp.exp(decay_one)[:, None, None] * state + state_one, state)

    _, starts = lax.scan(advance, start_state, (block_decay, block_state))
    lifted = queries.astype(jnp.float32) * jnp.exp(running).transpose(0, 2, 1)[:, :, :, None]
    across = jnp.einsum("bihd,bhde->bihe", lifted, starts, precision=highest)
    mixed = within + across
    normed = mixed * lax.rsqrt(jnp.mean(mixed * mixed, axis=-1, keepdims=True) + 1e-06)
    light_out = (normed.reshape(local_rows, heads_here * HD) * light_gain).astype(jnp.bfloat16)
    own_head = lax.axis_index("head")
    kv_local = max(1, KVH // lax.axis_size("head"))
    group_width = HEADS // KVH
    first_kv = own_head * heads_here // group_width
    key_rows = lax.dynamic_slice_in_dim(keys2, first_kv * HD, kv_local * HD, 1)
    value_rows = lax.dynamic_slice_in_dim(values2, first_kv * HD, kv_local * HD, 1)
    grouped = heads_here // kv_local
    scale = HD ** (-0.5)
    own_shard = lax.axis_index("seq")
    groups = [(query2, own_shard * local_rows + jnp.arange(local_rows, dtype=jnp.int32))]
    group_heads = [
        rows.reshape(rows.shape[0], kv_local, grouped, HD) for rows, device_slots in groups
    ]
    group_places = [device_slots for rows, device_slots in groups]

    def attend(carry, query_heads, query_pos, key_part, value_part, key_start):
        peak, total, summed = carry
        part_rows = key_part.shape[0]
        key_heads = key_part.reshape(part_rows, kv_local, HD)
        value_heads = value_part.reshape(part_rows, kv_local, HD)
        logits = (
            jnp.einsum("tkgd,skd->kgts", query_heads, key_heads, preferred_element_type=jnp.float32)
            * scale
        )
        key_pos = key_start + jnp.arange(part_rows, dtype=jnp.int32)
        allowed = key_pos[None, :] <= query_pos[:, None]
        new_peak = jnp.maximum(peak, jnp.max(jnp.where(allowed, logits, -jnp.inf), axis=-1))
        probs = jnp.where(allowed, jnp.exp(logits - new_peak[:, :, :, None]), 0.0)
        factor = jnp.exp(peak - new_peak)
        total = factor * total + jnp.sum(probs, axis=-1)
        update = jnp.einsum(
            "kgts,skd->kgtd",
            probs.astype(jnp.bfloat16),
            value_heads,
            preferred_element_type=jnp.float32,
        )
        summed = factor[:, :, :, None] * summed + update
        return (new_peak, total, summed)

    initial = tuple(
        (
            (
                jnp.full((kv_local, grouped, device_slots.shape[0]), -1e30, jnp.float32),
                jnp.zeros((kv_local, grouped, device_slots.shape[0]), jnp.float32),
                jnp.zeros((kv_local, grouped, device_slots.shape[0], HD), jnp.float32),
            )
            for device_slots in group_places
        )
    )
    key_part = lax.all_gather(key_rows, "seq", axis=0, tiled=True)
    value_part = lax.all_gather(value_rows, "seq", axis=0, tiled=True)
    piece_rows = key_part.shape[0]
    sub_rows = 512
    sub_count = piece_rows // sub_rows

    def one_sub(index, inner):
        offset = index * sub_rows
        key_sub = lax.dynamic_slice_in_dim(key_part, offset, sub_rows, 0)
        value_sub = lax.dynamic_slice_in_dim(value_part, offset, sub_rows, 0)
        query_heads = group_heads[0]
        query_pos = group_places[0]

        def live(state, query_heads=query_heads, query_pos=query_pos):
            return attend(state, query_heads, query_pos, key_sub, value_sub, offset)

        def skipped(state):
            return state

        results = [lax.cond(offset <= query_pos[-1], live, skipped, inner[0])]
        return tuple(results)

    finished = lax.fori_loop(0, sub_count, one_sub, initial)
    outputs = []
    for peak, total, summed in finished:
        outputs.append(
            (summed / total[:, :, :, None])
            .transpose(2, 0, 1, 3)
            .reshape(summed.shape[2], heads_here * HD)
            .astype(jnp.bfloat16)
        )
    soft_out = outputs[0]
    return (light_out, soft_out)


def solution(mesh):
    placed = (
        P("seq", "head"),
        P("seq", "head"),
        P("seq", "head"),
        P("head", "seq"),
        P("head"),
        P("seq", "head"),
        P("seq", None),
        P("seq", None),
    )
    return jax.shard_map(
        local,
        mesh=mesh,
        in_specs=placed,
        out_specs=(P("seq", "head"), P("seq", "head")),
        check_vma=False,
    )
```

profile of v0, /device:TPU:481, one launch (start us, length us, event | category | flops | bytes accessed | tf_op | source)
XLA Modules:
  0.0 276.4 jit_solution(12271863843769052138)
XLA Ops:
  14.0 1.8 fusion.28
  16.2 26.8 %all-gather = bf16[32,4,1]{1,2,0:T(2,128)(2,1)S(1)} all-gather(bf16[1,4,1]{1,2,0:T(2,128)(2,1)S(1)} %slice.27), channel_id=2, replica_groups=mesh['seq'=32,'head'=16] {'seq'}, dimensions={0}, use_global_device_ids=true | all-gather | bytes 264 | tf_op jit(solution)/shard_map/all_gather | solution.py:15
  43.5 37.1 %all-gather.6.cloned.1.call-done = bf16[8192,128]{1,0:T(8,128)(2,1)} async-done(((bf16[256,128]{1,0:T(8,128)(2,1)}), bf16[8192,128]{1,0:T(8,128)(2,1)}) %all-gather.6.cloned.1.call-update) | async-done | bytes 2097168 | tf_op jit(solution)/shard_map/all_gather | solution.py:131
  80.6 70.9 %all-gather.8.cloned.1.call-done = bf16[8192,128]{1,0:T(8,128)(2,1)} async-done(((bf16[256,128]{1,0:T(8,128)(2,1)}), bf16[8192,128]{1,0:T(8,128)(2,1)}) %all-gather.8.cloned.1.call-update) | async-done | bytes 2097168 | tf_op jit(solution)/shard_map/all_gather | solution.py:132
  151.5 80.9 %while.36 = (s32[]{:T(128)}, f32[1,4,256]{2,1,0:T(4,128)S(1)}, f32[1,4,256]{2,1,0:T(4,128)S(1)}, f32[1,4,256,128]{3,2,1,0:T(8,128)S(1)}, s32[256]{0:T(256)S(1)},...) while((s32[]{:T(128)}, f32[1,4,256]{2,1,0:T(4,128)S(1)}, ...), condition=%wide.region_10.11_spmd, body=%wide.region_5.10_spmd.sunk | while | flops 274599424 | bytes 8459565 | solution.py:153
  152.8 3.8 %conditional.2 = ((f32[1,4,256]{2,1,0:T(4,128)S(1)}, f32[1,4,256]{2,1,0:T(4,128)S(1)}, f32[1,4,256,128]{3,2,1,0:T(8,128)S(1)})) conditional(s32[]{:T(128)} %convert_element_type.129, (f32[1,4,256]{2,1,0:T(4,128)S(1)}, f32[1,4,256]{2,1,0:T(4,128)S(1)}, f32[1,4,256,128]{3,2,1,0:T(8,128)S(1)}) %tuple.87, (s32[]{:T(128)}, s32[256]{0:T(256)S(1)}, ...), branch_computations={%region_6.6_spmd, %region_7.9_spmd} | conditional | flops 274599424 | bytes 8459342 | solution.py:150
  157.8 3.8 %conditional.2 = ((f32[1,4,256]{2,1,0:T(4,128)S(1)}, f32[1,4,256]{2,1,0:T(4,128)S(1)}, f32[1,4,256,128]{3,2,1,0:T(8,128)S(1)})) conditional(s32[]{:T(128)} %convert_element_type.129, (f32[1,4,256]{2,1,0:T(4,128)S(1)}, f32[1,4,256]{2,1,0:T(4,128)S(1)}, f32[1,4,256,128]{3,2,1,0:T(8,128)S(1)}) %tuple.87, (s32[]{:T(128)}, s32[256]{0:T(256)S(1)}, ...), branch_computations={%region_6.6_spmd, %region_7.9_spmd} | conditional | flops 274599424 | bytes 8459342 | solution.py:150
  162.9 3.8 %conditional.2 = ((f32[1,4,256]{2,1,0:T(4,128)S(1)}, f32[1,4,256]{2,1,0:T(4,128)S(1)}, f32[1,4,256,128]{3,2,1,0:T(8,128)S(1)})) conditional(s32[]{:T(128)} %convert_element_type.129, (f32[1,4,256]{2,1,0:T(4,128)S(1)}, f32[1,4,256]{2,1,0:T(4,128)S(1)}, f32[1,4,256,128]{3,2,1,0:T(8,128)S(1)}) %tuple.87, (s32[]{:T(128)}, s32[256]{0:T(256)S(1)}, ...), branch_computations={%region_6.6_spmd, %region_7.9_spmd} | conditional | flops 274599424 | bytes 8459342 | solution.py:150
  167.9 3.8 %conditional.2 = ((f32[1,4,256]{2,1,0:T(4,128)S(1)}, f32[1,4,256]{2,1,0:T(4,128)S(1)}, f32[1,4,256,128]{3,2,1,0:T(8,128)S(1)})) conditional(s32[]{:T(128)} %convert_element_type.129, (f32[1,4,256]{2,1,0:T(4,128)S(1)}, f32[1,4,256]{2,1,0:T(4,128)S(1)}, f32[1,4,256,128]{3,2,1,0:T(8,128)S(1)}) %tuple.87, (s32[]{:T(128)}, s32[256]{0:T(256)S(1)}, ...), branch_computations={%region_6.6_spmd, %region_7.9_spmd} | conditional | flops 274599424 | bytes 8459342 | solution.py:150
  173.0 3.8 %conditional.2 = ((f32[1,4,256]{2,1,0:T(4,128)S(1)}, f32[1,4,256]{2,1,0:T(4,128)S(1)}, f32[1,4,256,128]{3,2,1,0:T(8,128)S(1)})) conditional(s32[]{:T(128)} %convert_element_type.129, (f32[1,4,256]{2,1,0:T(4,128)S(1)}, f32[1,4,256]{2,1,0:T(4,128)S(1)}, f32[1,4,256,128]{3,2,1,0:T(8,128)S(1)}) %tuple.87, (s32[]{:T(128)}, s32[256]{0:T(256)S(1)}, ...), branch_computations={%region_6.6_spmd, %region_7.9_spmd} | conditional | flops 274599424 | bytes 8459342 | solution.py:150
  178.1 3.8 %conditional.2 = ((f32[1,4,256]{2,1,0:T(4,128)S(1)}, f32[1,4,256]{2,1,0:T(4,128)S(1)}, f32[1,4,256,128]{3,2,1,0:T(8,128)S(1)})) conditional(s32[]{:T(128)} %convert_element_type.129, (f32[1,4,256]{2,1,0:T(4,128)S(1)}, f32[1,4,256]{2,1,0:T(4,128)S(1)}, f32[1,4,256,128]{3,2,1,0:T(8,128)S(1)}) %tuple.87, (s32[]{:T(128)}, s32[256]{0:T(256)S(1)}, ...), branch_computations={%region_6.6_spmd, %region_7.9_spmd} | conditional | flops 274599424 | bytes 8459342 | solution.py:150
  183.1 3.8 %conditional.2 = ((f32[1,4,256]{2,1,0:T(4,128)S(1)}, f32[1,4,256]{2,1,0:T(4,128)S(1)}, f32[1,4,256,128]{3,2,1,0:T(8,128)S(1)})) conditional(s32[]{:T(128)} %convert_element_type.129, (f32[1,4,256]{2,1,0:T(4,128)S(1)}, f32[1,4,256]{2,1,0:T(4,128)S(1)}, f32[1,4,256,128]{3,2,1,0:T(8,128)S(1)}) %tuple.87, (s32[]{:T(128)}, s32[256]{0:T(256)S(1)}, ...), branch_computations={%region_6.6_spmd, %region_7.9_spmd} | conditional | flops 274599424 | bytes 8459342 | solution.py:150
  188.2 3.8 %conditional.2 = ((f32[1,4,256]{2,1,0:T(4,128)S(1)}, f32[1,4,256]{2,1,0:T(4,128)S(1)}, f32[1,4,256,128]{3,2,1,0:T(8,128)S(1)})) conditional(s32[]{:T(128)} %convert_element_type.129, (f32[1,4,256]{2,1,0:T(4,128)S(1)}, f32[1,4,256]{2,1,0:T(4,128)S(1)}, f32[1,4,256,128]{3,2,1,0:T(8,128)S(1)}) %tuple.87, (s32[]{:T(128)}, s32[256]{0:T(256)S(1)}, ...), branch_computations={%region_6.6_spmd, %region_7.9_spmd} | conditional | flops 274599424 | bytes 8459342 | solution.py:150
  189.8 1.7 fusion.5
  193.2 3.8 %conditional.2 = ((f32[1,4,256]{2,1,0:T(4,128)S(1)}, f32[1,4,256]{2,1,0:T(4,128)S(1)}, f32[1,4,256,128]{3,2,1,0:T(8,128)S(1)})) conditional(s32[]{:T(128)} %convert_element_type.129, (f32[1,4,256]{2,1,0:T(4,128)S(1)}, f32[1,4,256]{2,1,0:T(4,128)S(1)}, f32[1,4,256,128]{3,2,1,0:T(8,128)S(1)}) %tuple.87, (s32[]{:T(128)}, s32[256]{0:T(256)S(1)}, ...), branch_computations={%region_6.6_spmd, %region_7.9_spmd} | conditional | flops 274599424 | bytes 8459342 | solution.py:150
  194.8 1.7 fusion.5
  198.3 3.8 %conditional.2 = ((f32[1,4,256]{2,1,0:T(4,128)S(1)}, f32[1,4,256]{2,1,0:T(4,128)S(1)}, f32[1,4,256,128]{3,2,1,0:T(8,128)S(1)})) conditional(s32[]{:T(128)} %convert_element_type.129, (f32[1,4,256]{2,1,0:T(4,128)S(1)}, f32[1,4,256]{2,1,0:T(4,128)S(1)}, f32[1,4,256,128]{3,2,1,0:T(8,128)S(1)}) %tuple.87, (s32[]{:T(128)}, s32[256]{0:T(256)S(1)}, ...), branch_computations={%region_6.6_spmd, %region_7.9_spmd} | conditional | flops 274599424 | bytes 8459342 | solution.py:150
  203.4 3.8 %conditional.2 = ((f32[1,4,256]{2,1,0:T(4,128)S(1)}, f32[1,4,256]{2,1,0:T(4,128)S(1)}, f32[1,4,256,128]{3,2,1,0:T(8,128)S(1)})) conditional(s32[]{:T(128)} %convert_element_type.129, (f32[1,4,256]{2,1,0:T(4,128)S(1)}, f32[1,4,256]{2,1,0:T(4,128)S(1)}, f32[1,4,256,128]{3,2,1,0:T(8,128)S(1)}) %tuple.87, (s32[]{:T(128)}, s32[256]{0:T(256)S(1)}, ...), branch_computations={%region_6.6_spmd, %region_7.9_spmd} | conditional | flops 274599424 | bytes 8459342 | solution.py:150
  208.4 3.8 %conditional.2 = ((f32[1,4,256]{2,1,0:T(4,128)S(1)}, f32[1,4,256]{2,1,0:T(4,128)S(1)}, f32[1,4,256,128]{3,2,1,0:T(8,128)S(1)})) conditional(s32[]{:T(128)} %convert_element_type.129, (f32[1,4,256]{2,1,0:T(4,128)S(1)}, f32[1,4,256]{2,1,0:T(4,128)S(1)}, f32[1,4,256,128]{3,2,1,0:T(8,128)S(1)}) %tuple.87, (s32[]{:T(128)}, s32[256]{0:T(256)S(1)}, ...), branch_computations={%region_6.6_spmd, %region_7.9_spmd} | conditional | flops 274599424 | bytes 8459342 | solution.py:150
  213.5 3.8 %conditional.2 = ((f32[1,4,256]{2,1,0:T(4,128)S(1)}, f32[1,4,256]{2,1,0:T(4,128)S(1)}, f32[1,4,256,128]{3,2,1,0:T(8,128)S(1)})) conditional(s32[]{:T(128)} %convert_element_type.129, (f32[1,4,256]{2,1,0:T(4,128)S(1)}, f32[1,4,256]{2,1,0:T(4,128)S(1)}, f32[1,4,256,128]{3,2,1,0:T(8,128)S(1)}) %tuple.87, (s32[]{:T(128)}, s32[256]{0:T(256)S(1)}, ...), branch_computations={%region_6.6_spmd, %region_7.9_spmd} | conditional | flops 274599424 | bytes 8459342 | solution.py:150
  218.5 3.8 %conditional.2 = ((f32[1,4,256]{2,1,0:T(4,128)S(1)}, f32[1,4,256]{2,1,0:T(4,128)S(1)}, f32[1,4,256,128]{3,2,1,0:T(8,128)S(1)})) conditional(s32[]{:T(128)} %convert_element_type.129, (f32[1,4,256]{2,1,0:T(4,128)S(1)}, f32[1,4,256]{2,1,0:T(4,128)S(1)}, f32[1,4,256,128]{3,2,1,0:T(8,128)S(1)}) %tuple.87, (s32[]{:T(128)}, s32[256]{0:T(256)S(1)}, ...), branch_computations={%region_6.6_spmd, %region_7.9_spmd} | conditional | flops 274599424 | bytes 8459342 | solution.py:150
  223.6 3.8 %conditional.2 = ((f32[1,4,256]{2,1,0:T(4,128)S(1)}, f32[1,4,256]{2,1,0:T(4,128)S(1)}, f32[1,4,256,128]{3,2,1,0:T(8,128)S(1)})) conditional(s32[]{:T(128)} %convert_element_type.129, (f32[1,4,256]{2,1,0:T(4,128)S(1)}, f32[1,4,256]{2,1,0:T(4,128)S(1)}, f32[1,4,256,128]{3,2,1,0:T(8,128)S(1)}) %tuple.87, (s32[]{:T(128)}, s32[256]{0:T(256)S(1)}, ...), branch_computations={%region_6.6_spmd, %region_7.9_spmd} | conditional | flops 274599424 | bytes 8459342 | solution.py:150
  228.6 3.8 %conditional.2 = ((f32[1,4,256]{2,1,0:T(4,128)S(1)}, f32[1,4,256]{2,1,0:T(4,128)S(1)}, f32[1,4,256,128]{3,2,1,0:T(8,128)S(1)})) conditional(s32[]{:T(128)} %convert_element_type.129, (f32[1,4,256]{2,1,0:T(4,128)S(1)}, f32[1,4,256]{2,1,0:T(4,128)S(1)}, f32[1,4,256,128]{3,2,1,0:T(8,128)S(1)}) %tuple.87, (s32[]{:T(128)}, s32[256]{0:T(256)S(1)}, ...), branch_computations={%region_6.6_spmd, %region_7.9_spmd} | conditional | flops 274599424 | bytes 8459342 | solution.py:150
  233.6 33.8 %while.37 = (s32[]{:T(128)}, f32[4,128,128]{2,1,0:T(8,128)S(1)}, s32[]{:T(128)}, bf16[32,4]{1,0:T(8,128)(2,1)S(1)}, bf16[32,4,128,128]{3,2,1,0:T(8,128)(2,1)}, /*index=5*/s32[]{:T(128)}, s32[]{:T(128)}) while((s32[]{:T(128)}, f32[4,128,128]{2,1,0:T(8,128)S(1)}, s32[]{:T(128)}, bf16[32,4]{1,0:T(8,128)(2,1)S(1)}, ...), condition=%wide.region_3.4_spmd.clone, body=%wide.region_2.3_spmd.clone.sunk | while | flops 327688 | bytes 655505 | solution.py:32
  (262 shorter events, 109.8 us)
Async XLA Ops:
  7.2 1.0 copy-start
  7.2 8.7 %copy-start.1 = (bf16[256,512]{1,0:T(8,128)(2,1)S(1)}, bf16[256,512]{1,0:T(8,128)(2,1)}, u32[]{:S(2)}) copy-start(bf16[256,512]{1,0:T(8,128)(2,1)} %param.19) | copy-start | bytes 786436
  7.2 73.4 %all-gather.6.cloned.1.call-start = ((), (), s32[]{:S(2)}) async-start(), calls=%async_computation | async-start | bytes 2162688 | tf_op jit(solution)/shard_map/all_gather | solution.py:131
  8.9 142.6 %all-gather.8.cloned.1.call-start = ((), (), s32[]{:S(2)}) async-start(), calls=%async_computation.1 | async-start | bytes 2162688 | tf_op jit(solution)/shard_map/all_gather | solution.py:132
  10.4 223.2 %all-gather.10.cloned.1.call-start = ((), (), s32[]{:S(2)}) async-start(), calls=%async_computation.2 | async-start | bytes 4325376 | tf_op jit(solution)/shard_map/all_gather | solution.py:15
  232.9 34.6 %copy-start.2 = (bf16[256,512]{1,0:T(8,128)(2,1)S(1)}, bf16[256,512]{1,0:T(8,128)(2,1)}, u32[]{:S(2)}) copy-start(bf16[256,512]{1,0:T(8,128)(2,1)} %param.14) | copy-start | bytes 786436
  233.6 34.6 %copy-start.4 = (bf16[256,512]{1,0:T(8,128)(2,1)S(1)}, bf16[256,512]{1,0:T(8,128)(2,1)}, u32[]{:S(2)}) copy-start(bf16[256,512]{1,0:T(8,128)(2,1)} %param.16) | copy-start | bytes 786436
  268.2 0.9 copy-start.3
Sparse Core Ops, SparseCore 0:
  10.7 69.8 all-gather.5
  82.7 68.6 all-gather.7
  154.1 71.0 all-gather.9
where the time goes:
time: 278 us; the launch traced here: 276 us
  waiting for transfers between devices  108 us (39%)
  matrix products  52.5 us (19%)
  other arithmetic  45.3 us (16%)
  blocking collectives  26.8 us (10%)
  local copies, waits for them, and re-layouts  17 us (6%)
  between operations  14 us (5%)
  loops' own time  12.6 us (5%)
    all_gather x1, waiting for transfers between devices, local(): value_part = lax.all_gather(value_rows, 'seq', axis=0, tiled=True)  70.9 us
    all_gather x1, waiting for transfers between devices, local(): key_part = lax.all_gather(key_rows, 'seq', axis=0, tiled=True)  37.1 us
    select_n x32, other arithmetic, step(): return jax.tree.map(lambda a, b: jnp.where(reached, a, b), new, before)  32.4 us
    dot_general x16, matrix products, attend(): jnp.einsum('kgts,skd->kgtd', probs.astype(jnp.bfloat16), value_heads, pre...  27.1 us
    all_gather x1, blocking collectives, carried_in(): lax.all_gather(part.astype(kind), axis)  26.8 us
    dot_general x16, matrix products, attend(): jnp.einsum('tkgd,skd->kgts', query_heads, key_heads, preferred_element_ty...  22.2 us
    another operation x1, loops' own time, local(): finished = lax.fori_loop(0, sub_count, one_sub, initial)  10.6 us
    slice x16, local copies, waits for them, and re-layouts, one_sub(): results = [lax.cond(offset <= query_pos[-1], live, skipped, inner[0])]  9.85 us
  transfers between devices with their start and end apart: 3, of which 2 were waited for; matrix products, arithmetic and copies ran while one was open for 28% of the time, Pallas kernels for 0%

commit v1 on v0

v1 whole, which is shorter than its diff:
```python
import jax
import jax.numpy as jnp
from jax import lax
from jax.experimental import pallas as pl
from jax.experimental.pallas import tpu as pltpu
from jax.sharding import PartitionSpec as P

HEADS = 64
HD = 128
KVH = 8
BLOCK = 256
LOCAL = 4
SHARDS = 32
PIECE = LOCAL * HD // SHARDS
CHUNK = 2048
SCALE = HD**-0.5 * 1.4426950408889634
NEG = -1e30
HUGE = 2.0**100
NT = (((1,), (1,)), ((), ()))
TN = (((0,), (0,)), ((), ()))
f32, bf16 = jnp.float32, jnp.bfloat16


def iota(shape, dim):
    return lax.broadcasted_iota(jnp.int32, shape, dim)


def dot(a, b, dims=(((1,), (0,)), ((), ())), precision=None):
    return lax.dot_general(a, b, dims, precision=precision, preferred_element_type=f32)


def split3(x):
    hi = x.astype(bf16).astype(f32)
    rest = x - hi
    mid = rest.astype(bf16).astype(f32)
    return hi, mid, rest - mid


def pick_kernel(place_ref, keys_ref, values_ref, out_ref):
    out_ref[:, :HD] = keys_ref[...]
    out_ref[:, HD:] = values_ref[...]


def pick(place, keys2, values2):
    rows = keys2.shape[0]
    column = pl.BlockSpec((rows, HD), lambda i, place: (0, place[1] // 2))
    return pl.pallas_call(
        pick_kernel,
        out_shape=jax.ShapeDtypeStruct((rows, 2 * HD), bf16),
        grid_spec=pltpu.PrefetchScalarGridSpec(
            num_scalar_prefetch=1,
            grid=(1,),
            in_specs=[column, column],
            out_specs=pl.BlockSpec((rows, 2 * HD), lambda i, place: (0, 0)),
        ),
        name="pick",
    )(place, keys2, values2)


def decay_columns(decay):
    lower = (iota((BLOCK, BLOCK), 1) <= iota((BLOCK, BLOCK), 0)).astype(f32)
    return dot(lower, decay, NT, lax.Precision.HIGHEST)


def state_kernel(keys_ref, values_ref, decay_ref, out_ref):
    running = decay_columns(decay_ref[...])
    last = running[BLOCK - 1 : BLOCK, :]
    tail = jnp.exp(last - running)
    parts = HD // PIECE
    for h in range(LOCAL):
        cols = slice(h * HD, (h + 1) * HD)
        scaled = (keys_ref[:, cols].astype(f32) * tail[:, h : h + 1]).astype(bf16)
        state = dot(scaled, values_ref[:, cols], TN).astype(bf16)
        hi, mid, lo = split3(last[:, h : h + 1])
        row = iota((PIECE, HD), 0)
        told = jnp.where(row == 0, hi, jnp.where(row == 1, mid, lo)).astype(bf16)
        for i in range(parts):
            out_ref[h * parts + i, :PIECE, :] = state[i * PIECE : (i + 1) * PIECE, :]
            out_ref[h * parts + i, PIECE:, :] = told


def scan_kernel(in_ref, out_ref):
    state = jnp.zeros((PIECE, HD), f32)
    for s in range(SHARDS):
        out_ref[s] = state.astype(bf16)
        told = in_ref[s, PIECE:, :].astype(f32)
        total = told[0:1] + told[1:2] + told[2:3]
        state = jnp.exp(total) * state + in_ref[s, :PIECE, :].astype(f32)


def mix_kernel(query_ref, keys_ref, values_ref, decay_ref, state_ref, gain_ref, out_ref):
    decay = decay_ref[...]
    running = decay_columns(decay)
    upper = (iota((BLOCK, BLOCK), 0) <= iota((BLOCK, BLOCK), 1)).astype(f32)
    along = dot(decay, upper, precision=lax.Precision.HIGHEST)
    grow = jnp.exp(running)
    lower = iota((BLOCK, BLOCK), 1) <= iota((BLOCK, BLOCK), 0)
    for h in range(LOCAL):
        cols = slice(h * HD, (h + 1) * HD)
        query = query_ref[:, cols]
        spread = jnp.where(lower, running[:, h : h + 1] - along[h : h + 1, :], NEG)
        weighted = (dot(query, keys_ref[:, cols], NT) * jnp.exp(spread)).astype(bf16)
        lifted = query.astype(f32) * grow[:, h : h + 1]
        high = lifted.astype(bf16)
        low = (lifted - high.astype(f32)).astype(bf16)
        state = state_ref[h * HD : (h + 1) * HD, :]
        mixed = dot(weighted, values_ref[:, cols]) + dot(high, state) + dot(low, state)
        norm = lax.rsqrt(jnp.mean(mixed * mixed, axis=-1, keepdims=True) + 1e-06)
        out_ref[:, cols] = (mixed * norm * gain_ref[:, cols]).astype(bf16)


def lightning(query, keys, values, decay, gain):
    sent = pl.pallas_call(
        state_kernel,
        out_shape=jax.ShapeDtypeStruct((SHARDS, 2 * PIECE, HD), bf16),
        name="block_state",
    )(keys, values, decay)
    pieces = lax.all_to_all(sent, "seq", 0, 0)
    before = pl.pallas_call(
        scan_kernel,
        out_shape=jax.ShapeDtypeStruct((SHARDS, PIECE, HD), bf16),
        name="state_scan",
    )(pieces)
    state = lax.all_to_all(before, "seq", 0, 0).reshape(LOCAL * HD, HD)
    return pl.pallas_call(
        mix_kernel,
        out_shape=jax.ShapeDtypeStruct(query.shape, bf16),
        name="mix",
    )(query, keys, values, decay, state, gain.reshape(1, LOCAL * HD))


def own_kernel(query_ref, kv_ref, wide_ref, sums_ref):
    keys = kv_ref[:, :HD]
    values = jnp.concatenate([kv_ref[:, HD:], jnp.ones((BLOCK, HD), bf16)], 1)
    allowed = iota((BLOCK, BLOCK), 1) <= iota((BLOCK, BLOCK), 0)
    col = iota((BLOCK, HD), 1)
    for h in range(LOCAL):
        rows = slice(h * BLOCK, (h + 1) * BLOCK)
        query = query_ref[:, h * HD : (h + 1) * HD]
        logits = jnp.where(allowed, dot(query, keys, NT), NEG)
        peak = jnp.max(logits, axis=1, keepdims=True)
        probs = jnp.exp2((logits - peak) * SCALE).astype(bf16)
        sums_ref[rows, :] = dot(probs, values)
        hi, mid, lo = split3(-peak)
        extra = jnp.where(col == 0, hi, jnp.where(col == 1, mid, jnp.where(col == 2, lo, 0.0)))
        extra = jnp.where(col == 3, 1.0, extra)
        wide_ref[rows, :] = jnp.concatenate([query, extra.astype(bf16)], 1)


def attend_kernel(place_ref, wide_ref, first_ref, kv_ref, all_ref, out_ref, sums_ref, held_ref):
    step = pl.program_id(0)
    shard = place_ref[0]
    limit = shard * BLOCK

    @pl.when(step == 0)
    def _():
        sums_ref[...] = first_ref[...]

    @pl.when(step * CHUNK < limit)
    def _():
        col = iota((CHUNK, HD), 1)
        late = iota((CHUNK, HD), 0) + step * CHUNK >= limit
        extra = jnp.where(col < 3, 1.0, jnp.where((col == 3) & late, NEG, 0.0)).astype(bf16)
        keys = jnp.concatenate([kv_ref[:, :HD], extra], 1)
        values = jnp.concatenate([kv_ref[:, HD:], jnp.ones((CHUNK, HD), bf16)], 1)

        def logits(h):
            return dot(wide_ref[h * BLOCK : (h + 1) * BLOCK, :], keys, NT)

        ahead = logits(0)
        probs = None
        for h in range(LOCAL + 1):
            after = logits(h + 1) if h + 1 < LOCAL else None
            if probs is not None:
                sums_ref[(h - 1) * BLOCK : h * BLOCK, :] += dot(probs, values)
            if h < LOCAL:
                probs = jnp.exp2(ahead * SCALE).astype(bf16)
            ahead = after

    @pl.when(step == pl.num_programs(0) - 1)
    def _():
        biggest = jnp.max(sums_ref[:, HD:])
        fine = biggest < HUGE

        @pl.when(fine)
        def _():
            for h in range(LOCAL):
                sums = sums_ref[h * BLOCK : (h + 1) * BLOCK, :]
                out_ref[:, h * HD : (h + 1) * HD] = (sums[:, :HD] / sums[:, HD:]).astype(bf16)

        @pl.when(jnp.logical_not(fine))
        def _():
            row = iota((BLOCK, BLOCK), 0)
            col = iota((BLOCK, BLOCK), 1)
            for h in range(LOCAL):
                rows = slice(h * BLOCK, (h + 1) * BLOCK)
                query = wide_ref[rows, :HD]

                def one(j, carry):
                    peak, total, summed = carry
                    pltpu.sync_copy(all_ref.at[pl.ds(j * BLOCK, BLOCK), :], held_ref)
                    scores = dot(query, held_ref[:, :HD], NT) * SCALE
                    allowed = j * BLOCK + col <= limit + row
                    scores = jnp.where(allowed, scores, NEG)
                    top = jnp.maximum(peak, jnp.max(scores, axis=1, keepdims=True))
                    probs = jnp.where(allowed, jnp.exp2(scores - top), 0.0)
                    factor = jnp.exp2(peak - top)
                    total = factor * total + jnp.sum(probs, axis=1, keepdims=True)
                    summed = factor * summed + dot(probs.astype(bf16), held_ref[:, HD:])
                    return top, total, summed

                start = (
                    jnp.full((BLOCK, 1), NEG, f32),
                    jnp.zeros((BLOCK, 1), f32),
                    jnp.zeros((BLOCK, HD), f32),
                )
                _, total, summed = lax.fori_loop(0, shard + 1, one, start)
                out_ref[:, h * HD : (h + 1) * HD] = (summed / total).astype(bf16)


def attention(place, query, kv, gathered):
    rows = LOCAL * BLOCK
    wide, first = pl.pallas_call(
        own_kernel,
        out_shape=[
            jax.ShapeDtypeStruct((rows, 2 * HD), bf16),
            jax.ShapeDtypeStruct((rows, 2 * HD), f32),
        ],
        name="own_block",
    )(query, kv)
    steps = gathered.shape[0] // CHUNK
    whole = pl.BlockSpec((rows, 2 * HD), lambda j, place: (0, 0))

    def needed(j, place):
        return (jnp.minimum(j, jnp.maximum(place[0] * BLOCK - 1, 0) // CHUNK), 0)

    return pl.pallas_call(
        attend_kernel,
        out_shape=jax.ShapeDtypeStruct(query.shape, bf16),
        grid_spec=pltpu.PrefetchScalarGridSpec(
            num_scalar_prefetch=1,
            grid=(steps,),
            in_specs=[
                whole,
                whole,
                pl.BlockSpec((CHUNK, 2 * HD), needed),
                pl.BlockSpec(memory_space=pl.ANY),
            ],
            out_specs=pl.BlockSpec(query.shape, lambda j, place: (0, 0)),
            scratch_shapes=[pltpu.VMEM((rows, 2 * HD), f32), pltpu.VMEM((BLOCK, 2 * HD), bf16)],
        ),
        compiler_params=pltpu.CompilerParams(vmem_limit_bytes=48 * 2**20),
        name="attend",
    )(place, wide, first, gathered, gathered)


def local(light_query, light_keys, light_values, log_decay, light_gain, query2, keys2, values2):
    place = jnp.stack([lax.axis_index("seq"), lax.axis_index("head")]).astype(jnp.int32)
    kv = pick(place, keys2, values2)
    gathered = lax.all_gather(kv, "seq", axis=0, tiled=True)
    light_out = lightning(light_query, light_keys, light_values, log_decay, light_gain)
    soft_out = attention(place, query2, kv, gathered)
    return (light_out, soft_out)


def solution(mesh):
    placed = (
        P("seq", "head"),
        P("seq", "head"),
        P("seq", "head"),
        P("head", "seq"),
        P("head"),
        P("seq", "head"),
        P("seq", None),
        P("seq", None),
    )
    return jax.shard_map(
        local,
        mesh=mesh,
        in_specs=placed,
        out_specs=(P("seq", "head"), P("seq", "head")),
        check_vma=False,
    )
```

time: 278 us -> 194 us (0.70)
  Pallas kernels: 0 us -> 104 us
  waiting for transfers between devices: 108 us -> 31 us
  matrix products: 52.5 us -> 0 us
  other arithmetic: 45.3 us -> 0.67 us
  loops' own time: 12.6 us -> 0 us
  local copies, waits for them, and re-layouts: 17 us -> 5.11 us
  starting transfers between devices: 0.12 us -> 10.7 us
    pallas_call x0 -> x6, Pallas kernels: none -> 104 us  [the longest x1 91.5 us: attention(): pl.pallas_call(attend_kernel, out_shape=jax.ShapeDtypeStruct(query.shape,...]
    all_gather x3 -> x1, waiting for transfers between devices: 108 us -> 20.4 us  [local(): gathered = lax.all_gather(kv, 'seq', axis=0, tiled=True)]
    dot_general x35 -> x0, matrix products: 52.5 us -> none  [the longest x16 27.1 us: attend(): jnp.einsum('kgts,skd->kgtd', probs.astype(jnp.bfloat16), value_heads, pre...]
    select_n x32 -> x0, other arithmetic: 32.4 us -> none  [step(): return jax.tree.map(lambda a, b: jnp.where(reached, a, b), new, before)]
    all_to_all x0 -> x1, blocking collectives: none -> 27.7 us  [lightning(): pieces = lax.all_to_all(sent, 'seq', 0, 0)]
    all_gather x1 -> x0, blocking collectives: 26.8 us -> none  [carried_in(): lax.all_gather(part.astype(kind), axis)]
    another operation x18 -> x0, loops' own time: 12.6 us -> none  [the longest x1 10.6 us: local(): finished = lax.fori_loop(0, sub_count, one_sub, initial)]
    all_to_all x0 -> x1, starting transfers between devices: none -> 10.6 us  [lightning(): state = lax.all_to_all(before, 'seq', 0, 0).reshape(LOCAL * HD, HD)]
  transfers between devices with their start and end apart: 3 -> 2, of which waited for: 2 -> 2; matrix products, arithmetic and copies ran while one was open for 28% -> 0% of each run, Pallas kernels for 0% -> 5%
where the time goes in v1:
time: 194 us; the launch traced here: 193 us
  Pallas kernels  104 us (54%)
  waiting for transfers between devices  31 us (16%)
  blocking collectives  27.7 us (14%)
  between operations  14 us (7%)
  starting transfers between devices  10.7 us (6%)
  local copies, waits for them, and re-layouts  5.11 us (3%)
    pallas_call x1, Pallas kernels, attention(): pl.pallas_call(attend_kernel, out_shape=jax.ShapeDtypeStruct(query.shape,...  91.5 us
    all_to_all x1, blocking collectives, lightning(): pieces = lax.all_to_all(sent, 'seq', 0, 0)  27.7 us
    all_gather x1, waiting for transfers between devices, local(): gathered = lax.all_gather(kv, 'seq', axis=0, tiled=True)  20.4 us
    all_to_all x1, starting transfers between devices, lightning(): state = lax.all_to_all(before, 'seq', 0, 0).reshape(LOCAL * HD, HD)  10.6 us
    all_to_all x1, waiting for transfers between devices, lightning(): state = lax.all_to_all(before, 'seq', 0, 0).reshape(LOCAL * HD, HD)  10.5 us
    unnamed x10, local copies, waits for them, and re-layouts  5.11 us
  transfers between devices with their start and end apart: 2, of which 2 were waited for; matrix products, arithmetic and copies ran while one was open for 0% of the time, Pallas kernels for 5%

profile of v1, /device:TPU:481, one launch (start us, length us, event | category | flops | bytes accessed | tf_op | source)
XLA Modules:
  0.0 193.2 jit_solution(7407244342763953131)
XLA Ops:
  7.2 0.0 all-gather.2.cloned.1.call-start
  7.2 0.7 pad_add_fusion.place_ref
  7.9 0.0 copy-start.3
  7.9 2.4 %pick.1.kv_ref = bf16[256,256]{1,0:T(8,128)(2,1)} custom-call(s32[2]{0:T(128)} %pad_add_fusion.place_ref, bf16[256,1024]{1,0:T(8,128)(2,1)} %keys_ref.5, bf16[256,1024]{1,0:T(8,128)(2,1)} %values_ref.5), custom_call_target="tpu_custom_call" | custom-call | tf_op jit(solution)/shard_map/pick/pallas_call | solution.py:47
  10.2 0.0 all-gather.2.cloned.1.call-update
  10.3 2.6 %block_state.1 = bf16[32,32,128]{2,1,0:T(8,128)(2,1)} custom-call(bf16[256,512]{1,0:T(8,128)(2,1)} %keys_ref.4, bf16[256,512]{1,0:T(8,128)(2,1)} %values_ref.4, f32[4,256]{1,0:T(4,128)} %decay_ref.3), custom_call_target="tpu_custom_call" | custom-call | tf_op jit(solution)/shard_map/block_state/pallas_call | solution.py:113
  12.9 27.7 %all_to_all.10.in_ref = bf16[32,32,128]{2,1,0:T(8,128)(2,1)} all-to-all(bf16[32,32,128]{2,1,0:T(8,128)(2,1)} %block_state.1), channel_id=1, replica_groups=mesh['seq'=32,'head'=16] {'seq'}, dimensions={0} | all-to-all | bytes 524288 | tf_op jit(solution)/shard_map/all_to_all | solution.py:118
  40.6 1.7 state_scan.1
  42.3 10.6 %all-to-all-start.1 = ((bf16[32,16,128]{2,1,0:T(8,128)(2,1)}), bf16[32,16,128]{2,1,0:T(8,128)(2,1)S(1)}, u32[]{:S(2)}, u32[]{:S(2)}) async-start(bf16[32,16,128]{2,1,0:T(8,128)(2,1)} %state_scan.1), calls=%async_computation.1 | async-start | bytes 262144 | tf_op jit(solution)/shard_map/all_to_all | solution.py:124
  52.9 2.7 %own_block.1 = (bf16[1024,256]{1,0:T(8,128)(2,1)}, f32[1024,256]{1,0:T(8,128)}) custom-call(bf16[256,512]{1,0:T(8,128)(2,1)} %query_ref.3, bf16[256,256]{1,0:T(8,128)(2,1)} %pick.1.kv_ref), custom_call_target="tpu_custom_call" | custom-call | tf_op jit(solution)/shard_map/own_block/pallas_call | solution.py:223
  55.6 10.5 %all-to-all-done.1 = bf16[32,16,128]{2,1,0:T(8,128)(2,1)S(1)} async-done(((bf16[32,16,128]{2,1,0:T(8,128)(2,1)}), bf16[32,16,128]{2,1,0:T(8,128)(2,1)S(1)}, u32[]{:S(2)}, u32[]{:S(2)}) %all-to-all-start.1) | async-done | bytes 131104 | tf_op jit(solution)/shard_map/all_to_all | solution.py:124
  66.2 0.0 copy-start.4
  66.2 0.7 copy-done.4
  66.8 3.1 %mix.1 = bf16[256,512]{1,0:T(8,128)(2,1)} custom-call(bf16[256,512]{1,0:T(8,128)(2,1)} %query_ref.2, bf16[256,512]{1,0:T(8,128)(2,1)} %keys_ref.4, bf16[256,512]{1,0:T(8,128)(2,1)} %values_ref.4, f32[4,256]{1,0:T(4,128)} %decay_ref.3, bf16[512,128]{1,0:T(8,128)(2,1)} %bitcast.4, f32[1,512]{1,0:T(1,128)} %bitcast.5), custom_call_target="tpu_custom_call" | custom-call | tf_op jit(solution)/shard_map/mix/pallas_call | solution.py:125
  70.0 20.4 %all-gather.2.cloned.1.call-done.kv_ref.all_ref = bf16[8192,256]{1,0:T(8,128)(2,1)} async-done(((bf16[256,256]{1,0:T(8,128)(2,1)}), bf16[8192,256]{1,0:T(8,128)(2,1)}) %all-gather.2.cloned.1.call-update) | async-done | bytes 4194320 | tf_op jit(solution)/shard_map/all_gather | solution.py:260
  90.4 0.0 copy-done.3
  90.4 0.0 copy-start
  90.4 2.2 %copy-done = bf16[8192,256]{1,0:T(8,128)(2,1)S(1)} copy-done((bf16[8192,256]{1,0:T(8,128)(2,1)S(1)}, bf16[8192,256]{1,0:T(8,128)(2,1)}, u32[]{:S(2)}) %copy-start) | copy-done | bytes 4194328
  92.6 0.0 copy-start.1
  92.6 1.2 copy-done.1
  93.8 0.0 copy-start.2
  93.8 1.0 copy-done.2
  94.8 91.5 %attend.1 = bf16[256,512]{1,0:T(8,128)(2,1)} custom-call(s32[2]{0:T(128)S(1)} %copy-done.3, bf16[1024,256]{1,0:T(8,128)(2,1)S(1)} %copy-done.2, f32[1024,256]{1,0:T(8,128)S(1)} %copy-done.1, bf16[8192,256]{1,0:T(8,128)(2,1)S(1)} %copy-done, bf16[8192,256]{1,0:T(8,128)(2,1)S(1)} %copy-done), custom_call_target="tpu_custom_call" | custom-call | tf_op jit(solution)/shard_map/attend/pallas_call | solution.py:237
Async XLA Ops:
  7.2 83.2 %all-gather.2.cloned.1.call-start = ((), (), s32[]{:S(2)}) async-start(), calls=%async_computation.2 | async-start | bytes 4325376 | tf_op jit(solution)/shard_map/all_gather | solution.py:260
  7.9 82.5 %copy-start.3 = (s32[2]{0:T(128)S(1)}, s32[2]{0:T(128)}, u32[]{:S(2)}) copy-start(s32[2]{0:T(128)} %pad_add_fusion.place_ref) | copy-start | bytes 28
  42.3 23.9 %all-to-all-start.1 = ((bf16[32,16,128]{2,1,0:T(8,128)(2,1)}), bf16[32,16,128]{2,1,0:T(8,128)(2,1)S(1)}, u32[]{:S(2)}, u32[]{:S(2)}) async-start(bf16[32,16,128]{2,1,0:T(8,128)(2,1)} %state_scan.1), calls=%async_computation.1 | async-start | bytes 262144 | tf_op jit(solution)/shard_map/all_to_all | solution.py:124
  66.2 0.7 copy-start.4
  90.4 2.2 %copy-start = (bf16[8192,256]{1,0:T(8,128)(2,1)S(1)}, bf16[8192,256]{1,0:T(8,128)(2,1)}, u32[]{:S(2)}) copy-start(bf16[8192,256]{1,0:T(8,128)(2,1)} %all-gather.2.cloned.1.call-done.kv_ref.all_ref) | copy-start | bytes 12582916
  92.6 1.2 copy-start.1
  93.8 1.0 copy-start.2
Sparse Core Ops, SparseCore 0:
  10.4 79.9 all-gather.1

commit v2 on v1

v2 whole, which is shorter than its diff:
```python
import jax
import jax.numpy as jnp
from jax import lax
from jax.experimental import pallas as pl
from jax.experimental.pallas import tpu as pltpu
from jax.sharding import PartitionSpec as P

HEADS = 64
HD = 128
KVH = 8
BLOCK = 256
CHIPS = 16
LOCAL = 4
HALF = LOCAL // 2
ROWS = LOCAL * BLOCK
SHARE = BLOCK // 2
SCALE = HD**-0.5 * 1.4426950408889634
NEG = -1e30
HUGE = 2.0**100
NT = (((1,), (1,)), ((), ()))
TN = (((0,), (0,)), ((), ()))
f32, bf16 = jnp.float32, jnp.bfloat16

FAR = (
    [(z, z + 4) for z in range(12)],
    [(z, z + 8) for z in range(8)],
    [(z, z + 12) for z in range(4)],
)
FIFTH = (
    [(z, z + 5) for z in range(11)] + [(11, 0), (12, 1)],
    [(z, z + 10) for z in range(6)] + [(6, 0), (7, 1)],
    [(0, 15), (1, 0), (2, 1)],
)
NEAR = [[(z, z + d) for z in range(CHIPS - d)] for d in (1, 2)]
UP1 = [(z, z + 1) for z in range(15)]
UP2 = [(z, z + 2) for z in range(14)]
DOWN1 = [(z, z - 1) for z in range(5, 16)] + [(0, 15)]
DOWN2 = [(z, z - 2) for z in range(5, 16)] + [(0, 14), (1, 15)]


def on_core(core, chips):
    return [(2 * a + core, 2 * b + core) for a, b in chips]


def on_both(chips):
    return on_core(0, chips) + on_core(1, chips)


PAIRS = [[s, s + 1] for s in range(0, 2 * CHIPS, 2)]
SWAP = [(s, s ^ 1) for s in range(2 * CHIPS)]
MATES = [(h, h ^ 1) for h in range(16)]


def iota(shape, dim):
    return lax.broadcasted_iota(jnp.int32, shape, dim)


def dot(a, b, dims=(((1,), (0,)), ((), ())), precision=None):
    return lax.dot_general(a, b, dims, precision=precision, preferred_element_type=f32)


def split3(x):
    hi = x.astype(bf16).astype(f32)
    rest = x - hi
    mid = rest.astype(bf16).astype(f32)
    return hi, mid, rest - mid


def shape(*dims, dtype=f32):
    return jax.ShapeDtypeStruct(dims, dtype)


def call(kernel, out_shape, place, *args, left=0, scratch=(), name=None, flops=0, limit=16):
    def spec(dims):
        return pl.BlockSpec(dims, lambda i, place: (0,) * len(dims))

    many = isinstance(out_shape, list)
    outs = out_shape if many else [out_shape]
    specs = [spec(a.shape) for a in args]
    if left:
        specs[-left:] = [pl.BlockSpec(memory_space=pl.ANY)] * left
    out_specs = [spec(o.shape) for o in outs]
    return pl.pallas_call(
        kernel,
        out_shape=out_shape,
        grid_spec=pltpu.PrefetchScalarGridSpec(
            num_scalar_prefetch=1,
            grid=(1,),
            in_specs=specs,
            out_specs=out_specs if many else out_specs[0],
            scratch_shapes=scratch,
        ),
        compiler_params=pltpu.CompilerParams(vmem_limit_bytes=limit * 2**20),
        cost_estimate=pl.CostEstimate(
            flops=flops, bytes_accessed=sum(a.size * a.dtype.itemsize for a in args), transcendentals=0
        ),
        name=name,
    )(place, *args)


def pick_kernel(place_ref, keys_ref, values_ref, out_ref, share_ref):
    out_ref[:, :HD] = keys_ref[...]
    out_ref[:, HD:] = values_ref[...]
    start = pl.multiple_of(place_ref[1] % 2 * SHARE, SHARE)
    share_ref[...] = out_ref[pl.ds(start, SHARE), :]


def pick(place, keys2, values2):
    column = pl.BlockSpec((BLOCK, HD), lambda i, place: (0, place[1] // 2))
    return pl.pallas_call(
        pick_kernel,
        out_shape=[shape(BLOCK, 2 * HD, dtype=bf16), shape(SHARE, 2 * HD, dtype=bf16)],
        grid_spec=pltpu.PrefetchScalarGridSpec(
            num_scalar_prefetch=1,
            grid=(1,),
            in_specs=[column, column],
            out_specs=[
                pl.BlockSpec((BLOCK, 2 * HD), lambda i, place: (0, 0)),
                pl.BlockSpec((SHARE, 2 * HD), lambda i, place: (0, 0)),
            ],
        ),
        name="pick",
    )(place, keys2, values2)


STATE = LOCAL * HD
CARRIED = HALF * HD
TAIL = 16


def decay_columns(decay):
    lower = (iota((BLOCK, BLOCK), 1) <= iota((BLOCK, BLOCK), 0)).astype(f32)
    return dot(lower, decay, NT, lax.Precision.HIGHEST)


def told_rows(columns):
    lane, row = iota((TAIL, HD), 1), iota((TAIL, HD), 0)
    out = jnp.zeros((TAIL, HD), f32)
    for h, value in enumerate(columns):
        hi, mid, lo = split3(value)
        parts = jnp.where(row == 0, hi, jnp.where(row == 1, mid, jnp.where(row == 2, lo, 0.0)))
        out = jnp.where(lane == h, parts, out)
    return out.astype(bf16)


def told(rows):
    return jnp.sum(rows.astype(f32), axis=0, keepdims=True)


def state_kernel(keys_ref, values_ref, decay_ref, out_ref):
    running = decay_columns(decay_ref[...])
    last = running[BLOCK - 1 : BLOCK, :]
    tail = jnp.exp(last - running)
    for h in range(LOCAL):
        cols = slice(h * HD, (h + 1) * HD)
        scaled = (keys_ref[:, cols].astype(f32) * tail[:, h : h + 1]).astype(bf16)
        out_ref[cols, :] = dot(scaled, values_ref[:, cols], TN).astype(bf16)
    out_ref[STATE:, :] = told_rows([last[:, h : h + 1] for h in range(LOCAL)])


def chip_kernel(place_ref, both_ref, out_ref):
    core = place_ref[0] % 2
    size = STATE + TAIL
    first, second = told(both_ref[STATE:size, :]), told(both_ref[size + STATE :, :])
    sums = []
    for i in range(HALF):
        start = pl.multiple_of((core * HALF + i) * HD, HD)

        def head(row):
            return jnp.where(core == 0, row[:, i : i + 1], row[:, HALF + i : HALF + i + 1])

        later = head(second)
        state = jnp.exp(later) * both_ref[pl.ds(start, HD), :].astype(f32)
        state = state + both_ref[pl.ds(size + start, HD), :].astype(f32)
        out_ref[i * HD : (i + 1) * HD, :] = state.astype(bf16)
        sums.append(head(first) + later)
    out_ref[CARRIED:, :] = told_rows(sums)


def chain(refs):
    states, total = [], None
    decays = [told(ref[CARRIED:, :]) for ref in refs]
    for i in range(HALF):
        rows = slice(i * HD, (i + 1) * HD)
        state = refs[-1][rows, :].astype(f32)
        for ref, decay in zip(refs[-2::-1], decays[-2::-1]):
            state = ref[rows, :].astype(f32) + jnp.exp(decay[:, i : i + 1]) * state
        states.append(state)
    total = sum(decays[1:], decays[0])
    return states, total


def window_kernel(*refs):
    out_ref = refs[-1]
    states, total = chain(refs[:-1])
    for i, state in enumerate(states):
        out_ref[i * HD : (i + 1) * HD, :] = state.astype(bf16)
    out_ref[CARRIED:, :] = told_rows([total[:, i : i + 1] for i in range(HALF)])


def before_kernel(near1_ref, near2_ref, far1_ref, far2_ref, far3_ref, out_ref):
    near, decay = chain([near1_ref, near2_ref])
    far, _ = chain([far1_ref, far2_ref, far3_ref])
    for i in range(HALF):
        state = near[i] + jnp.exp(decay[:, i : i + 1]) * far[i]
        out_ref[i * HD : (i + 1) * HD, :] = state.astype(bf16)


def mix_kernel(
    place_ref, query_ref, keys_ref, values_ref, decay_ref, gain_ref, both_ref, before_ref, out_ref
):
    core = place_ref[0] % 2
    decay = decay_ref[...]
    running = decay_columns(decay)
    upper = (iota((BLOCK, BLOCK), 0) <= iota((BLOCK, BLOCK), 1)).astype(f32)
    along = dot(decay, upper, precision=lax.Precision.HIGHEST)
    grow = jnp.exp(running)
    lower = iota((BLOCK, BLOCK), 1) <= iota((BLOCK, BLOCK), 0)
    first = jnp.exp(told(both_ref[STATE : STATE + TAIL, :]))
    for h in range(LOCAL):
        cols = slice(h * HD, (h + 1) * HD)
        query = query_ref[:, cols]
        spread = jnp.where(lower, running[:, h : h + 1] - along[h : h + 1, :], NEG)
        weighted = (dot(query, keys_ref[:, cols], NT) * jnp.exp(spread)).astype(bf16)
        lifted = query.astype(f32) * grow[:, h : h + 1]
        high = lifted.astype(bf16)
        low = (lifted - high.astype(f32)).astype(bf16)
        state = before_ref[cols, :].astype(f32)
        after = first[:, h : h + 1] * state + both_ref[cols, :].astype(f32)
        state = jnp.where(core == 0, state, after).astype(bf16)
        mixed = dot(weighted, values_ref[:, cols]) + dot(high, state) + dot(low, state)
        norm = lax.rsqrt(jnp.mean(mixed * mixed, axis=-1, keepdims=True) + 1e-06)
        out_ref[:, cols] = (mixed * norm * gain_ref[:, cols]).astype(bf16)


def chip_states(place, keys, values, decay):
    mine = pl.pallas_call(state_kernel, out_shape=shape(STATE + TAIL, HD, dtype=bf16), name="block_state")(
        keys, values, decay
    )
    both = lax.all_gather(mine, "seq", axis=0, tiled=True, axis_index_groups=PAIRS)
    carried = shape(CARRIED + TAIL, HD, dtype=bf16)
    chip = call(chip_kernel, carried, place, both, name="chip_state")
    below = lax.ppermute(chip, "seq", on_both(NEAR[0]))
    return both, chip, below


def windows(chip, below):
    def window(*parts):
        out = shape(CARRIED + TAIL, HD, dtype=bf16)
        return pl.pallas_call(window_kernel, out_shape=out, name="window_state")(*parts)

    below2 = lax.ppermute(window(chip, below), "seq", on_both(NEAR[1]))
    return [below, below2], window(chip, below, below2)


def mixed(place, query, keys, values, decay, gain, both, near, window, after):
    far = [lax.ppermute(window, "seq", on_both(pairs)) for pairs in FAR]
    far, _ = lax.optimization_barrier((far, after))
    before = pl.pallas_call(before_kernel, out_shape=shape(CARRIED, HD, dtype=bf16), name="state_before")(
        *near, *far
    )
    before = lax.all_gather(before, "seq", axis=0, tiled=True, axis_index_groups=PAIRS)
    gain = gain.reshape(1, LOCAL * HD)
    out = shape(*query.shape, dtype=bf16)
    return call(mix_kernel, out, place, query, keys, values, decay, gain, both, before, name="mix")


FAR_BLOCKS = tuple((4 * core + i, 5 * i) for core in (0, 1) for i in (1, 2, 3))


def near_blocks(core):
    out = []
    for side in range(2):
        for hops in (1, 2):
            first = jnp.where(core == side, hops, 5 - hops)
            out += [first + 5 * i for both in range(2) for i in range(3)]
    return out


def attend(wide_ref, sums_ref, blocks):
    col = iota((SHARE, HD), 1)
    counts = jnp.where(col < 3, 1.0, 0.0)
    misses = jnp.where(col < 3, 1.0, jnp.where(col == 3, NEG, 0.0))
    extra = jnp.concatenate([jnp.where(ok, counts, misses).astype(bf16) for _, ok in blocks], 0)
    kv = jnp.concatenate([rows for rows, _ in blocks], 0)
    keys = jnp.concatenate([kv[:, :HD], extra], 1)
    values = jnp.concatenate([kv[:, HD:], jnp.ones(extra.shape, bf16)], 1)
    tiles = sums_ref.shape[0] // BLOCK

    def logits(i):
        return dot(wide_ref[i * BLOCK : (i + 1) * BLOCK, :], keys, NT)

    ahead = logits(0)
    probs = None
    for i in range(tiles + 1):
        after = logits(i + 1) if i + 1 < tiles else None
        if probs is not None:
            sums_ref[(i - 1) * BLOCK : i * BLOCK, :] += dot(probs, values)
        if i < tiles:
            probs = jnp.exp2(ahead * SCALE).astype(bf16)
        ahead = after


def rows_of(ref, block):
    return ref[block * SHARE : (block + 1) * SHARE, :]


def near_kernel(place_ref, query_ref, mate_ref, kv_ref, far_ref, wide_ref, sums_ref):
    core, chip = place_ref[0] % 2, place_ref[0] // 2
    keys = kv_ref[:, :HD]
    values = jnp.concatenate([kv_ref[:, HD:], jnp.ones((BLOCK, HD), bf16)], 1)
    col = iota((BLOCK, HD), 1)
    allowed = iota((BLOCK, BLOCK), 1) <= iota((BLOCK, BLOCK), 0)
    for side, ref in enumerate((query_ref, mate_ref)):
        for h in range(LOCAL):
            rows = slice(side * ROWS + h * BLOCK, side * ROWS + (h + 1) * BLOCK)
            query = ref[:, h * HD : (h + 1) * HD]
            logits = jnp.where(allowed, dot(query, keys, NT), NEG)
            peak = jnp.max(logits, axis=1, keepdims=True)
            if side == 0:
                probs = jnp.exp2((logits - peak) * SCALE).astype(bf16)
                sums_ref[rows, :] = dot(probs, values)
            else:
                sums_ref[rows, :] = jnp.zeros((BLOCK, 2 * HD), f32)
            hi, mid, lo = split3(-peak)
            extra = jnp.where(col == 0, hi, jnp.where(col == 1, mid, jnp.where(col == 2, lo, 0.0)))
            extra = jnp.where(col == 3, 1.0, extra)
            wide_ref[rows, :] = jnp.concatenate([query, extra.astype(bf16)], 1)

    @pl.when((chip >= 5) | (core == 1))
    def _():
        blocks = [(rows_of(far_ref, 0), core == 1)]
        attend(wide_ref, sums_ref, blocks + [(rows_of(far_ref, i), chip >= d) for i, d in FAR_BLOCKS])


def rest_kernel(diagonal, place_ref, wide_ref, sums_in_ref, *refs):
    near_refs = refs[:4]
    kv_ref, far_ref, out_ref, sums_ref, peak_ref, held_ref = refs[4:]
    core, chip = place_ref[0] % 2, place_ref[0] // 2
    distances = near_blocks(core)
    sums_ref[...] = sums_in_ref[...]

    @pl.when(chip >= 1)
    def _():
        attend(
            wide_ref,
            sums_ref,
            [(rows_of(near_refs[i // 6], i % 6), chip >= d) for i, d in enumerate(distances)],
        )

    minus = jnp.where(iota((HD, HD), 0) < 3, -1.0, 0.0).astype(bf16)
    peak_ref[...] = dot(wide_ref[:, HD:], minus)

    @pl.when(jnp.logical_not(jnp.max(sums_ref[:, HD:]) < HUGE))
    def _():
        @pl.loop(0, LOCAL)
        def _(h):
            rows = pl.ds(pl.multiple_of(h * BLOCK, BLOCK), BLOCK)
            query = wide_ref[rows, :HD]
            whole = jnp.zeros((BLOCK, SHARE), jnp.int32)

            def add(carry, source, i, allowed):
                peak, total, summed = carry
                pltpu.sync_copy(source.at[pl.ds(pl.multiple_of(i * SHARE, SHARE), SHARE), :], held_ref)
                scores = jnp.where(allowed, dot(query, held_ref[:, :HD], NT), NEG)
                top = jnp.maximum(peak, jnp.max(scores, axis=1, keepdims=True))
                probs = jnp.where(allowed, jnp.exp2((scores - top) * SCALE), 0.0)
                factor = jnp.exp2((peak - top) * SCALE)
                total = factor * total + jnp.sum(probs, axis=1, keepdims=True)
                return top, total, factor * summed + dot(probs.astype(bf16), held_ref[:, HD:])

            def diagonal_part(j, carry):
                return add(carry, kv_ref, j, j * SHARE + iota((BLOCK, SHARE), 1) <= iota((BLOCK, SHARE), 0))

            def far_part(j, carry):
                first = jnp.where(core == 1, 0, CHIPS)
                distance = jnp.where(j == 0, first, jnp.where(j == 4, CHIPS, j % 4 * 5))
                return add(carry, far_ref, j, whole + chip >= distance)

            carry = (jnp.full((BLOCK, 1), NEG, f32), jnp.zeros((BLOCK, 1), f32), jnp.zeros((BLOCK, HD), f32))
            if diagonal:
                carry = lax.fori_loop(0, 2, diagonal_part, carry)
            carry = lax.fori_loop(0, 8, far_part, carry)
            for source, ref in enumerate(near_refs):

                def near_part(j, carry):
                    return add(carry, ref, j, whole + chip >= distances[6 * source] + j % 3 * 5)

                carry = lax.fori_loop(0, 6, near_part, carry)
            peak, total, summed = carry
            sums_ref[rows, :] = jnp.concatenate([summed, jnp.broadcast_to(total, (BLOCK, HD))], 1)
            peak_ref[rows, :] = jnp.broadcast_to(peak, (BLOCK, HD))

    lane = iota((BLOCK, HD), 1)
    stats = jnp.zeros((BLOCK, HD), f32)
    for h in range(LOCAL):
        rows = slice(h * BLOCK, (h + 1) * BLOCK)
        out_ref[:, h * HD : (h + 1) * HD] = sums_ref[rows, :HD].astype(out_ref.dtype)
        stats = jnp.where(lane % LOCAL == h, jnp.where(lane < 3 * LOCAL, sums_ref[rows, HD:], peak_ref[rows, :]), stats)
    hi, mid, lo = split3(stats)
    part = lane // LOCAL % 3
    stats = jnp.where(part == 0, hi, jnp.where(part == 1, mid, lo))
    out_ref[:, LOCAL * HD :] = stats.astype(out_ref.dtype)


def merge_kernel(mine_ref, other_ref, out_ref):
    wide = LOCAL * HD
    lane, head = iota((HD, wide), 0), iota((HD, wide), 1) // HD

    def spread(ref, i):
        chosen = (lane // LOCAL // 3 == i) & (lane % LOCAL == head) & (lane < 6 * LOCAL)
        return dot(ref[:, wide:].astype(bf16), jnp.where(chosen, 1.0, 0.0).astype(bf16))

    here, there = spread(mine_ref, 1), spread(other_ref, 1)
    top = jnp.maximum(here, there)
    here, there = jnp.exp2((here - top) * SCALE), jnp.exp2((there - top) * SCALE)
    whole = here * spread(mine_ref, 0) + there * spread(other_ref, 0)
    summed = here * mine_ref[:, :wide].astype(f32) + there * other_ref[:, :wide].astype(f32)
    out_ref[...] = (summed / whole).astype(bf16)


def attention(place, query, kv, share, chip, below):
    brought = [lax.ppermute(share, "seq", on_both(pairs)) for pairs in FIFTH]
    query, _ = lax.optimization_barrier((query, chip))
    mate = lax.ppermute(query, "head", MATES)
    brought, _ = lax.optimization_barrier((jnp.concatenate([share, *brought]), chip))
    far = lax.all_gather(brought, "seq", axis=0, tiled=True, axis_index_groups=PAIRS)
    far, below = lax.optimization_barrier((far, below))
    out = lax.dynamic_slice_in_dim(far.reshape(2, 4 * SHARE, 2 * HD), place[0] % 2 * SHARE, 3 * SHARE, 1)
    out = out.reshape(6 * SHARE, 2 * HD)
    next1 = lax.ppermute(out, "seq", on_core(0, UP1) + on_core(1, DOWN1))
    second1 = lax.ppermute(out, "seq", on_core(0, UP2) + on_core(1, DOWN2))
    near, window = windows(chip, below)
    wide, sums = call(
        near_kernel,
        [shape(2 * ROWS, 2 * HD, dtype=bf16), shape(2 * ROWS, 2 * HD)],
        place,
        query,
        mate,
        kv,
        far,
        name="attend_near",
        limit=32,
        flops=4 * ROWS * 8 * BLOCK * 2 * HD,
    )
    next1, second1, sums, window = lax.optimization_barrier((next1, second1, sums, window))
    next2 = lax.ppermute(next1, "seq", SWAP)
    second2 = lax.ppermute(second1, "seq", SWAP)

    def rest(side, dtype):
        def kernel(*refs):
            rest_kernel(side == 0, *refs)

        return pl.pallas_call(
            kernel,
            out_shape=shape(BLOCK, LOCAL * HD + HD, dtype=dtype),
            grid_spec=pltpu.PrefetchScalarGridSpec(
                num_scalar_prefetch=1,
                grid=(1,),
                in_specs=[pl.BlockSpec((ROWS, 2 * HD), lambda i, place: (side, 0))] * 2
                + [pl.BlockSpec(out.shape, lambda i, place: (0, 0))] * 4
                + [pl.BlockSpec(memory_space=pl.ANY)] * 2,
                out_specs=pl.BlockSpec((BLOCK, LOCAL * HD + HD), lambda i, place: (0, 0)),
                scratch_shapes=[
                    pltpu.VMEM((ROWS, 2 * HD), f32),
                    pltpu.VMEM((ROWS, HD), f32),
                    pltpu.VMEM((SHARE, 2 * HD), bf16),
                ],
            ),
            compiler_params=pltpu.CompilerParams(vmem_limit_bytes=32 * 2**20),
            cost_estimate=pl.CostEstimate(
                flops=4 * ROWS * 12 * BLOCK * 2 * HD, bytes_accessed=2**22, transcendentals=0
            ),
            name="attend_rest",
        )(place, wide, sums, next1, second1, next2, second2, kv, far)

    other = lax.ppermute(rest(1, bf16), "head", MATES)
    mine = rest(0, f32)
    soft_out = pl.pallas_call(merge_kernel, out_shape=shape(*query.shape, dtype=bf16), name="merge")(mine, other)
    return soft_out, window, near, mine


def local(light_query, light_keys, light_values, log_decay, light_gain, query2, keys2, values2):
    place = jnp.stack([lax.axis_index("seq"), lax.axis_index("head")]).astype(jnp.int32)
    kv, share = pick(place, keys2, values2)
    both, chip, below = chip_states(place, light_keys, light_values, log_decay)
    soft_out, window, near, mine = attention(place, query2, kv, share, chip, below)
    light_out = mixed(
        place, light_query, light_keys, light_values, log_decay, light_gain, both, near, window, mine
    )
    return (light_out, soft_out)


def solution(mesh):
    placed = (
        P("seq", "head"),
        P("seq", "head"),
        P("seq", "head"),
        P("head", "seq"),
        P("head"),
        P("seq", "head"),
        P("seq", None),
        P("seq", None),
    )
    return jax.shard_map(
        local,
        mesh=mesh,
        in_specs=placed,
        out_specs=(P("seq", "head"), P("seq", "head")),
        check_vma=False,
    )
```

time: 194 us -> 157 us (0.81)
  starting transfers between devices: 10.7 us -> 33.3 us
  blocking collectives: 27.7 us -> 7.13 us
  waiting for transfers between devices: 31 us -> 12 us
  between operations: 14 us -> 0.99 us
  Pallas kernels: 104 us -> 97.6 us
    ppermute x0 -> x14, starting transfers between devices: none -> 33.3 us  [the longest x1 9.59 us: attention(): second1 = lax.ppermute(out, 'seq', on_core(0, UP2) + on_core(1, DOWN2))]
    all_to_all x1 -> x0, blocking collectives: 27.7 us -> none  [lightning(): pieces = lax.all_to_all(sent, 'seq', 0, 0)]
    all_gather x1 -> x0, waiting for transfers between devices: 20.4 us -> none  [local(): gathered = lax.all_gather(kv, 'seq', axis=0, tiled=True)]
    ppermute x0 -> x14, waiting for transfers between devices: none -> 12 us  [the longest x1 8.61 us: windows(): below2 = lax.ppermute(window(chip, below), 'seq', on_both(NEAR[1]))]
    all_to_all x1 -> x0, starting transfers between devices: 10.6 us -> none  [lightning(): state = lax.all_to_all(before, 'seq', 0, 0).reshape(LOCAL * HD, HD)]
    all_to_all x1 -> x0, waiting for transfers between devices: 10.5 us -> none  [lightning(): state = lax.all_to_all(before, 'seq', 0, 0).reshape(LOCAL * HD, HD)]
    all_gather x0 -> x3, blocking collectives: none -> 7.13 us  [the longest x1 2.52 us: attention(): lax.all_gather(brought, 'seq', axis=0, tiled=True, axis_index_groups=PAIRS)]
    pallas_call x6 -> x11, Pallas kernels: 104 us -> 97.6 us  [the longest x2 77.7 us: rest(): pl.pallas_call(kernel, out_shape=shape(BLOCK, LOCAL * HD + HD, dtype=dtyp...]
  transfers between devices with their start and end apart: 2 -> 14, of which waited for: 2 -> 3; matrix products, arithmetic and copies ran while one was open for 0% -> 1% of each run, Pallas kernels for 5% -> 60%
where the time goes in v2:
time: 157 us; the launch traced here: 156 us
  Pallas kernels  97.6 us (62%)
  starting transfers between devices  33.3 us (21%)
  waiting for transfers between devices  12 us (8%)
  blocking collectives  7.13 us (5%)
  local copies, waits for them, and re-layouts  3.55 us (2%)
    pallas_call x2, Pallas kernels, rest(): pl.pallas_call(kernel, out_shape=shape(BLOCK, LOCAL * HD + HD, dtype=dtyp...  77.7 us
    ppermute x1, starting transfers between devices, attention(): second1 = lax.ppermute(out, 'seq', on_core(0, UP2) + on_core(1, DOWN2))  9.59 us
    ppermute x1, waiting for transfers between devices, windows(): below2 = lax.ppermute(window(chip, below), 'seq', on_both(NEAR[1]))  8.61 us
    pallas_call x3, Pallas kernels, call(): pl.pallas_call(kernel, out_shape=out_shape, grid_spec=pltpu.PrefetchScala...  7.43 us
    ppermute x3, starting transfers between devices, attention(): brought = [lax.ppermute(share, 'seq', on_both(pairs)) for pairs in FIFTH]  4 us
    ppermute x3, starting transfers between devices, mixed(): far = [lax.ppermute(window, 'seq', on_both(pairs)) for pairs in FAR]  3.88 us
    unnamed x34, local copies, waits for them, and re-layouts  3.52 us
    ppermute x1, starting transfers between devices, attention(): other = lax.ppermute(rest(1, bf16), 'head', MATES)  3.35 us
  transfers between devices with their start and end apart: 14, of which 3 were waited for; matrix products, arithmetic and copies ran while one was open for 1% of the time, Pallas kernels for 60%

profile of v2, /device:TPU:481, one launch (start us, length us, event | category | flops | bytes accessed | tf_op | source)
XLA Modules:
  0.0 156.0 jit_solution(12109326247011348816)
XLA Ops:
  1.2 2.4 %pick.1 = (bf16[256,256]{1,0:T(8,128)(2,1)}, bf16[128,256]{1,0:T(8,128)(2,1)}) custom-call(s32[2]{0:T(128)} %pad_add_fusion.place_ref.refs_0_, bf16[256,1024]{1,0:T(8,128)(2,1)} %keys_ref.4, bf16[256,1024]{1,0:T(8,128)(2,1)} %values_ref.4), custom_call_target="tpu_custom_call" | custom-call | tf_op jit(solution)/shard_map/pick/pallas_call | solution.py:110
  3.6 1.4 collective-permute-start.2
  5.0 1.3 collective-permute-start.1
  6.3 1.3 collective-permute-start
  7.6 2.6 %block_state.1 = bf16[528,128]{1,0:T(8,128)(2,1)} custom-call(bf16[256,512]{1,0:T(8,128)(2,1)} %keys_ref.5, bf16[256,512]{1,0:T(8,128)(2,1)} %values_ref.5, f32[4,256]{1,0:T(4,128)} %decay_ref.3), custom_call_target="tpu_custom_call" | custom-call | tf_op jit(solution)/shard_map/block_state/pallas_call | solution.py:237
  10.2 2.5 %all_gather.9.both_ref = bf16[1056,128]{1,0:T(8,128)(2,1)S(1)} all-gather(bf16[528,128]{1,0:T(8,128)(2,1)} %block_state.1), channel_id=1, replica_groups={{0,16},{32,48},{64,80},{96,112},{128,144},{160,176},{192,208},{224,240}..., dimensions={0}, use_global_device_ids=true | all-gather | bytes 405504 | tf_op jit(solution)/shard_map/all_gather | solution.py:240
  14.8 3.1 %collective-permute-start.7 = (bf16[256,512]{1,0:T(8,128)(2,1)S(1)}, bf16[256,512]{1,0:T(8,128)(2,1)S(1)}, u32[]{:S(2)}, u32[]{:S(2)}) collective-permute-start(bf16[256,512]{1,0:T(8,128)(2,1)S(1)} %copy-done.8), channel_id=1, source_target_pairs={{0,1},{1,0},{2,3},{3,2},{4,5},{5,4},{6,7},{7,6},{8,9},{9,8},{10,11... | collective-permute-start | bytes 786440 | tf_op jit(solution)/shard_map/ppermute | solution.py:425
  18.2 3.1 %collective-permute-done = bf16[128,256]{1,0:T(8,128)(2,1)S(1)} collective-permute-done((bf16[128,256]{1,0:T(8,128)(2,1)}, bf16[128,256]{1,0:T(8,128)(2,1)S(1)}, u32[]{:S(2)}, u32[]{:S(2)}) %collective-permute-start) | collective-permute-done | bytes 65568 | tf_op jit(solution)/shard_map/ppermute | solution.py:423
  22.1 2.5 %all_gather.10.far_ref.refs_8_ = bf16[1024,256]{1,0:T(8,128)(2,1)S(1)} all-gather(bf16[512,256]{1,0:T(8,128)(2,1)S(1)} %pad_maximum_fusion), channel_id=1, replica_groups={{0,16},{32,48},{64,80},{96,112},{128,144},{160,176},{192,208},{224,240}..., dimensions={0}, use_global_device_ids=true | all-gather | bytes 786432 | tf_op jit(solution)/shard_map/all_gather | solution.py:427
  24.7 2.5 %collective-permute-start.5 = (bf16[768,256]{1,0:T(8,128)(2,1)S(1)}, bf16[768,256]{1,0:T(8,128)(2,1)S(1)}, u32[]{:S(2)}, u32[]{:S(2)}) collective-permute-start(bf16[768,256]{1,0:T(8,128)(2,1)S(1)} %bitcast.7), channel_id=1, source_target_pairs={{0,32},{32,64},{64,96},{96,128},{128,160},{160,192},{192,224},{224... | collective-permute-start | bytes 1179656 | tf_op jit(solution)/shard_map/ppermute | solution.py:431
  27.1 9.6 %collective-permute-start.6 = (bf16[768,256]{1,0:T(8,128)(2,1)S(1)}, bf16[768,256]{1,0:T(8,128)(2,1)S(1)}, u32[]{:S(2)}, u32[]{:S(2)}) collective-permute-start(bf16[768,256]{1,0:T(8,128)(2,1)S(1)} %bitcast.8), channel_id=1, source_target_pairs={{0,64},{32,96},{64,128},{96,160},{128,192},{160,224},{192,256},{22... | collective-permute-start | bytes 1179656 | tf_op jit(solution)/shard_map/ppermute | solution.py:432
  36.8 1.6 %window_state.2 = bf16[272,128]{1,0:T(8,128)(2,1)} custom-call(bf16[272,128]{1,0:T(8,128)(2,1)} %copy-done.3, bf16[272,128]{1,0:T(8,128)(2,1)} %copy-done.10), custom_call_target="tpu_custom_call" | custom-call | tf_op jit(solution)/shard_map/window_state/pallas_call | solution.py:250
  39.7 8.6 %collective-permute-done.4.refs_2_.near2_ref = bf16[272,128]{1,0:T(8,128)(2,1)S(1)} collective-permute-done((bf16[272,128]{1,0:T(8,128)(2,1)}, bf16[272,128]{1,0:T(8,128)(2,1)S(1)}, u32[]{:S(2)}, u32[]{:S(2)}) %collective-permute-start.4) | collective-permute-done | bytes 69664 | tf_op jit(solution)/shard_map/ppermute | solution.py:252
  48.9 1.7 %window_state.3 = bf16[272,128]{1,0:T(8,128)(2,1)} custom-call(bf16[272,128]{1,0:T(8,128)(2,1)} %copy-done.3, bf16[272,128]{1,0:T(8,128)(2,1)} %copy-done.10, bf16[272,128]{1,0:T(8,128)(2,1)} %copy-done.12), custom_call_target="tpu_custom_call" | custom-call | tf_op jit(solution)/shard_map/window_state/pallas_call | solution.py:250
  50.6 4.1 %attend_near.1 = (bf16[2048,256]{1,0:T(8,128)(2,1)S(1)}, f32[2048,256]{1,0:T(8,128)S(1)}) custom-call(s32[2]{0:T(128)S(1)} %copy-done.6, bf16[256,512]{1,0:T(8,128)(2,1)S(1)} %copy-done.8, bf16[256,512]{1,0:T(8,128)(2,1)S(1)} %collective-permute-done.7.mate_ref, bf16[256,256]{1,0:T(8,128)(2,1)S(1)} %copy-done.9, bf16[1024,256]{1,0:T(8,128)(2,1)S(1)} %all_gather.10.far_ref.refs_8_), custom_call_target="tpu_custom_call" | custom-call | flops 2147483648 | bytes 1179648 | tf_op jit(solution)/shard_map/attend_near/pallas_call | solution.py:83
  54.8 1.9 %collective-permute-start.11 = (bf16[768,256]{1,0:T(8,128)(2,1)S(1)}, bf16[768,256]{1,0:T(8,128)(2,1)S(1)}, u32[]{:S(2)}, u32[]{:S(2)}) collective-permute-start(bf16[768,256]{1,0:T(8,128)(2,1)S(1)} %collective-permute-done.5.refs_3_), channel_id=1, source_target_pairs={{0,16},{16,0},{32,48},{48,32},{64,80},{80,64},{96,112},{112,96},{1... | collective-permute-start | bytes 1179656 | tf_op jit(solution)/shard_map/ppermute | solution.py:447
  56.7 2.4 %collective-permute-start.12 = (bf16[768,256]{1,0:T(8,128)(2,1)S(1)}, bf16[768,256]{1,0:T(8,128)(2,1)S(1)}, u32[]{:S(2)}, u32[]{:S(2)}) collective-permute-start(bf16[768,256]{1,0:T(8,128)(2,1)S(1)} %collective-permute-done.6.refs_4_), channel_id=1, source_target_pairs={{0,16},{16,0},{32,48},{48,32},{64,80},{80,64},{96,112},{112,96},{1... | collective-permute-start | bytes 1179656 | tf_op jit(solution)/shard_map/ppermute | solution.py:448
  63.1 4.6 %attend_rest.3 = bf16[256,640]{1,0:T(8,128)(2,1)S(1)} custom-call(s32[2]{0:T(128)S(1)} %copy-done.6, bf16[2048,256]{1,0:T(8,128)(2,1)S(1)} %get-tuple-element.25.refs_1_, f32[2048,256]{1,0:T(8,128)S(1)} %get-tuple-element.26.refs_2_, bf16[768,256]{1,0:T(8,128)(2,1)S(1)} %collective-permute-done.5.refs_3_, ...), custom_call_target="tpu_custom_call" | custom-call | flops 3221225472 | bytes 4194304 | tf_op jit(solution)/shard_map/attend_rest/pallas_call | solution.py:454
  67.7 3.4 %collective-permute-start.13 = (bf16[256,640]{1,0:T(8,128)(2,1)S(1)}, bf16[256,640]{1,0:T(8,128)(2,1)S(1)}, u32[]{:S(2)}, u32[]{:S(2)}) collective-permute-start(bf16[256,640]{1,0:T(8,128)(2,1)S(1)} %attend_rest.3), channel_id=1, source_target_pairs={{0,1},{1,0},{2,3},{3,2},{4,5},{5,4},{6,7},{7,6},{8,9},{9,8},{10,11... | collective-permute-start | bytes 983048 | tf_op jit(solution)/shard_map/ppermute | solution.py:477
  71.0 73.2 %attend_rest.2.mine_ref = f32[256,640]{1,0:T(8,128)S(1)} custom-call(s32[2]{0:T(128)S(1)} %copy-done.6, bf16[2048,256]{1,0:T(8,128)(2,1)S(1)} %get-tuple-element.25.refs_1_, f32[2048,256]{1,0:T(8,128)S(1)} %get-tuple-element.26.refs_2_, bf16[768,256]{1,0:T(8,128)(2,1)S(1)} %collective-permute-done.5.refs_3_, ...), custom_call_target="tpu_custom_call" | custom-call | flops 3221225472 | bytes 4194304 | tf_op jit(solution)/shard_map/attend_rest/pallas_call | solution.py:454
  146.4 1.8 %state_before.1 = bf16[256,128]{1,0:T(8,128)(2,1)} custom-call(bf16[272,128]{1,0:T(8,128)(2,1)} %copy-done.10, bf16[272,128]{1,0:T(8,128)(2,1)} %copy-done.12, bf16[272,128]{1,0:T(8,128)(2,1)} %copy-done.13, bf16[272,128]{1,0:T(8,128)(2,1)} %copy-done.14, bf16[272,128]{1,0:T(8,128)(2,1)} %copy-done.15), custom_call_target="tpu_custom_call" | custom-call | tf_op jit(solution)/shard_map/state_before/pallas_call | solution.py:259
  148.1 2.1 %all_gather.11.before_ref = bf16[512,128]{1,0:T(8,128)(2,1)S(1)} all-gather(bf16[256,128]{1,0:T(8,128)(2,1)} %state_before.1), channel_id=1, replica_groups={{0,16},{32,48},{64,80},{96,112},{128,144},{160,176},{192,208},{224,240}..., dimensions={0}, use_global_device_ids=true | all-gather | bytes 196608 | tf_op jit(solution)/shard_map/all_gather | solution.py:262
  150.3 2.6 %mix.1 = bf16[256,512]{1,0:T(8,128)(2,1)} custom-call(s32[2]{0:T(128)S(1)} %copy-done.6, bf16[256,512]{1,0:T(8,128)(2,1)S(1)} %copy-done.4, bf16[256,512]{1,0:T(8,128)(2,1)S(1)} %copy-done, bf16[256,512]{1,0:T(8,128)(2,1)S(1)} %copy-done.1, f32[4,256]{1,0:T(4,128)S(1)} %copy-done.5, f32[1,512]{1,0:T(1,128)S(1)} %bitcast.6, ...), custom_call_target="tpu_custom_call" | custom-call | bytes 1193984 | tf_op jit(solution)/shard_map/mix/pallas_call | solution.py:83
  153.6 2.4 %merge.1 = bf16[256,512]{1,0:T(8,128)(2,1)} custom-call(f32[256,640]{1,0:T(8,128)} %copy-done.2, bf16[256,640]{1,0:T(8,128)(2,1)} %copy-done.11), custom_call_target="tpu_custom_call" | custom-call | tf_op jit(solution)/shard_map/merge/pallas_call | solution.py:479
  (55 shorter events, 12.4 us)
Async XLA Ops:
  0.6 14.1 %copy-start.8 = (bf16[256,512]{1,0:T(8,128)(2,1)S(1)}, bf16[256,512]{1,0:T(8,128)(2,1)}, u32[]{:S(2)}) copy-start(bf16[256,512]{1,0:T(8,128)(2,1)} %query_ref.1) | copy-start | bytes 786436
  1.2 11.5 %copy-start.6 = (s32[2]{0:T(128)S(1)}, s32[2]{0:T(128)}, u32[]{:S(2)}) copy-start(s32[2]{0:T(128)} %pad_add_fusion.place_ref.refs_0_) | copy-start | bytes 28
  3.6 47.0 %copy-start.9 = (bf16[256,256]{1,0:T(8,128)(2,1)S(1)}, bf16[256,256]{1,0:T(8,128)(2,1)}, u32[]{:S(2)}) copy-start(bf16[256,256]{1,0:T(8,128)(2,1)} %get-tuple-element.22.kv_ref.refs_7_) | copy-start | bytes 393220
  3.6 14.3 %collective-permute-start.2 = (bf16[128,256]{1,0:T(8,128)(2,1)}, bf16[128,256]{1,0:T(8,128)(2,1)S(1)}, u32[]{:S(2)}, u32[]{:S(2)}) collective-permute-start(bf16[128,256]{1,0:T(8,128)(2,1)} %get-tuple-element.17), channel_id=1, source_target_pairs={{0,480},{32,0},{64,32},{16,496},{48,16},{80,48},{1,481},{33,1},{65... | collective-permute-start | bytes 196616 | tf_op jit(solution)/shard_map/ppermute | solution.py:423
  5.0 13.2 %collective-permute-start.1 = (bf16[128,256]{1,0:T(8,128)(2,1)}, bf16[128,256]{1,0:T(8,128)(2,1)S(1)}, u32[]{:S(2)}, u32[]{:S(2)}) collective-permute-start(bf16[128,256]{1,0:T(8,128)(2,1)} %get-tuple-element.17), channel_id=1, source_target_pairs={{0,320},{32,352},{64,384},{96,416},{128,448},{160,480},{192,0},{22... | collective-permute-start | bytes 196616 | tf_op jit(solution)/shard_map/ppermute | solution.py:423
  6.3 15.0 %collective-permute-start = (bf16[128,256]{1,0:T(8,128)(2,1)}, bf16[128,256]{1,0:T(8,128)(2,1)S(1)}, u32[]{:S(2)}, u32[]{:S(2)}) collective-permute-start(bf16[128,256]{1,0:T(8,128)(2,1)} %get-tuple-element.17), channel_id=1, source_target_pairs={{0,160},{32,192},{64,224},{96,256},{128,288},{160,320},{192,352},{... | collective-permute-start | bytes 196616 | tf_op jit(solution)/shard_map/ppermute | solution.py:423
  13.4 23.3 %copy-start.3 = (bf16[272,128]{1,0:T(8,128)(2,1)}, bf16[272,128]{1,0:T(8,128)(2,1)S(1)}, u32[]{:S(2)}) copy-start(bf16[272,128]{1,0:T(8,128)(2,1)S(1)} %chip_state.1.refs_0_) | copy-start | bytes 208900
  13.5 11.2 %collective-permute-start.3 = (bf16[272,128]{1,0:T(8,128)(2,1)S(1)}, bf16[272,128]{1,0:T(8,128)(2,1)S(1)}, u32[]{:S(2)}, u32[]{:S(2)}) collective-permute-start(bf16[272,128]{1,0:T(8,128)(2,1)S(1)} %chip_state.1.refs_0_), channel_id=1, source_target_pairs={{0,32},{32,64},{64,96},{96,128},{128,160},{160,192},{192,224},{224... | collective-permute-start | bytes 208904 | tf_op jit(solution)/shard_map/ppermute | solution.py:243
  14.8 35.8 %collective-permute-start.7 = (bf16[256,512]{1,0:T(8,128)(2,1)S(1)}, bf16[256,512]{1,0:T(8,128)(2,1)S(1)}, u32[]{:S(2)}, u32[]{:S(2)}) collective-permute-start(bf16[256,512]{1,0:T(8,128)(2,1)S(1)} %copy-done.8), channel_id=1, source_target_pairs={{0,1},{1,0},{2,3},{3,2},{4,5},{5,4},{6,7},{7,6},{8,9},{9,8},{10,11... | collective-permute-start | bytes 786440 | tf_op jit(solution)/shard_map/ppermute | solution.py:425
  24.6 12.1 %copy-start.10 = (bf16[272,128]{1,0:T(8,128)(2,1)}, bf16[272,128]{1,0:T(8,128)(2,1)S(1)}, u32[]{:S(2)}) copy-start(bf16[272,128]{1,0:T(8,128)(2,1)S(1)} %collective-permute-done.3.refs_1_.near1_ref) | copy-start | bytes 208900
  24.7 30.1 %collective-permute-start.5 = (bf16[768,256]{1,0:T(8,128)(2,1)S(1)}, bf16[768,256]{1,0:T(8,128)(2,1)S(1)}, u32[]{:S(2)}, u32[]{:S(2)}) collective-permute-start(bf16[768,256]{1,0:T(8,128)(2,1)S(1)} %bitcast.7), channel_id=1, source_target_pairs={{0,32},{32,64},{64,96},{96,128},{128,160},{160,192},{192,224},{224... | collective-permute-start | bytes 1179656 | tf_op jit(solution)/shard_map/ppermute | solution.py:431
  27.1 27.6 %collective-permute-start.6 = (bf16[768,256]{1,0:T(8,128)(2,1)S(1)}, bf16[768,256]{1,0:T(8,128)(2,1)S(1)}, u32[]{:S(2)}, u32[]{:S(2)}) collective-permute-start(bf16[768,256]{1,0:T(8,128)(2,1)S(1)} %bitcast.8), channel_id=1, source_target_pairs={{0,64},{32,96},{64,128},{96,160},{128,192},{160,224},{192,256},{22... | collective-permute-start | bytes 1179656 | tf_op jit(solution)/shard_map/ppermute | solution.py:432
  38.4 9.9 %collective-permute-start.4 = (bf16[272,128]{1,0:T(8,128)(2,1)}, bf16[272,128]{1,0:T(8,128)(2,1)S(1)}, u32[]{:S(2)}, u32[]{:S(2)}) collective-permute-start(bf16[272,128]{1,0:T(8,128)(2,1)} %window_state.2), channel_id=1, source_target_pairs={{0,64},{32,96},{64,128},{96,160},{128,192},{160,224},{192,256},{22... | collective-permute-start | bytes 208904 | tf_op jit(solution)/shard_map/ppermute | solution.py:252
  54.8 8.3 %collective-permute-start.11 = (bf16[768,256]{1,0:T(8,128)(2,1)S(1)}, bf16[768,256]{1,0:T(8,128)(2,1)S(1)}, u32[]{:S(2)}, u32[]{:S(2)}) collective-permute-start(bf16[768,256]{1,0:T(8,128)(2,1)S(1)} %collective-permute-done.5.refs_3_), channel_id=1, source_target_pairs={{0,16},{16,0},{32,48},{48,32},{64,80},{80,64},{96,112},{112,96},{1... | collective-permute-start | bytes 1179656 | tf_op jit(solution)/shard_map/ppermute | solution.py:447
  56.7 6.3 %collective-permute-start.12 = (bf16[768,256]{1,0:T(8,128)(2,1)S(1)}, bf16[768,256]{1,0:T(8,128)(2,1)S(1)}, u32[]{:S(2)}, u32[]{:S(2)}) collective-permute-start(bf16[768,256]{1,0:T(8,128)(2,1)S(1)} %collective-permute-done.6.refs_4_), channel_id=1, source_target_pairs={{0,16},{16,0},{32,48},{48,32},{64,80},{80,64},{96,112},{112,96},{1... | collective-permute-start | bytes 1179656 | tf_op jit(solution)/shard_map/ppermute | solution.py:448
  59.1 85.9 %collective-permute-start.8 = (bf16[272,128]{1,0:T(8,128)(2,1)S(1)}, bf16[272,128]{1,0:T(8,128)(2,1)S(1)}, u32[]{:S(2)}, u32[]{:S(2)}) collective-permute-start(bf16[272,128]{1,0:T(8,128)(2,1)S(1)} %copy-done.16), channel_id=1, source_target_pairs={{0,128},{32,160},{64,192},{96,224},{128,256},{160,288},{192,320},{... | collective-permute-start | bytes 208904 | tf_op jit(solution)/shard_map/ppermute | solution.py:257
  60.4 84.6 %collective-permute-start.9 = (bf16[272,128]{1,0:T(8,128)(2,1)S(1)}, bf16[272,128]{1,0:T(8,128)(2,1)S(1)}, u32[]{:S(2)}, u32[]{:S(2)}) collective-permute-start(bf16[272,128]{1,0:T(8,128)(2,1)S(1)} %copy-done.16), channel_id=1, source_target_pairs={{0,256},{32,288},{64,320},{96,352},{128,384},{160,416},{192,448},{... | collective-permute-start | bytes 208904 | tf_op jit(solution)/shard_map/ppermute | solution.py:257
  61.7 83.4 %collective-permute-start.10 = (bf16[272,128]{1,0:T(8,128)(2,1)S(1)}, bf16[272,128]{1,0:T(8,128)(2,1)S(1)}, u32[]{:S(2)}, u32[]{:S(2)}) collective-permute-start(bf16[272,128]{1,0:T(8,128)(2,1)S(1)} %copy-done.16), channel_id=1, source_target_pairs={{0,384},{32,416},{64,448},{96,480},{16,400},{48,432},{80,464},{112... | collective-permute-start | bytes 208904 | tf_op jit(solution)/shard_map/ppermute | solution.py:257
  67.6 82.6 %copy-start = (bf16[256,512]{1,0:T(8,128)(2,1)S(1)}, bf16[256,512]{1,0:T(8,128)(2,1)}, u32[]{:S(2)}) copy-start(bf16[256,512]{1,0:T(8,128)(2,1)} %keys_ref.5) | copy-start | bytes 786436
  67.6 82.6 %copy-start.1 = (bf16[256,512]{1,0:T(8,128)(2,1)S(1)}, bf16[256,512]{1,0:T(8,128)(2,1)}, u32[]{:S(2)}) copy-start(bf16[256,512]{1,0:T(8,128)(2,1)} %values_ref.5) | copy-start | bytes 786436
  67.6 82.6 %copy-start.4 = (bf16[256,512]{1,0:T(8,128)(2,1)S(1)}, bf16[256,512]{1,0:T(8,128)(2,1)}, u32[]{:S(2)}) copy-start(bf16[256,512]{1,0:T(8,128)(2,1)} %query_ref.2) | copy-start | bytes 786436
  67.7 82.6 %copy-start.5 = (f32[4,256]{1,0:T(4,128)S(1)}, f32[4,256]{1,0:T(4,128)}, u32[]{:S(2)}) copy-start(f32[4,256]{1,0:T(4,128)} %decay_ref.3) | copy-start | bytes 12292
  67.7 82.6 %copy-start.7 = (f32[512]{0:T(512)S(1)}, f32[512]{0:T(512)}, u32[]{:S(2)}) copy-start(f32[512]{0:T(512)} %param.12) | copy-start | bytes 6148
  67.7 85.1 %collective-permute-start.13 = (bf16[256,640]{1,0:T(8,128)(2,1)S(1)}, bf16[256,640]{1,0:T(8,128)(2,1)S(1)}, u32[]{:S(2)}, u32[]{:S(2)}) collective-permute-start(bf16[256,640]{1,0:T(8,128)(2,1)S(1)} %attend_rest.3), channel_id=1, source_target_pairs={{0,1},{1,0},{2,3},{3,2},{4,5},{5,4},{6,7},{7,6},{8,9},{9,8},{10,11... | collective-permute-start | bytes 983048 | tf_op jit(solution)/shard_map/ppermute | solution.py:477
  (7 other events, 12.6 us)

commit v3 on v2

--- a/solution.py
+++ b/solution.py
@@ -11,7 +11,6 @@
 BLOCK = 256
 CHIPS = 16
 LOCAL = 4
-HALF = LOCAL // 2
 ROWS = LOCAL * BLOCK
 SHARE = BLOCK // 2
 SCALE = HD**-0.5 * 1.4426950408889634
@@ -21,17 +20,13 @@
 TN = (((0,), (0,)), ((), ()))
 f32, bf16 = jnp.float32, jnp.bfloat16
 
-FAR = (
-    [(z, z + 4) for z in range(12)],
-    [(z, z + 8) for z in range(8)],
-    [(z, z + 12) for z in range(4)],
-)
-FIFTH = (
-    [(z, z + 5) for z in range(11)] + [(11, 0), (12, 1)],
-    [(z, z + 10) for z in range(6)] + [(6, 0), (7, 1)],
-    [(0, 15), (1, 0), (2, 1)],
-)
-NEAR = [[(z, z + d) for z in range(CHIPS - d)] for d in (1, 2)]
+def below(distance):
+    return [(z, z + distance) for z in range(CHIPS - distance)]
+
+
+FIVE = below(5) + [(11, 0), (12, 1)]
+TEN = below(10) + [(6, 0), (7, 1)]
+FIFTEEN = below(15) + [(1, 0), (2, 1)]
 UP1 = [(z, z + 1) for z in range(15)]
 UP2 = [(z, z + 2) for z in range(14)]
 DOWN1 = [(z, z - 1) for z in range(5, 16)] + [(0, 15)]
@@ -42,10 +37,6 @@
     return [(2 * a + core, 2 * b + core) for a, b in chips]
 
 
-def on_both(chips):
-    return on_core(0, chips) + on_core(1, chips)
-
-
 PAIRS = [[s, s + 1] for s in range(0, 2 * CHIPS, 2)]
 SWAP = [(s, s ^ 1) for s in range(2 * CHIPS)]
 MATES = [(h, h ^ 1) for h in range(16)]
@@ -57,6 +48,10 @@
 
 def dot(a, b, dims=(((1,), (0,)), ((), ())), precision=None):
     return lax.dot_general(a, b, dims, precision=precision, preferred_element_type=f32)
+
+
+def after(*values):
+    return lax.optimization_barrier(values)
 
 
 def split3(x):
@@ -124,8 +119,8 @@
 
 
 STATE = LOCAL * HD
-CARRIED = HALF * HD
 TAIL = 16
+SENT = STATE + TAIL
 
 
 def decay_columns(decay):
@@ -158,56 +153,45 @@
     out_ref[STATE:, :] = told_rows([last[:, h : h + 1] for h in range(LOCAL)])
 
 
-def chip_kernel(place_ref, both_ref, out_ref):
-    core = place_ref[0] % 2
-    size = STATE + TAIL
-    first, second = told(both_ref[STATE:size, :]), told(both_ref[size + STATE :, :])
-    sums = []
-    for i in range(HALF):
-        start = pl.multiple_of((core * HALF + i) * HD, HD)
-
-        def head(row):
-            return jnp.where(core == 0, row[:, i : i + 1], row[:, HALF + i : HALF + i + 1])
-
-        later = head(second)
-        state = jnp.exp(later) * both_ref[pl.ds(start, HD), :].astype(f32)
-        state = state + both_ref[pl.ds(size + start, HD), :].astype(f32)
-        out_ref[i * HD : (i + 1) * HD, :] = state.astype(bf16)
-        sums.append(head(first) + later)
-    out_ref[CARRIED:, :] = told_rows(sums)
-
-
-def chain(refs):
-    states, total = [], None
-    decays = [told(ref[CARRIED:, :]) for ref in refs]
-    for i in range(HALF):
-        rows = slice(i * HD, (i + 1) * HD)
-        state = refs[-1][rows, :].astype(f32)
-        for ref, decay in zip(refs[-2::-1], decays[-2::-1]):
-            state = ref[rows, :].astype(f32) + jnp.exp(decay[:, i : i + 1]) * state
-        states.append(state)
-    total = sum(decays[1:], decays[0])
-    return states, total
-
-
-def window_kernel(*refs):
+def chain(parts):
+    decays = [told(part[STATE:, :]) for part in parts]
+
+    def state(h):
+        rows = slice(h * HD, (h + 1) * HD)
+        out = parts[-1][rows, :].astype(f32)
+        for part, decay in zip(parts[-2::-1], decays[-2::-1]):
+            out = part[rows, :].astype(f32) + jnp.exp(decay[:, h : h + 1]) * out
+        return out
+
+    return state, sum(decays[1:], decays[0])
+
+
+def chain_kernel(order, *refs):
     out_ref = refs[-1]
-    states, total = chain(refs[:-1])
-    for i, state in enumerate(states):
-        out_ref[i * HD : (i + 1) * HD, :] = state.astype(bf16)
-    out_ref[CARRIED:, :] = told_rows([total[:, i : i + 1] for i in range(HALF)])
-
-
-def before_kernel(near1_ref, near2_ref, far1_ref, far2_ref, far3_ref, out_ref):
-    near, decay = chain([near1_ref, near2_ref])
-    far, _ = chain([far1_ref, far2_ref, far3_ref])
-    for i in range(HALF):
-        state = near[i] + jnp.exp(decay[:, i : i + 1]) * far[i]
-        out_ref[i * HD : (i + 1) * HD, :] = state.astype(bf16)
+    state, total = chain([refs[i].at[j * SENT : (j + 1) * SENT] for i, j in order])
+    for h in range(LOCAL):
+        out_ref[h * HD : (h + 1) * HD, :] = state(h).astype(bf16)
+    out_ref[STATE:, :] = told_rows([total[:, h : h + 1] for h in range(LOCAL)])
+
+
+def chained(name, order, *arrays):
+    def kernel(*refs):
+        chain_kernel(order, *refs)
+
+    return pl.pallas_call(kernel, out_shape=shape(SENT, HD, dtype=bf16), name=name)(*arrays)
+
+
+JOINED = (0, 2, 1)
+
+
+def join(first, second):
+    return lax.all_gather(
+        jnp.concatenate([first, second]), "seq", axis=0, tiled=True, axis_index_groups=PAIRS
+    )
 
 
 def mix_kernel(
-    place_ref, query_ref, keys_ref, values_ref, decay_ref, gain_ref, both_ref, before_ref, out_ref
+    place_ref, query_ref, keys_ref, values_ref, decay_ref, gain_ref, both_ref, near_ref, far_ref, out_ref
 ):
     core = place_ref[0] % 2
     decay = decay_ref[...]
@@ -216,7 +200,9 @@
     along = dot(decay, upper, precision=lax.Precision.HIGHEST)
     grow = jnp.exp(running)
     lower = iota((BLOCK, BLOCK), 1) <= iota((BLOCK, BLOCK), 0)
-    first = jnp.exp(told(both_ref[STATE : STATE + TAIL, :]))
+    first = jnp.exp(told(both_ref[STATE:SENT, :]))
+    near, decays = chain([near_ref.at[j * SENT : (j + 1) * SENT] for j in JOINED])
+    far, _ = chain([far_ref.at[j * SENT : (j + 1) * SENT] for j in JOINED])
     for h in range(LOCAL):
         cols = slice(h * HD, (h + 1) * HD)
         query = query_ref[:, cols]
@@ -225,7 +211,7 @@
         lifted = query.astype(f32) * grow[:, h : h + 1]
         high = lifted.astype(bf16)
         low = (lifted - high.astype(f32)).astype(bf16)
-        state = before_ref[cols, :].astype(f32)
+        state = near(h) + jnp.exp(decays[:, h : h + 1]) * far(h)
         after = first[:, h : h + 1] * state + both_ref[cols, :].astype(f32)
         state = jnp.where(core == 0, state, after).astype(bf16)
         mixed = dot(weighted, values_ref[:, cols]) + dot(high, state) + dot(low, state)
@@ -233,47 +219,31 @@
         out_ref[:, cols] = (mixed * norm * gain_ref[:, cols]).astype(bf16)
 
 
-def chip_states(place, keys, values, decay):
-    mine = pl.pallas_call(state_kernel, out_shape=shape(STATE + TAIL, HD, dtype=bf16), name="block_state")(
+def chip_states(keys, values, decay):
+    mine = pl.pallas_call(state_kernel, out_shape=shape(SENT, HD, dtype=bf16), name="block_state")(
         keys, values, decay
     )
     both = lax.all_gather(mine, "seq", axis=0, tiled=True, axis_index_groups=PAIRS)
-    carried = shape(CARRIED + TAIL, HD, dtype=bf16)
-    chip = call(chip_kernel, carried, place, both, name="chip_state")
-    below = lax.ppermute(chip, "seq", on_both(NEAR[0]))
-    return both, chip, below
-
-
-def windows(chip, below):
-    def window(*parts):
-        out = shape(CARRIED + TAIL, HD, dtype=bf16)
-        return pl.pallas_call(window_kernel, out_shape=out, name="window_state")(*parts)
-
-    below2 = lax.ppermute(window(chip, below), "seq", on_both(NEAR[1]))
-    return [below, below2], window(chip, below, below2)
-
-
-def mixed(place, query, keys, values, decay, gain, both, near, window, after):
-    far = [lax.ppermute(window, "seq", on_both(pairs)) for pairs in FAR]
-    far, _ = lax.optimization_barrier((far, after))
-    before = pl.pallas_call(before_kernel, out_shape=shape(CARRIED, HD, dtype=bf16), name="state_before")(
-        *near, *far
-    )
-    before = lax.all_gather(before, "seq", axis=0, tiled=True, axis_index_groups=PAIRS)
-    gain = gain.reshape(1, LOCAL * HD)
-    out = shape(*query.shape, dtype=bf16)
-    return call(mix_kernel, out, place, query, keys, values, decay, gain, both, before, name="mix")
-
-
-FAR_BLOCKS = tuple((4 * core + i, 5 * i) for core in (0, 1) for i in (1, 2, 3))
+    return both, chained("chip_state", [(0, 1), (0, 0)], both)
+
+
+def bring(state, distances):
+    first, second, third = distances
+    return (
+        lax.ppermute(state, "seq", on_core(0, below(first)) + on_core(1, below(second))),
+        lax.ppermute(state, "seq", on_core(0, below(third))),
+    )
+
+
+FAR_BLOCKS = tuple((i, 15 - 5 * (i // 2)) for i in range(6))
 
 
 def near_blocks(core):
     out = []
     for side in range(2):
         for hops in (1, 2):
-            first = jnp.where(core == side, hops, 5 - hops)
-            out += [first + 5 * i for both in range(2) for i in range(3)]
+            first = jnp.where(core == side, 10 + hops, 15 - hops)
+            out += [first - 5 * (i // 2) for i in range(6)]
     return out
 
 
@@ -329,7 +299,7 @@
 
     @pl.when((chip >= 5) | (core == 1))
     def _():
-        blocks = [(rows_of(far_ref, 0), core == 1)]
+        blocks = [(rows_of(far_ref, 6), core == 1)]
         attend(wide_ref, sums_ref, blocks + [(rows_of(far_ref, i), chip >= d) for i, d in FAR_BLOCKS])
 
 
@@ -373,18 +343,17 @@
                 return add(carry, kv_ref, j, j * SHARE + iota((BLOCK, SHARE), 1) <= iota((BLOCK, SHARE), 0))
 
             def far_part(j, carry):
-                first = jnp.where(core == 1, 0, CHIPS)
-                distance = jnp.where(j == 0, first, jnp.where(j == 4, CHIPS, j % 4 * 5))
+                distance = jnp.where(j < 6, 15 - j // 2 * 5, jnp.where(core == 1, 0, CHIPS))
                 return add(carry, far_ref, j, whole + chip >= distance)
 
             carry = (jnp.full((BLOCK, 1), NEG, f32), jnp.zeros((BLOCK, 1), f32), jnp.zeros((BLOCK, HD), f32))
             if diagonal:
                 carry = lax.fori_loop(0, 2, diagonal_part, carry)
-            carry = lax.fori_loop(0, 8, far_part, carry)
+            carry = lax.fori_loop(0, 7, far_part, carry)
             for source, ref in enumerate(near_refs):
 
                 def near_part(j, carry):
-                    return add(carry, ref, j, whole + chip >= distances[6 * source] + j % 3 * 5)
+                    return add(carry, ref, j, whole + chip >= distances[6 * source] - j // 2 * 5)
 
                 carry = lax.fori_loop(0, 6, near_part, carry)
             peak, total, summed = carry
@@ -419,18 +388,23 @@
     out_ref[...] = (summed / whole).astype(bf16)
 
 
-def attention(place, query, kv, share, chip, below):
-    brought = [lax.ppermute(share, "seq", on_both(pairs)) for pairs in FIFTH]
-    query, _ = lax.optimization_barrier((query, chip))
+def attention(place, query, kv, own, chip):
+    core = place[0] % 2
+    far = lax.ppermute(own, "seq", on_core(0, TEN) + on_core(1, FIVE))
+    farther = lax.ppermute(own, "seq", on_core(0, FIFTEEN))
+    near = bring(chip, (1, 2, 3))
+    query, _ = after(query, chip)
     mate = lax.ppermute(query, "head", MATES)
-    brought, _ = lax.optimization_barrier((jnp.concatenate([share, *brought]), chip))
-    far = lax.all_gather(brought, "seq", axis=0, tiled=True, axis_index_groups=PAIRS)
-    far, below = lax.optimization_barrier((far, below))
-    out = lax.dynamic_slice_in_dim(far.reshape(2, 4 * SHARE, 2 * HD), place[0] % 2 * SHARE, 3 * SHARE, 1)
-    out = out.reshape(6 * SHARE, 2 * HD)
+    far = jnp.where(core == 0, jnp.concatenate([farther, far]), jnp.concatenate([far, own]))
+    far = lax.all_gather(far, "seq", axis=0, tiled=True, axis_index_groups=PAIRS)
+    out = lax.dynamic_slice_in_dim(far, (1 - core) * 2 * SHARE, 6 * SHARE, 0)
     next1 = lax.ppermute(out, "seq", on_core(0, UP1) + on_core(1, DOWN1))
     second1 = lax.ppermute(out, "seq", on_core(0, UP2) + on_core(1, DOWN2))
-    near, window = windows(chip, below)
+    _, *near = after(out, *near)
+    near = join(*near)
+    four = chained("window_state", [(0, 0)] + [(1, j) for j in JOINED], chip, near)
+    four_far = bring(four, (4, 8, 12))
+    far, _ = after(far, four)
     wide, sums = call(
         near_kernel,
         [shape(2 * ROWS, 2 * HD, dtype=bf16), shape(2 * ROWS, 2 * HD)],
@@ -443,9 +417,9 @@
         limit=32,
         flops=4 * ROWS * 8 * BLOCK * 2 * HD,
     )
-    next1, second1, sums, window = lax.optimization_barrier((next1, second1, sums, window))
     next2 = lax.ppermute(next1, "seq", SWAP)
     second2 = lax.ppermute(second1, "seq", SWAP)
+    wide, *four_far = after(wide, *four_far)
 
     def rest(side, dtype):
         def kernel(*refs):
@@ -477,16 +451,29 @@
     other = lax.ppermute(rest(1, bf16), "head", MATES)
     mine = rest(0, f32)
     soft_out = pl.pallas_call(merge_kernel, out_shape=shape(*query.shape, dtype=bf16), name="merge")(mine, other)
-    return soft_out, window, near, mine
+    return soft_out, near, four_far
 
 
 def local(light_query, light_keys, light_values, log_decay, light_gain, query2, keys2, values2):
     place = jnp.stack([lax.axis_index("seq"), lax.axis_index("head")]).astype(jnp.int32)
     kv, share = pick(place, keys2, values2)
-    both, chip, below = chip_states(place, light_keys, light_values, log_decay)
-    soft_out, window, near, mine = attention(place, query2, kv, share, chip, below)
-    light_out = mixed(
-        place, light_query, light_keys, light_values, log_decay, light_gain, both, near, window, mine
+    own = lax.all_gather(share, "seq", axis=0, tiled=True, axis_index_groups=PAIRS)
+    state_keys, _ = after(light_keys, own)
+    both, chip = chip_states(state_keys, light_values, log_decay)
+    soft_out, near, far = attention(place, query2, kv, own, chip)
+    light_out = call(
+        mix_kernel,
+        shape(*light_query.shape, dtype=bf16),
+        place,
+        light_query,
+        light_keys,
+        light_values,
+        log_decay,
+        light_gain.reshape(1, LOCAL * HD),
+        both,
+        near,
+        join(*far),
+        name="mix",
     )
     return (light_out, soft_out)
 

time: 157 us -> 147 us (0.936)
  blocking collectives: 7.13 us -> 24.3 us
  starting transfers between devices: 33.3 us -> 19.5 us
  waiting for transfers between devices: 12 us -> 5.77 us
  Pallas kernels: 97.6 us -> 93.2 us
  local copies, waits for them, and re-layouts: 3.55 us -> 1.65 us
    all_gather x2 -> x4, blocking collectives: 4.62 us -> 20 us  [the longest x2 9.14 us: join(): lax.all_gather(jnp.concatenate([first, second]), 'seq', axis=0, tiled=Tru...]
    ppermute x8 -> x6, waiting for transfers between devices: 12 us -> 4.21 us  [the longest x2 3.09 us: bring(): lax.ppermute(state, 'seq', on_core(0, below(first)) + on_core(1, below(se...]
    ppermute x1, starting transfers between devices: 9.59 us -> 2.1 us  [attention(): second1 = lax.ppermute(out, 'seq', on_core(0, UP2) + on_core(1, DOWN2))]
    ppermute x8 -> x6, starting transfers between devices: 10.4 us -> 5.85 us  [the longest x2 2.56 us: bring(): lax.ppermute(state, 'seq', on_core(0, below(first)) + on_core(1, below(se...]
    pallas_call x2, Pallas kernels: 77.7 us -> 75.5 us  [rest(): pl.pallas_call(kernel, out_shape=shape(BLOCK, LOCAL * HD + HD, dtype=dtyp...]
    unnamed x34 -> x24, local copies, waits for them, and re-layouts: 3.52 us -> 1.62 us
    all_gather x1, blocking collectives: 2.52 us -> 4.37 us  [chip_states(): lax.all_gather(mine, 'seq', axis=0, tiled=True, axis_index_groups=PAIRS)]
    pallas_call x4 -> x3, Pallas kernels: 7.68 us -> 6.27 us  [the longest x2 3.69 us: chained(): pl.pallas_call(kernel, out_shape=shape(SENT, HD, dtype=bf16), name=name)]
  transfers between devices with their start and end apart: 14 -> 12, of which waited for: 3 -> 3; matrix products, arithmetic and copies ran while one was open for 1% -> 0% of each run, Pallas kernels for 60% -> 57%
where the time goes in v3:
time: 147 us; the launch traced here: 146 us
  Pallas kernels  93.2 us (63%)
  blocking collectives  24.3 us (17%)
  starting transfers between devices  19.5 us (13%)
  waiting for transfers between devices  5.77 us (4%)
  local copies, waits for them, and re-layouts  1.65 us (1%)
    pallas_call x2, Pallas kernels, rest(): pl.pallas_call(kernel, out_shape=shape(BLOCK, LOCAL * HD + HD, dtype=dtyp...  75.5 us
    all_gather x2, blocking collectives, join(): lax.all_gather(jnp.concatenate([first, second]), 'seq', axis=0, tiled=Tru...  9.14 us
    all_gather x1, blocking collectives, attention(): lax.all_gather(far, 'seq', axis=0, tiled=True, axis_index_groups=PAIRS)  8.28 us
    pallas_call x2, Pallas kernels, call(): pl.pallas_call(kernel, out_shape=out_shape, grid_spec=pltpu.PrefetchScala...  6.66 us
    all_gather x1, blocking collectives, chip_states(): lax.all_gather(mine, 'seq', axis=0, tiled=True, axis_index_groups=PAIRS)  4.37 us
    pallas_call x2, Pallas kernels, chained(): pl.pallas_call(kernel, out_shape=shape(SENT, HD, dtype=bf16), name=name)  3.69 us
    ppermute x2, waiting for transfers between devices, bring(): lax.ppermute(state, 'seq', on_core(0, below(first)) + on_core(1, below(se...  3.09 us
  transfers between devices with their start and end apart: 12, of which 3 were waited for; matrix products, arithmetic and copies ran while one was open for 0% of the time, Pallas kernels for 57%

profile of v3, /device:TPU:481, one launch (start us, length us, event | category | flops | bytes accessed | tf_op | source)
XLA Modules:
  0.0 146.1 jit_solution(1482117577831195159)
XLA Ops:
  1.2 2.2 %pick.1 = (bf16[256,256]{1,0:T(8,128)(2,1)}, bf16[128,256]{1,0:T(8,128)(2,1)}) custom-call(s32[2]{0:T(128)} %pad_add_fusion.place_ref.refs_0_, bf16[256,1024]{1,0:T(8,128)(2,1)} %keys_ref.2, bf16[256,1024]{1,0:T(8,128)(2,1)} %values_ref.3), custom_call_target="tpu_custom_call" | custom-call | tf_op jit(solution)/shard_map/pick/pallas_call | solution.py:105
  3.5 2.6 %all_gather.15 = bf16[256,256]{1,0:T(8,128)(2,1)S(1)} all-gather(bf16[128,256]{1,0:T(8,128)(2,1)} %get-tuple-element.14), channel_id=1, replica_groups={{0,16},{32,48},{64,80},{96,112},{128,144},{160,176},{192,208},{224,240}..., dimensions={0}, use_global_device_ids=true | all-gather | bytes 196608 | tf_op jit(solution)/shard_map/all_gather | solution.py:460
  6.0 1.3 collective-permute-start.1
  8.0 2.6 %block_state.1 = bf16[528,128]{1,0:T(8,128)(2,1)} custom-call(bf16[256,512]{1,0:T(8,128)(2,1)} %keys_ref.4, bf16[256,512]{1,0:T(8,128)(2,1)} %values_ref.5, f32[4,256]{1,0:T(4,128)} %decay_ref.3), custom_call_target="tpu_custom_call" | custom-call | tf_op jit(solution)/shard_map/block_state/pallas_call | solution.py:223
  10.6 4.4 %all_gather.16.refs_0_.both_ref = bf16[1056,128]{1,0:T(8,128)(2,1)} all-gather(bf16[528,128]{1,0:T(8,128)(2,1)} %block_state.1), channel_id=1, replica_groups={{0,16},{32,48},{64,80},{96,112},{128,144},{160,176},{192,208},{224,240}..., dimensions={0}, use_global_device_ids=true | all-gather | bytes 405504 | tf_op jit(solution)/shard_map/all_gather | solution.py:226
  15.0 1.7 %chip_state.1.refs_0_ = bf16[528,128]{1,0:T(8,128)(2,1)} custom-call(bf16[1056,128]{1,0:T(8,128)(2,1)} %all_gather.16.refs_0_.both_ref), custom_call_target="tpu_custom_call" | custom-call | tf_op jit(solution)/shard_map/chip_state/pallas_call | solution.py:181
  16.7 1.3 collective-permute-start.2
  19.9 8.3 %all_gather.17.far_ref.refs_8_ = bf16[1024,256]{1,0:T(8,128)(2,1)S(1)} all-gather(bf16[512,256]{1,0:T(8,128)(2,1)S(1)} %maximum_select_fusion), channel_id=1, replica_groups={{0,16},{32,48},{64,80},{96,112},{128,144},{160,176},{192,208},{224,240}..., dimensions={0}, use_global_device_ids=true | all-gather | bytes 786432 | tf_op jit(solution)/shard_map/all_gather | solution.py:399
  28.2 1.9 %collective-permute-start.7 = (bf16[768,256]{1,0:T(8,128)(2,1)S(1)}, bf16[768,256]{1,0:T(8,128)(2,1)S(1)}, u32[]{:S(2)}, u32[]{:S(2)}) collective-permute-start(bf16[768,256]{1,0:T(8,128)(2,1)S(1)} %constant_dynamic-slice_fusion), channel_id=1, source_target_pairs={{0,32},{32,64},{64,96},{96,128},{128,160},{160,192},{192,224},{224... | collective-permute-start | bytes 1179656 | tf_op jit(solution)/shard_map/ppermute | solution.py:401
  30.1 2.1 %collective-permute-start.8 = (bf16[768,256]{1,0:T(8,128)(2,1)S(1)}, bf16[768,256]{1,0:T(8,128)(2,1)S(1)}, u32[]{:S(2)}, u32[]{:S(2)}) collective-permute-start(bf16[768,256]{1,0:T(8,128)(2,1)S(1)} %constant_dynamic-slice_fusion), channel_id=1, source_target_pairs={{0,64},{32,96},{64,128},{96,160},{128,192},{160,224},{192,256},{22... | collective-permute-start | bytes 1179656 | tf_op jit(solution)/shard_map/ppermute | solution.py:402
  32.2 2.7 %collective-permute-start.4 = (bf16[256,512]{1,0:T(8,128)(2,1)S(1)}, bf16[256,512]{1,0:T(8,128)(2,1)S(1)}, u32[]{:S(2)}, u32[]{:S(2)}) collective-permute-start(bf16[256,512]{1,0:T(8,128)(2,1)S(1)} %copy-done.9), channel_id=1, source_target_pairs={{0,1},{1,0},{2,3},{3,2},{4,5},{5,4},{6,7},{7,6},{8,9},{9,8},{10,11... | collective-permute-start | bytes 786440 | tf_op jit(solution)/shard_map/ppermute | solution.py:397
  35.0 2.3 %all_gather.18.refs_1_.near_ref = bf16[2112,128]{1,0:T(8,128)(2,1)} all-gather(bf16[1056,128]{1,0:T(8,128)(2,1)S(1)} %pad_maximum_fusion), channel_id=1, replica_groups={{0,16},{32,48},{64,80},{96,112},{128,144},{160,176},{192,208},{224,240}..., dimensions={0}, use_global_device_ids=true | all-gather | bytes 811008 | tf_op jit(solution)/shard_map/all_gather | solution.py:188
  37.3 2.0 %window_state.1 = bf16[528,128]{1,0:T(8,128)(2,1)} custom-call(bf16[528,128]{1,0:T(8,128)(2,1)} %chip_state.1.refs_0_, bf16[2112,128]{1,0:T(8,128)(2,1)} %all_gather.18.refs_1_.near_ref), custom_call_target="tpu_custom_call" | custom-call | tf_op jit(solution)/shard_map/window_state/pallas_call | solution.py:181
  41.2 1.5 %collective-permute-done.7.refs_3_ = bf16[768,256]{1,0:T(8,128)(2,1)S(1)} collective-permute-done((bf16[768,256]{1,0:T(8,128)(2,1)S(1)}, bf16[768,256]{1,0:T(8,128)(2,1)S(1)}, u32[]{:S(2)}, u32[]{:S(2)}) %collective-permute-start.7) | collective-permute-done | bytes 393248 | tf_op jit(solution)/shard_map/ppermute | solution.py:401
  42.8 1.9 %collective-permute-start.9 = (bf16[768,256]{1,0:T(8,128)(2,1)S(1)}, bf16[768,256]{1,0:T(8,128)(2,1)S(1)}, u32[]{:S(2)}, u32[]{:S(2)}) collective-permute-start(bf16[768,256]{1,0:T(8,128)(2,1)S(1)} %collective-permute-done.7.refs_3_), channel_id=1, source_target_pairs={{0,16},{16,0},{32,48},{48,32},{64,80},{80,64},{96,112},{112,96},{1... | collective-permute-start | bytes 1179656 | tf_op jit(solution)/shard_map/ppermute | solution.py:420
  44.7 2.4 %collective-permute-start.10 = (bf16[768,256]{1,0:T(8,128)(2,1)S(1)}, bf16[768,256]{1,0:T(8,128)(2,1)S(1)}, u32[]{:S(2)}, u32[]{:S(2)}) collective-permute-start(bf16[768,256]{1,0:T(8,128)(2,1)S(1)} %collective-permute-done.8.refs_4_), channel_id=1, source_target_pairs={{0,16},{16,0},{32,48},{48,32},{64,80},{80,64},{96,112},{112,96},{1... | collective-permute-start | bytes 1179656 | tf_op jit(solution)/shard_map/ppermute | solution.py:421
  47.1 4.1 %attend_near.1 = (bf16[2048,256]{1,0:T(8,128)(2,1)S(1)}, f32[2048,256]{1,0:T(8,128)S(1)}) custom-call(s32[2]{0:T(128)S(1)} %copy-done.8, bf16[256,512]{1,0:T(8,128)(2,1)S(1)} %copy-done.9, bf16[256,512]{1,0:T(8,128)(2,1)S(1)} %collective-permute-done.4.mate_ref, bf16[256,256]{1,0:T(8,128)(2,1)S(1)} %copy-done.10, ...), custom_call_target="tpu_custom_call" | custom-call | flops 2147483648 | bytes 1179648 | tf_op jit(solution)/shard_map/attend_near/pallas_call | solution.py:78
  51.2 3.1 %collective-permute-done.5 = bf16[528,128]{1,0:T(8,128)(2,1)S(1)} collective-permute-done((bf16[528,128]{1,0:T(8,128)(2,1)}, bf16[528,128]{1,0:T(8,128)(2,1)S(1)}, u32[]{:S(2)}, u32[]{:S(2)}) %collective-permute-start.5) | collective-permute-done | bytes 135200 | tf_op jit(solution)/shard_map/ppermute | solution.py:233
  54.5 4.5 %attend_rest.3 = bf16[256,640]{1,0:T(8,128)(2,1)S(1)} custom-call(s32[2]{0:T(128)S(1)} %copy-done.8, bf16[2048,256]{1,0:T(8,128)(2,1)S(1)} %get-tuple-element.24.refs_1_, f32[2048,256]{1,0:T(8,128)S(1)} %get-tuple-element.25.refs_2_, bf16[768,256]{1,0:T(8,128)(2,1)S(1)} %collective-permute-done.7.refs_3_, ...), custom_call_target="tpu_custom_call" | custom-call | flops 3221225472 | bytes 4194304 | tf_op jit(solution)/shard_map/attend_rest/pallas_call | solution.py:428
  59.0 2.6 %collective-permute-start.11 = (bf16[256,640]{1,0:T(8,128)(2,1)S(1)}, bf16[256,640]{1,0:T(8,128)(2,1)S(1)}, u32[]{:S(2)}, u32[]{:S(2)}) collective-permute-start(bf16[256,640]{1,0:T(8,128)(2,1)S(1)} %attend_rest.3), channel_id=1, source_target_pairs={{0,1},{1,0},{2,3},{3,2},{4,5},{5,4},{6,7},{7,6},{8,9},{9,8},{10,11... | collective-permute-start | bytes 983048 | tf_op jit(solution)/shard_map/ppermute | solution.py:451
  61.6 6.8 %all_gather.19.far_ref = bf16[2112,128]{1,0:T(8,128)(2,1)S(1)} all-gather(bf16[1056,128]{1,0:T(8,128)(2,1)S(1)} %pad_maximum_fusion.1), channel_id=1, replica_groups={{0,16},{32,48},{64,80},{96,112},{128,144},{160,176},{192,208},{224,240}..., dimensions={0}, use_global_device_ids=true | all-gather | bytes 811008 | tf_op jit(solution)/shard_map/all_gather | solution.py:188
  68.5 2.6 %mix.1 = bf16[256,512]{1,0:T(8,128)(2,1)} custom-call(s32[2]{0:T(128)S(1)} %copy-done.8, bf16[256,512]{1,0:T(8,128)(2,1)S(1)} %copy-done.5, bf16[256,512]{1,0:T(8,128)(2,1)S(1)} %copy-done.2, bf16[256,512]{1,0:T(8,128)(2,1)S(1)} %copy-done.3, f32[4,256]{1,0:T(4,128)S(1)} %copy-done.6, f32[1,512]{1,0:T(1,128)S(1)} %bitcast.3, ...), custom_call_target="tpu_custom_call" | custom-call | bytes 2144256 | tf_op jit(solution)/shard_map/mix/pallas_call | solution.py:78
  71.0 71.0 %attend_rest.2.mine_ref = f32[256,640]{1,0:T(8,128)S(1)} custom-call(s32[2]{0:T(128)S(1)} %copy-done.8, bf16[2048,256]{1,0:T(8,128)(2,1)S(1)} %get-tuple-element.24.refs_1_, f32[2048,256]{1,0:T(8,128)S(1)} %get-tuple-element.25.refs_2_, bf16[768,256]{1,0:T(8,128)(2,1)S(1)} %collective-permute-done.7.refs_3_, ...), custom_call_target="tpu_custom_call" | custom-call | flops 3221225472 | bytes 4194304 | tf_op jit(solution)/shard_map/attend_rest/pallas_call | solution.py:428
  143.7 2.4 %merge.1 = bf16[256,512]{1,0:T(8,128)(2,1)} custom-call(f32[256,640]{1,0:T(8,128)} %copy-done.4, bf16[256,640]{1,0:T(8,128)(2,1)} %copy-done.11), custom_call_target="tpu_custom_call" | custom-call | tf_op jit(solution)/shard_map/merge/pallas_call | solution.py:453
  (43 shorter events, 6.8 us)
Async XLA Ops:
  3.5 28.8 %copy-start.9 = (bf16[256,512]{1,0:T(8,128)(2,1)S(1)}, bf16[256,512]{1,0:T(8,128)(2,1)}, u32[]{:S(2)}) copy-start(bf16[256,512]{1,0:T(8,128)(2,1)} %query_ref.1) | copy-start | bytes 786436
  6.0 13.8 %collective-permute-start.1 = (bf16[256,256]{1,0:T(8,128)(2,1)S(1)}, bf16[256,256]{1,0:T(8,128)(2,1)S(1)}, u32[]{:S(2)}, u32[]{:S(2)}) collective-permute-start(bf16[256,256]{1,0:T(8,128)(2,1)S(1)} %all_gather.15), channel_id=1, source_target_pairs={{0,320},{32,352},{64,384},{96,416},{128,448},{160,480},{192,0},{22... | collective-permute-start | bytes 393224 | tf_op jit(solution)/shard_map/ppermute | solution.py:393
  7.3 12.5 %collective-permute-start = (bf16[256,256]{1,0:T(8,128)(2,1)S(1)}, bf16[256,256]{1,0:T(8,128)(2,1)S(1)}, u32[]{:S(2)}, u32[]{:S(2)}) collective-permute-start(bf16[256,256]{1,0:T(8,128)(2,1)S(1)} %all_gather.15), channel_id=1, source_target_pairs={{0,480},{32,0},{64,32},{1,481},{33,1},{65,33},{2,482},{34,2},{66,3... | collective-permute-start | bytes 393224 | tf_op jit(solution)/shard_map/ppermute | solution.py:394
  16.7 18.2 %collective-permute-start.2 = (bf16[528,128]{1,0:T(8,128)(2,1)}, bf16[528,128]{1,0:T(8,128)(2,1)S(1)}, u32[]{:S(2)}, u32[]{:S(2)}) collective-permute-start(bf16[528,128]{1,0:T(8,128)(2,1)} %chip_state.1.refs_0_), channel_id=1, source_target_pairs={{0,32},{32,64},{64,96},{96,128},{128,160},{160,192},{192,224},{224... | collective-permute-start | bytes 405512 | tf_op jit(solution)/shard_map/ppermute | solution.py:233
  18.0 16.9 %collective-permute-start.3 = (bf16[528,128]{1,0:T(8,128)(2,1)}, bf16[528,128]{1,0:T(8,128)(2,1)S(1)}, u32[]{:S(2)}, u32[]{:S(2)}) collective-permute-start(bf16[528,128]{1,0:T(8,128)(2,1)} %chip_state.1.refs_0_), channel_id=1, source_target_pairs={{0,96},{32,128},{64,160},{96,192},{128,224},{160,256},{192,288},{2... | collective-permute-start | bytes 405512 | tf_op jit(solution)/shard_map/ppermute | solution.py:234
  18.7 28.4 %copy-start.8 = (s32[2]{0:T(128)S(1)}, s32[2]{0:T(128)}, u32[]{:S(2)}) copy-start(s32[2]{0:T(128)} %pad_add_fusion.place_ref.refs_0_) | copy-start | bytes 28
  18.7 28.4 %copy-start.10 = (bf16[256,256]{1,0:T(8,128)(2,1)S(1)}, bf16[256,256]{1,0:T(8,128)(2,1)}, u32[]{:S(2)}) copy-start(bf16[256,256]{1,0:T(8,128)(2,1)} %get-tuple-element.19.kv_ref.refs_7_) | copy-start | bytes 393220
  28.2 14.6 %collective-permute-start.7 = (bf16[768,256]{1,0:T(8,128)(2,1)S(1)}, bf16[768,256]{1,0:T(8,128)(2,1)S(1)}, u32[]{:S(2)}, u32[]{:S(2)}) collective-permute-start(bf16[768,256]{1,0:T(8,128)(2,1)S(1)} %constant_dynamic-slice_fusion), channel_id=1, source_target_pairs={{0,32},{32,64},{64,96},{96,128},{128,160},{160,192},{192,224},{224... | collective-permute-start | bytes 1179656 | tf_op jit(solution)/shard_map/ppermute | solution.py:401
  30.1 14.6 %collective-permute-start.8 = (bf16[768,256]{1,0:T(8,128)(2,1)S(1)}, bf16[768,256]{1,0:T(8,128)(2,1)S(1)}, u32[]{:S(2)}, u32[]{:S(2)}) collective-permute-start(bf16[768,256]{1,0:T(8,128)(2,1)S(1)} %constant_dynamic-slice_fusion), channel_id=1, source_target_pairs={{0,64},{32,96},{64,128},{96,160},{128,192},{160,224},{192,256},{22... | collective-permute-start | bytes 1179656 | tf_op jit(solution)/shard_map/ppermute | solution.py:402
  32.2 14.9 %collective-permute-start.4 = (bf16[256,512]{1,0:T(8,128)(2,1)S(1)}, bf16[256,512]{1,0:T(8,128)(2,1)S(1)}, u32[]{:S(2)}, u32[]{:S(2)}) collective-permute-start(bf16[256,512]{1,0:T(8,128)(2,1)S(1)} %copy-done.9), channel_id=1, source_target_pairs={{0,1},{1,0},{2,3},{3,2},{4,5},{5,4},{6,7},{7,6},{8,9},{9,8},{10,11... | collective-permute-start | bytes 786440 | tf_op jit(solution)/shard_map/ppermute | solution.py:397
  39.3 15.1 %collective-permute-start.5 = (bf16[528,128]{1,0:T(8,128)(2,1)}, bf16[528,128]{1,0:T(8,128)(2,1)S(1)}, u32[]{:S(2)}, u32[]{:S(2)}) collective-permute-start(bf16[528,128]{1,0:T(8,128)(2,1)} %window_state.1), channel_id=1, source_target_pairs={{0,128},{32,160},{64,192},{96,224},{128,256},{160,288},{192,320},{... | collective-permute-start | bytes 405512 | tf_op jit(solution)/shard_map/ppermute | solution.py:233
  40.5 13.8 %collective-permute-start.6 = (bf16[528,128]{1,0:T(8,128)(2,1)}, bf16[528,128]{1,0:T(8,128)(2,1)S(1)}, u32[]{:S(2)}, u32[]{:S(2)}) collective-permute-start(bf16[528,128]{1,0:T(8,128)(2,1)} %window_state.1), channel_id=1, source_target_pairs={{0,384},{32,416},{64,448},{96,480},{1,385},{33,417},{65,449},{97,4... | collective-permute-start | bytes 405512 | tf_op jit(solution)/shard_map/ppermute | solution.py:234
  42.8 11.6 %collective-permute-start.9 = (bf16[768,256]{1,0:T(8,128)(2,1)S(1)}, bf16[768,256]{1,0:T(8,128)(2,1)S(1)}, u32[]{:S(2)}, u32[]{:S(2)}) collective-permute-start(bf16[768,256]{1,0:T(8,128)(2,1)S(1)} %collective-permute-done.7.refs_3_), channel_id=1, source_target_pairs={{0,16},{16,0},{32,48},{48,32},{64,80},{80,64},{96,112},{112,96},{1... | collective-permute-start | bytes 1179656 | tf_op jit(solution)/shard_map/ppermute | solution.py:420
  44.7 9.7 %collective-permute-start.10 = (bf16[768,256]{1,0:T(8,128)(2,1)S(1)}, bf16[768,256]{1,0:T(8,128)(2,1)S(1)}, u32[]{:S(2)}, u32[]{:S(2)}) collective-permute-start(bf16[768,256]{1,0:T(8,128)(2,1)S(1)} %collective-permute-done.8.refs_4_), channel_id=1, source_target_pairs={{0,16},{16,0},{32,48},{48,32},{64,80},{80,64},{96,112},{112,96},{1... | collective-permute-start | bytes 1179656 | tf_op jit(solution)/shard_map/ppermute | solution.py:421
  54.4 14.0 %copy-start = (bf16[2112,128]{1,0:T(8,128)(2,1)S(1)}, bf16[2112,128]{1,0:T(8,128)(2,1)}, u32[]{:S(2)}) copy-start(bf16[2112,128]{1,0:T(8,128)(2,1)} %all_gather.18.refs_1_.near_ref) | copy-start | bytes 1622020
  54.4 14.0 %copy-start.1 = (bf16[1056,128]{1,0:T(8,128)(2,1)S(1)}, bf16[1056,128]{1,0:T(8,128)(2,1)}, u32[]{:S(2)}) copy-start(bf16[1056,128]{1,0:T(8,128)(2,1)} %all_gather.16.refs_0_.both_ref) | copy-start | bytes 811012
  54.4 14.0 %copy-start.2 = (bf16[256,512]{1,0:T(8,128)(2,1)S(1)}, bf16[256,512]{1,0:T(8,128)(2,1)}, u32[]{:S(2)}) copy-start(bf16[256,512]{1,0:T(8,128)(2,1)} %keys_ref.4) | copy-start | bytes 786436
  54.4 14.0 %copy-start.3 = (bf16[256,512]{1,0:T(8,128)(2,1)S(1)}, bf16[256,512]{1,0:T(8,128)(2,1)}, u32[]{:S(2)}) copy-start(bf16[256,512]{1,0:T(8,128)(2,1)} %values_ref.5) | copy-start | bytes 786436
  54.4 14.0 %copy-start.5 = (bf16[256,512]{1,0:T(8,128)(2,1)S(1)}, bf16[256,512]{1,0:T(8,128)(2,1)}, u32[]{:S(2)}) copy-start(bf16[256,512]{1,0:T(8,128)(2,1)} %query_ref.2) | copy-start | bytes 786436
  54.4 14.0 %copy-start.6 = (f32[4,256]{1,0:T(4,128)S(1)}, f32[4,256]{1,0:T(4,128)}, u32[]{:S(2)}) copy-start(f32[4,256]{1,0:T(4,128)} %decay_ref.3) | copy-start | bytes 12292
  54.4 14.0 %copy-start.7 = (f32[512]{0:T(512)S(1)}, f32[512]{0:T(512)}, u32[]{:S(2)}) copy-start(f32[512]{0:T(512)} %param.12) | copy-start | bytes 6148
  59.0 84.0 %collective-permute-start.11 = (bf16[256,640]{1,0:T(8,128)(2,1)S(1)}, bf16[256,640]{1,0:T(8,128)(2,1)S(1)}, u32[]{:S(2)}, u32[]{:S(2)}) collective-permute-start(bf16[256,640]{1,0:T(8,128)(2,1)S(1)} %attend_rest.3), channel_id=1, source_target_pairs={{0,1},{1,0},{2,3},{3,2},{4,5},{5,4},{6,7},{7,6},{8,9},{9,8},{10,11... | collective-permute-start | bytes 983048 | tf_op jit(solution)/shard_map/ppermute | solution.py:451
  142.1 0.9 copy-start.4
  142.9 0.7 copy-start.11

commit v4 on v3

--- a/solution.py
+++ b/solution.py
@@ -93,29 +93,30 @@
     )(place, *args)
 
 
-def pick_kernel(place_ref, keys_ref, values_ref, out_ref, share_ref):
-    out_ref[:, :HD] = keys_ref[...]
-    out_ref[:, HD:] = values_ref[...]
-    start = pl.multiple_of(place_ref[1] % 2 * SHARE, SHARE)
+def pick_kernel(keys_ref, values_ref, out_ref, share_ref, sems):
+    head = lax.axis_index("head")
+    column = pl.ds(pl.multiple_of(head // 2 * HD, HD), HD)
+    copies = [
+        pltpu.make_async_copy(ref.at[:, column], out_ref.at[:, i * HD : (i + 1) * HD], sems.at[i])
+        for i, ref in enumerate((keys_ref, values_ref))
+    ]
+    for copy in copies:
+        copy.start()
+    for copy in copies:
+        copy.wait()
+    start = pl.multiple_of(head % 2 * SHARE, SHARE)
     share_ref[...] = out_ref[pl.ds(start, SHARE), :]
 
 
-def pick(place, keys2, values2):
-    column = pl.BlockSpec((BLOCK, HD), lambda i, place: (0, place[1] // 2))
+def pick(keys2, values2):
     return pl.pallas_call(
         pick_kernel,
         out_shape=[shape(BLOCK, 2 * HD, dtype=bf16), shape(SHARE, 2 * HD, dtype=bf16)],
-        grid_spec=pltpu.PrefetchScalarGridSpec(
-            num_scalar_prefetch=1,
-            grid=(1,),
-            in_specs=[column, column],
-            out_specs=[
-                pl.BlockSpec((BLOCK, 2 * HD), lambda i, place: (0, 0)),
-                pl.BlockSpec((SHARE, 2 * HD), lambda i, place: (0, 0)),
-            ],
-        ),
+        in_specs=[pl.BlockSpec(memory_space=pl.ANY)] * 2,
+        out_specs=[pl.BlockSpec(memory_space=pltpu.VMEM)] * 2,
+        scratch_shapes=[pltpu.SemaphoreType.DMA((2,))],
         name="pick",
-    )(place, keys2, values2)
+    )(keys2, values2)
 
 
 STATE = LOCAL * HD
@@ -190,9 +191,22 @@
     )
 
 
-def mix_kernel(
-    place_ref, query_ref, keys_ref, values_ref, decay_ref, gain_ref, both_ref, near_ref, far_ref, out_ref
+def last_kernel(
+    place_ref,
+    query_ref,
+    keys_ref,
+    values_ref,
+    decay_ref,
+    gain_ref,
+    both_ref,
+    near_ref,
+    far_ref,
+    mine_ref,
+    other_ref,
+    out_ref,
+    soft_ref,
 ):
+    add_sums(mine_ref, other_ref, soft_ref)
     core = place_ref[0] % 2
     decay = decay_ref[...]
     running = decay_columns(decay)
@@ -238,13 +252,9 @@
 FAR_BLOCKS = tuple((i, 15 - 5 * (i // 2)) for i in range(6))
 
 
-def near_blocks(core):
-    out = []
-    for side in range(2):
-        for hops in (1, 2):
-            first = jnp.where(core == side, 10 + hops, 15 - hops)
-            out += [first - 5 * (i // 2) for i in range(6)]
-    return out
+NEAR_BLOCKS = tuple(
+    first - 5 * (i // 2) for hops in (2, 1) for first in (10 + hops, 15 - hops) for i in range(6)
+)
 
 
 def attend(wide_ref, sums_ref, blocks):
@@ -297,26 +307,32 @@
             extra = jnp.where(col == 3, 1.0, extra)
             wide_ref[rows, :] = jnp.concatenate([query, extra.astype(bf16)], 1)
 
-    @pl.when((chip >= 5) | (core == 1))
+    first = (rows_of(far_ref, 6), core == 1)
+
+    @pl.when(chip >= 5)
     def _():
-        blocks = [(rows_of(far_ref, 6), core == 1)]
-        attend(wide_ref, sums_ref, blocks + [(rows_of(far_ref, i), chip >= d) for i, d in FAR_BLOCKS])
-
-
-def rest_kernel(diagonal, place_ref, wide_ref, sums_in_ref, *refs):
-    near_refs = refs[:4]
-    kv_ref, far_ref, out_ref, sums_ref, peak_ref, held_ref = refs[4:]
+        attend(wide_ref, sums_ref, [first] + [(rows_of(far_ref, i), chip >= d) for i, d in FAR_BLOCKS])
+
+    @pl.when((chip < 5) & (core == 1))
+    def _():
+        attend(wide_ref, sums_ref, [first])
+
+
+def rest_kernel(mine, place_ref, wide_ref, sums_in_ref, *refs):
+    near_refs = refs[:2]
+    kv_ref, far_ref, out_ref, sums_ref, peak_ref, held_ref = refs[2:]
     core, chip = place_ref[0] % 2, place_ref[0] // 2
-    distances = near_blocks(core)
     sums_ref[...] = sums_in_ref[...]
 
-    @pl.when(chip >= 1)
+    blocks = [(rows_of(near_refs[i // 12], i % 12), chip >= d, d) for i, d in enumerate(NEAR_BLOCKS)]
+
+    @pl.when(chip >= 5)
     def _():
-        attend(
-            wide_ref,
-            sums_ref,
-            [(rows_of(near_refs[i // 6], i % 6), chip >= d) for i, d in enumerate(distances)],
-        )
+        attend(wide_ref, sums_ref, [(rows, ok) for rows, ok, _ in blocks])
+
+    @pl.when((chip >= 1) & (chip < 5))
+    def _():
+        attend(wide_ref, sums_ref, [(rows, ok) for rows, ok, d in blocks if d < 5])
 
     minus = jnp.where(iota((HD, HD), 0) < 3, -1.0, 0.0).astype(bf16)
     peak_ref[...] = dot(wide_ref[:, HD:], minus)
@@ -347,15 +363,16 @@
                 return add(carry, far_ref, j, whole + chip >= distance)
 
             carry = (jnp.full((BLOCK, 1), NEG, f32), jnp.zeros((BLOCK, 1), f32), jnp.zeros((BLOCK, HD), f32))
-            if diagonal:
+            if mine:
                 carry = lax.fori_loop(0, 2, diagonal_part, carry)
             carry = lax.fori_loop(0, 7, far_part, carry)
             for source, ref in enumerate(near_refs):
 
                 def near_part(j, carry):
-                    return add(carry, ref, j, whole + chip >= distances[6 * source] - j // 2 * 5)
-
-                carry = lax.fori_loop(0, 6, near_part, carry)
+                    first = jnp.where(j < 6, 12 - source, 13 + source)
+                    return add(carry, ref, j, whole + chip >= first - j % 6 // 2 * 5)
+
+                carry = lax.fori_loop(0, 12, near_part, carry)
             peak, total, summed = carry
             sums_ref[rows, :] = jnp.concatenate([summed, jnp.broadcast_to(total, (BLOCK, HD))], 1)
             peak_ref[rows, :] = jnp.broadcast_to(peak, (BLOCK, HD))
@@ -372,7 +389,7 @@
     out_ref[:, LOCAL * HD :] = stats.astype(out_ref.dtype)
 
 
-def merge_kernel(mine_ref, other_ref, out_ref):
+def add_sums(mine_ref, other_ref, out_ref):
     wide = LOCAL * HD
     lane, head = iota((HD, wide), 0), iota((HD, wide), 1) // HD
 
@@ -384,7 +401,7 @@
     top = jnp.maximum(here, there)
     here, there = jnp.exp2((here - top) * SCALE), jnp.exp2((there - top) * SCALE)
     whole = here * spread(mine_ref, 0) + there * spread(other_ref, 0)
-    summed = here * mine_ref[:, :wide].astype(f32) + there * other_ref[:, :wide].astype(f32)
+    summed = here * mine_ref[:, :wide] + there * other_ref[:, :wide].astype(f32)
     out_ref[...] = (summed / whole).astype(bf16)
 
 
@@ -392,6 +409,7 @@
     core = place[0] % 2
     far = lax.ppermute(own, "seq", on_core(0, TEN) + on_core(1, FIVE))
     farther = lax.ppermute(own, "seq", on_core(0, FIFTEEN))
+    query, farther = after(query, farther)
     near = bring(chip, (1, 2, 3))
     query, _ = after(query, chip)
     mate = lax.ppermute(query, "head", MATES)
@@ -417,24 +435,24 @@
         limit=32,
         flops=4 * ROWS * 8 * BLOCK * 2 * HD,
     )
-    next2 = lax.ppermute(next1, "seq", SWAP)
-    second2 = lax.ppermute(second1, "seq", SWAP)
-    wide, *four_far = after(wide, *four_far)
+    next1 = lax.all_gather(next1, "seq", axis=0, tiled=True, axis_index_groups=PAIRS)
+    second1 = lax.all_gather(second1, "seq", axis=0, tiled=True, axis_index_groups=PAIRS)
 
     def rest(side, dtype):
         def kernel(*refs):
             rest_kernel(side == 0, *refs)
 
+        out = shape(BLOCK, LOCAL * HD + HD, dtype=dtype)
         return pl.pallas_call(
             kernel,
-            out_shape=shape(BLOCK, LOCAL * HD + HD, dtype=dtype),
+            out_shape=out,
             grid_spec=pltpu.PrefetchScalarGridSpec(
                 num_scalar_prefetch=1,
                 grid=(1,),
                 in_specs=[pl.BlockSpec((ROWS, 2 * HD), lambda i, place: (side, 0))] * 2
-                + [pl.BlockSpec(out.shape, lambda i, place: (0, 0))] * 4
+                + [pl.BlockSpec(next1.shape, lambda i, place: (0, 0))] * 2
                 + [pl.BlockSpec(memory_space=pl.ANY)] * 2,
-                out_specs=pl.BlockSpec((BLOCK, LOCAL * HD + HD), lambda i, place: (0, 0)),
+                out_specs=pl.BlockSpec(out.shape, lambda i, place: (0, 0)),
                 scratch_shapes=[
                     pltpu.VMEM((ROWS, 2 * HD), f32),
                     pltpu.VMEM((ROWS, HD), f32),
@@ -442,28 +460,27 @@
                 ],
             ),
             compiler_params=pltpu.CompilerParams(vmem_limit_bytes=32 * 2**20),
-            cost_estimate=pl.CostEstimate(
-                flops=4 * ROWS * 12 * BLOCK * 2 * HD, bytes_accessed=2**22, transcendentals=0
-            ),
+            cost_estimate=pl.CostEstimate(flops=0, bytes_accessed=0, transcendentals=0),
             name="attend_rest",
-        )(place, wide, sums, next1, second1, next2, second2, kv, far)
-
-    other = lax.ppermute(rest(1, bf16), "head", MATES)
-    mine = rest(0, f32)
-    soft_out = pl.pallas_call(merge_kernel, out_shape=shape(*query.shape, dtype=bf16), name="merge")(mine, other)
-    return soft_out, near, four_far
+        )(place, wide, sums, second1, next1, kv, far)
+
+    send = rest(1, bf16)
+    other = lax.ppermute(send, "head", MATES)
+    wide, *four_far = after(wide, *four_far, send)[:-1]
+    return rest(0, f32), other, near, four_far
 
 
 def local(light_query, light_keys, light_values, log_decay, light_gain, query2, keys2, values2):
     place = jnp.stack([lax.axis_index("seq"), lax.axis_index("head")]).astype(jnp.int32)
-    kv, share = pick(place, keys2, values2)
+    kv, share = pick(keys2, values2)
     own = lax.all_gather(share, "seq", axis=0, tiled=True, axis_index_groups=PAIRS)
     state_keys, _ = after(light_keys, own)
     both, chip = chip_states(state_keys, light_values, log_decay)
-    soft_out, near, far = attention(place, query2, kv, own, chip)
-    light_out = call(
-        mix_kernel,
-        shape(*light_query.shape, dtype=bf16),
+    mine, other, near, far = attention(place, query2, kv, own, chip)
+    out = shape(*light_query.shape, dtype=bf16)
+    light_out, soft_out = call(
+        last_kernel,
+        [out, out],
         place,
         light_query,
         light_keys,
@@ -473,7 +490,9 @@
         both,
         near,
         join(*far),
-        name="mix",
+        mine,
+        other,
+        name="mix_and_add",
     )
     return (light_out, soft_out)
 

time: 147 us -> 134 us (0.912)
  the two profiles are of different devices: /device:TPU:481 before, /device:TPU:501 now
where the time goes in v4:
time: 134 us; the launch traced here: 133 us
  Pallas kernels  90.4 us (67%)
  blocking collectives  24.2 us (18%)
  starting transfers between devices  15.7 us (12%)
  waiting for transfers between devices  1.74 us (1%)
    pallas_call x2, Pallas kernels, rest(): pl.pallas_call(kernel, out_shape=out, grid_spec=pltpu.PrefetchScalarGridS...  75.4 us
    all_gather x1, blocking collectives, attention(): lax.all_gather(far, 'seq', axis=0, tiled=True, axis_index_groups=PAIRS)  8.02 us
    pallas_call x2, Pallas kernels, call(): pl.pallas_call(kernel, out_shape=out_shape, grid_spec=pltpu.PrefetchScala...  7.15 us
    all_gather x2, blocking collectives, join(): lax.all_gather(jnp.concatenate([first, second]), 'seq', axis=0, tiled=Tru...  4.52 us
    all_gather x1, blocking collectives, chip_states(): lax.all_gather(mine, 'seq', axis=0, tiled=True, axis_index_groups=PAIRS)  4.37 us
    pallas_call x2, Pallas kernels, chained(): pl.pallas_call(kernel, out_shape=shape(SENT, HD, dtype=bf16), name=name)  3.69 us
    ppermute x1, starting transfers between devices, attention(): other = lax.ppermute(send, 'head', MATES)  3.13 us
    ppermute x1, starting transfers between devices, attention(): mate = lax.ppermute(query, 'head', MATES)  2.83 us
  transfers between devices with their start and end apart: 10, of which 2 were waited for; matrix products, arithmetic and copies ran while one was open for 0% of the time, Pallas kernels for 64%

profile of v4, /device:TPU:501, one launch (start us, length us, event | category | flops | bytes accessed | tf_op | source)
XLA Modules:
  0.0 133.1 jit_solution(18160496703954663885)
XLA Ops:
  0.6 1.6 %pick.1 = (bf16[256,256]{1,0:T(8,128)(2,1)}, bf16[128,256]{1,0:T(8,128)(2,1)}) custom-call(bf16[256,1024]{1,0:T(8,128)(2,1)} %keys_ref.2, bf16[256,1024]{1,0:T(8,128)(2,1)} %values_ref.3), custom_call_target="tpu_custom_call" | custom-call | tf_op jit(solution)/shard_map/pick/pallas_call | solution.py:112
  2.2 2.6 %all_gather.21 = bf16[256,256]{1,0:T(8,128)(2,1)S(1)} all-gather(bf16[128,256]{1,0:T(8,128)(2,1)} %get-tuple-element.16), channel_id=1, replica_groups={{0,16},{32,48},{64,80},{96,112},{128,144},{160,176},{192,208},{224,240}..., dimensions={0}, use_global_device_ids=true | all-gather | bytes 196608 | tf_op jit(solution)/shard_map/all_gather | solution.py:476
  4.8 1.3 collective-permute-start.1
  6.1 0.7 collective-permute-start
  6.8 2.6 %block_state.1 = bf16[528,128]{1,0:T(8,128)(2,1)} custom-call(bf16[256,512]{1,0:T(8,128)(2,1)} %keys_ref.4, bf16[256,512]{1,0:T(8,128)(2,1)} %values_ref.5, f32[4,256]{1,0:T(4,128)} %decay_ref.3), custom_call_target="tpu_custom_call" | custom-call | tf_op jit(solution)/shard_map/block_state/pallas_call | solution.py:237
  9.3 4.4 %all_gather.22.refs_0_.both_ref = bf16[1056,128]{1,0:T(8,128)(2,1)} all-gather(bf16[528,128]{1,0:T(8,128)(2,1)} %block_state.1), channel_id=1, replica_groups={{0,16},{32,48},{64,80},{96,112},{128,144},{160,176},{192,208},{224,240}..., dimensions={0}, use_global_device_ids=true | all-gather | bytes 405504 | tf_op jit(solution)/shard_map/all_gather | solution.py:240
  13.7 1.7 %chip_state.1.refs_0_ = bf16[528,128]{1,0:T(8,128)(2,1)} custom-call(bf16[1056,128]{1,0:T(8,128)(2,1)} %all_gather.22.refs_0_.both_ref), custom_call_target="tpu_custom_call" | custom-call | tf_op jit(solution)/shard_map/chip_state/pallas_call | solution.py:182
  16.1 1.3 collective-permute-start.2
  17.5 1.1 collective-permute-done.1
  18.6 8.0 %all_gather.23.far_ref.refs_6_ = bf16[1024,256]{1,0:T(8,128)(2,1)S(1)} all-gather(bf16[512,256]{1,0:T(8,128)(2,1)S(1)} %maximum_select_fusion), channel_id=1, replica_groups={{0,16},{32,48},{64,80},{96,112},{128,144},{160,176},{192,208},{224,240}..., dimensions={0}, use_global_device_ids=true | all-gather | bytes 786432 | tf_op jit(solution)/shard_map/all_gather | solution.py:417
  26.7 1.9 %collective-permute-start.8 = (bf16[768,256]{1,0:T(8,128)(2,1)S(1)}, bf16[768,256]{1,0:T(8,128)(2,1)S(1)}, u32[]{:S(2)}, u32[]{:S(2)}) collective-permute-start(bf16[768,256]{1,0:T(8,128)(2,1)S(1)} %constant_dynamic-slice_fusion), channel_id=1, source_target_pairs={{0,32},{32,64},{64,96},{96,128},{128,160},{160,192},{192,224},{224... | collective-permute-start | bytes 1179656 | tf_op jit(solution)/shard_map/ppermute | solution.py:419
  28.6 1.9 %collective-permute-start.7 = (bf16[768,256]{1,0:T(8,128)(2,1)S(1)}, bf16[768,256]{1,0:T(8,128)(2,1)S(1)}, u32[]{:S(2)}, u32[]{:S(2)}) collective-permute-start(bf16[768,256]{1,0:T(8,128)(2,1)S(1)} %constant_dynamic-slice_fusion), channel_id=1, source_target_pairs={{0,64},{32,96},{64,128},{96,160},{128,192},{160,224},{192,256},{22... | collective-permute-start | bytes 1179656 | tf_op jit(solution)/shard_map/ppermute | solution.py:420
  30.6 2.8 %collective-permute-start.4 = (bf16[256,512]{1,0:T(8,128)(2,1)S(1)}, bf16[256,512]{1,0:T(8,128)(2,1)S(1)}, u32[]{:S(2)}, u32[]{:S(2)}) collective-permute-start(bf16[256,512]{1,0:T(8,128)(2,1)S(1)} %copy-done.8), channel_id=1, source_target_pairs={{0,1},{1,0},{2,3},{3,2},{4,5},{5,4},{6,7},{7,6},{8,9},{9,8},{10,11... | collective-permute-start | bytes 786440 | tf_op jit(solution)/shard_map/ppermute | solution.py:415
  33.4 2.3 %all_gather.24.refs_1_.near_ref = bf16[2112,128]{1,0:T(8,128)(2,1)} all-gather(bf16[1056,128]{1,0:T(8,128)(2,1)S(1)} %pad_maximum_fusion), channel_id=1, replica_groups={{0,16},{32,48},{64,80},{96,112},{128,144},{160,176},{192,208},{224,240}..., dimensions={0}, use_global_device_ids=true | all-gather | bytes 811008 | tf_op jit(solution)/shard_map/all_gather | solution.py:189
  35.8 2.0 %window_state.1 = bf16[528,128]{1,0:T(8,128)(2,1)} custom-call(bf16[528,128]{1,0:T(8,128)(2,1)} %chip_state.1.refs_0_, bf16[2112,128]{1,0:T(8,128)(2,1)} %all_gather.24.refs_1_.near_ref), custom_call_target="tpu_custom_call" | custom-call | tf_op jit(solution)/shard_map/window_state/pallas_call | solution.py:182
  38.4 1.3 collective-permute-start.5
  40.4 4.1 %attend_near.1 = (bf16[2048,256]{1,0:T(8,128)(2,1)S(1)}, f32[2048,256]{1,0:T(8,128)S(1)}) custom-call(s32[2]{0:T(128)S(1)} %pad_add_fusion.place_ref.refs_0_, bf16[256,512]{1,0:T(8,128)(2,1)S(1)} %copy-done.8, bf16[256,512]{1,0:T(8,128)(2,1)S(1)} %collective-permute-done.4.mate_ref, bf16[256,256]{1,0:T(8,128)(2,1)S(1)} %copy-done.4, ...), custom_call_target="tpu_custom_call" | custom-call | flops 2147483648 | bytes 1179648 | tf_op jit(solution)/shard_map/attend_near/pallas_call | solution.py:78
  44.5 2.4 %all_gather.26.refs_4_ = bf16[1536,256]{1,0:T(8,128)(2,1)S(1)} all-gather(bf16[768,256]{1,0:T(8,128)(2,1)S(1)} %collective-permute-done.8), channel_id=1, replica_groups={{0,16},{32,48},{64,80},{96,112},{128,144},{160,176},{192,208},{224,240}..., dimensions={0}, use_global_device_ids=true | all-gather | bytes 1179648 | tf_op jit(solution)/shard_map/all_gather | solution.py:438
  46.8 2.4 %all_gather.25.refs_3_ = bf16[1536,256]{1,0:T(8,128)(2,1)S(1)} all-gather(bf16[768,256]{1,0:T(8,128)(2,1)S(1)} %collective-permute-done.7), channel_id=1, replica_groups={{0,16},{32,48},{64,80},{96,112},{128,144},{160,176},{192,208},{224,240}..., dimensions={0}, use_global_device_ids=true | all-gather | bytes 1179648 | tf_op jit(solution)/shard_map/all_gather | solution.py:439
  49.2 4.6 %attend_rest.2 = bf16[256,640]{1,0:T(8,128)(2,1)S(1)} custom-call(s32[2]{0:T(128)S(1)} %pad_add_fusion.place_ref.refs_0_, bf16[2048,256]{1,0:T(8,128)(2,1)S(1)} %get-tuple-element.29.refs_1_, f32[2048,256]{1,0:T(8,128)S(1)} %get-tuple-element.26.refs_2_, bf16[1536,256]{1,0:T(8,128)(2,1)S(1)} %all_gather.25.refs_3_, ...), custom_call_target="tpu_custom_call" | custom-call | tf_op jit(solution)/shard_map/attend_rest/pallas_call | solution.py:446
  53.9 3.1 %collective-permute-start.9 = (bf16[256,640]{1,0:T(8,128)(2,1)S(1)}, bf16[256,640]{1,0:T(8,128)(2,1)S(1)}, u32[]{:S(2)}, u32[]{:S(2)}) collective-permute-start(bf16[256,640]{1,0:T(8,128)(2,1)S(1)} %attend_rest.2), channel_id=1, source_target_pairs={{0,1},{1,0},{2,3},{3,2},{4,5},{5,4},{6,7},{7,6},{8,9},{9,8},{10,11... | collective-permute-start | bytes 983048 | tf_op jit(solution)/shard_map/ppermute | solution.py:468
  57.0 70.7 %attend_rest.3.mine_ref = f32[256,640]{1,0:T(8,128)S(1)} custom-call(s32[2]{0:T(128)S(1)} %pad_add_fusion.place_ref.refs_0_, bf16[2048,256]{1,0:T(8,128)(2,1)S(1)} %get-tuple-element.29.refs_1_, f32[2048,256]{1,0:T(8,128)S(1)} %get-tuple-element.26.refs_2_, bf16[1536,256]{1,0:T(8,128)(2,1)S(1)} %all_gather.25.refs_3_, ...), custom_call_target="tpu_custom_call" | custom-call | tf_op jit(solution)/shard_map/attend_rest/pallas_call | solution.py:446
  127.8 2.2 %all_gather.27.far_ref = bf16[2112,128]{1,0:T(8,128)(2,1)S(1)} all-gather(bf16[1056,128]{1,0:T(8,128)(2,1)S(1)} %pad_maximum_fusion.1), channel_id=1, replica_groups={{0,16},{32,48},{64,80},{96,112},{128,144},{160,176},{192,208},{224,240}..., dimensions={0}, use_global_device_ids=true | all-gather | bytes 811008 | tf_op jit(solution)/shard_map/all_gather | solution.py:189
  130.1 3.1 %mix_and_add.1 = (bf16[256,512]{1,0:T(8,128)(2,1)}, bf16[256,512]{1,0:T(8,128)(2,1)}) custom-call(s32[2]{0:T(128)S(1)} %pad_add_fusion.place_ref.refs_0_, bf16[256,512]{1,0:T(8,128)(2,1)S(1)} %copy-done.5, bf16[256,512]{1,0:T(8,128)(2,1)S(1)} %copy-done.2, bf16[256,512]{1,0:T(8,128)(2,1)S(1)} %copy-done.3, f32[4,256]{1,0:T(4,128)S(1)} %copy-done.6, ...), custom_call_target="tpu_custom_call" | custom-call | bytes 3127296 | tf_op jit(solution)/shard_map/mix_and_add/pallas_call | solution.py:78
  (34 shorter events, 2.3 us)
Async XLA Ops:
  2.2 28.3 %copy-start.8 = (bf16[256,512]{1,0:T(8,128)(2,1)S(1)}, bf16[256,512]{1,0:T(8,128)(2,1)}, u32[]{:S(2)}) copy-start(bf16[256,512]{1,0:T(8,128)(2,1)} %query_ref.1) | copy-start | bytes 786436
  4.8 13.8 %collective-permute-start.1 = (bf16[256,256]{1,0:T(8,128)(2,1)S(1)}, bf16[256,256]{1,0:T(8,128)(2,1)S(1)}, u32[]{:S(2)}, u32[]{:S(2)}) collective-permute-start(bf16[256,256]{1,0:T(8,128)(2,1)S(1)} %all_gather.21), channel_id=1, source_target_pairs={{0,320},{32,352},{64,384},{96,416},{128,448},{160,480},{192,0},{22... | collective-permute-start | bytes 393224 | tf_op jit(solution)/shard_map/ppermute | solution.py:410
  6.1 11.4 %collective-permute-start = (bf16[256,256]{1,0:T(8,128)(2,1)S(1)}, bf16[256,256]{1,0:T(8,128)(2,1)S(1)}, u32[]{:S(2)}, u32[]{:S(2)}) collective-permute-start(bf16[256,256]{1,0:T(8,128)(2,1)S(1)} %all_gather.21), channel_id=1, source_target_pairs={{0,480},{32,0},{64,32},{1,481},{33,1},{65,33},{2,482},{34,2},{66,3... | collective-permute-start | bytes 393224 | tf_op jit(solution)/shard_map/ppermute | solution.py:411
  15.4 17.9 %collective-permute-start.3 = (bf16[528,128]{1,0:T(8,128)(2,1)}, bf16[528,128]{1,0:T(8,128)(2,1)S(1)}, u32[]{:S(2)}, u32[]{:S(2)}) collective-permute-start(bf16[528,128]{1,0:T(8,128)(2,1)} %chip_state.1.refs_0_), channel_id=1, source_target_pairs={{0,96},{32,128},{64,160},{96,192},{128,224},{160,256},{192,288},{2... | collective-permute-start | bytes 405512 | tf_op jit(solution)/shard_map/ppermute | solution.py:248
  16.1 17.3 %collective-permute-start.2 = (bf16[528,128]{1,0:T(8,128)(2,1)}, bf16[528,128]{1,0:T(8,128)(2,1)S(1)}, u32[]{:S(2)}, u32[]{:S(2)}) collective-permute-start(bf16[528,128]{1,0:T(8,128)(2,1)} %chip_state.1.refs_0_), channel_id=1, source_target_pairs={{0,32},{32,64},{64,96},{96,128},{128,160},{160,192},{192,224},{224... | collective-permute-start | bytes 405512 | tf_op jit(solution)/shard_map/ppermute | solution.py:247
  17.5 22.8 %copy-start.4 = (bf16[256,256]{1,0:T(8,128)(2,1)S(1)}, bf16[256,256]{1,0:T(8,128)(2,1)}, u32[]{:S(2)}) copy-start(bf16[256,256]{1,0:T(8,128)(2,1)} %get-tuple-element.23.kv_ref.refs_5_) | copy-start | bytes 393220
  26.7 17.8 %collective-permute-start.8 = (bf16[768,256]{1,0:T(8,128)(2,1)S(1)}, bf16[768,256]{1,0:T(8,128)(2,1)S(1)}, u32[]{:S(2)}, u32[]{:S(2)}) collective-permute-start(bf16[768,256]{1,0:T(8,128)(2,1)S(1)} %constant_dynamic-slice_fusion), channel_id=1, source_target_pairs={{0,32},{32,64},{64,96},{96,128},{128,160},{160,192},{192,224},{224... | collective-permute-start | bytes 1179656 | tf_op jit(solution)/shard_map/ppermute | solution.py:419
  28.6 18.2 %collective-permute-start.7 = (bf16[768,256]{1,0:T(8,128)(2,1)S(1)}, bf16[768,256]{1,0:T(8,128)(2,1)S(1)}, u32[]{:S(2)}, u32[]{:S(2)}) collective-permute-start(bf16[768,256]{1,0:T(8,128)(2,1)S(1)} %constant_dynamic-slice_fusion), channel_id=1, source_target_pairs={{0,64},{32,96},{64,128},{96,160},{128,192},{160,224},{192,256},{22... | collective-permute-start | bytes 1179656 | tf_op jit(solution)/shard_map/ppermute | solution.py:420
  30.6 9.8 %collective-permute-start.4 = (bf16[256,512]{1,0:T(8,128)(2,1)S(1)}, bf16[256,512]{1,0:T(8,128)(2,1)S(1)}, u32[]{:S(2)}, u32[]{:S(2)}) collective-permute-start(bf16[256,512]{1,0:T(8,128)(2,1)S(1)} %copy-done.8), channel_id=1, source_target_pairs={{0,1},{1,0},{2,3},{3,2},{4,5},{5,4},{6,7},{7,6},{8,9},{9,8},{10,11... | collective-permute-start | bytes 786440 | tf_op jit(solution)/shard_map/ppermute | solution.py:415
  37.7 19.3 %collective-permute-start.6 = (bf16[528,128]{1,0:T(8,128)(2,1)}, bf16[528,128]{1,0:T(8,128)(2,1)S(1)}, u32[]{:S(2)}, u32[]{:S(2)}) collective-permute-start(bf16[528,128]{1,0:T(8,128)(2,1)} %window_state.1), channel_id=1, source_target_pairs={{0,384},{32,416},{64,448},{96,480},{1,385},{33,417},{65,449},{97,4... | collective-permute-start | bytes 405512 | tf_op jit(solution)/shard_map/ppermute | solution.py:248
  38.4 18.7 %collective-permute-start.5 = (bf16[528,128]{1,0:T(8,128)(2,1)}, bf16[528,128]{1,0:T(8,128)(2,1)S(1)}, u32[]{:S(2)}, u32[]{:S(2)}) collective-permute-start(bf16[528,128]{1,0:T(8,128)(2,1)} %window_state.1), channel_id=1, source_target_pairs={{0,128},{32,160},{64,192},{96,224},{128,256},{160,288},{192,320},{... | collective-permute-start | bytes 405512 | tf_op jit(solution)/shard_map/ppermute | solution.py:247
  53.8 76.2 %copy-start = (bf16[2112,128]{1,0:T(8,128)(2,1)S(1)}, bf16[2112,128]{1,0:T(8,128)(2,1)}, u32[]{:S(2)}) copy-start(bf16[2112,128]{1,0:T(8,128)(2,1)} %all_gather.24.refs_1_.near_ref) | copy-start | bytes 1622020
  53.8 76.2 %copy-start.1 = (bf16[1056,128]{1,0:T(8,128)(2,1)S(1)}, bf16[1056,128]{1,0:T(8,128)(2,1)}, u32[]{:S(2)}) copy-start(bf16[1056,128]{1,0:T(8,128)(2,1)} %all_gather.22.refs_0_.both_ref) | copy-start | bytes 811012
  53.8 76.2 %copy-start.2 = (bf16[256,512]{1,0:T(8,128)(2,1)S(1)}, bf16[256,512]{1,0:T(8,128)(2,1)}, u32[]{:S(2)}) copy-start(bf16[256,512]{1,0:T(8,128)(2,1)} %keys_ref.4) | copy-start | bytes 786436
  53.8 76.2 %copy-start.3 = (bf16[256,512]{1,0:T(8,128)(2,1)S(1)}, bf16[256,512]{1,0:T(8,128)(2,1)}, u32[]{:S(2)}) copy-start(bf16[256,512]{1,0:T(8,128)(2,1)} %values_ref.5) | copy-start | bytes 786436
  53.8 76.2 %copy-start.5 = (bf16[256,512]{1,0:T(8,128)(2,1)S(1)}, bf16[256,512]{1,0:T(8,128)(2,1)}, u32[]{:S(2)}) copy-start(bf16[256,512]{1,0:T(8,128)(2,1)} %query_ref.2) | copy-start | bytes 786436
  53.9 76.2 %copy-start.6 = (f32[4,256]{1,0:T(4,128)S(1)}, f32[4,256]{1,0:T(4,128)}, u32[]{:S(2)}) copy-start(f32[4,256]{1,0:T(4,128)} %decay_ref.3) | copy-start | bytes 12292
  53.9 76.2 %copy-start.7 = (f32[512]{0:T(512)S(1)}, f32[512]{0:T(512)}, u32[]{:S(2)}) copy-start(f32[512]{0:T(512)} %param.12) | copy-start | bytes 6148
  53.9 76.1 %collective-permute-start.9 = (bf16[256,640]{1,0:T(8,128)(2,1)S(1)}, bf16[256,640]{1,0:T(8,128)(2,1)S(1)}, u32[]{:S(2)}, u32[]{:S(2)}) collective-permute-start(bf16[256,640]{1,0:T(8,128)(2,1)S(1)} %attend_rest.2), channel_id=1, source_target_pairs={{0,1},{1,0},{2,3},{3,2},{4,5},{5,4},{6,7},{7,6},{8,9},{9,8},{10,11... | collective-permute-start | bytes 983048 | tf_op jit(solution)/shard_map/ppermute | solution.py:468

commit v5 on v4

--- a/solution.py
+++ b/solution.py
@@ -201,12 +201,8 @@
     both_ref,
     near_ref,
     far_ref,
-    mine_ref,
-    other_ref,
     out_ref,
-    soft_ref,
 ):
-    add_sums(mine_ref, other_ref, soft_ref)
     core = place_ref[0] % 2
     decay = decay_ref[...]
     running = decay_columns(decay)
@@ -478,9 +474,9 @@
     both, chip = chip_states(state_keys, light_values, log_decay)
     mine, other, near, far = attention(place, query2, kv, own, chip)
     out = shape(*light_query.shape, dtype=bf16)
-    light_out, soft_out = call(
+    light_out = call(
         last_kernel,
-        [out, out],
+        out,
         place,
         light_query,
         light_keys,
@@ -490,10 +486,10 @@
         both,
         near,
         join(*far),
-        mine,
-        other,
-        name="mix_and_add",
-    )
+        name="mix",
+    )
+    other, _ = after(other, light_out)
+    soft_out = pl.pallas_call(add_sums, out_shape=out, name="add_sums")(mine, other)
     return (light_out, soft_out)
 
 

time: 134 us -> 138 us (1.030)
  starting transfers between devices: 15.7 us -> 20.8 us
  blocking collectives: 24.2 us -> 19.4 us
  Pallas kernels: 90.4 us -> 92.3 us
    all_gather x1, blocking collectives: 8.02 us -> 2.84 us  [attention(): lax.all_gather(far, 'seq', axis=0, tiled=True, axis_index_groups=PAIRS)]
    ppermute x1, starting transfers between devices: 1.92 us -> 7.08 us  [attention(): next1 = lax.ppermute(out, 'seq', on_core(0, UP1) + on_core(1, DOWN1))]
    pallas_call x0 -> x1, Pallas kernels: none -> 2.43 us  [local(): pl.pallas_call(add_sums, out_shape=out, name='add_sums')(mine, other)]
  transfers between devices with their start and end apart: 10 -> 10, of which waited for: 2 -> 1; matrix products, arithmetic and copies ran while one was open for 0% -> 0% of each run, Pallas kernels for 64% -> 65%
where the time goes in v5:
time: 138 us; the launch traced here: 136 us
  Pallas kernels  92.3 us (67%)
  starting transfers between devices  20.8 us (15%)
  blocking collectives  19.4 us (14%)
  waiting for transfers between devices  2.01 us (1%)
    pallas_call x2, Pallas kernels, rest(): pl.pallas_call(kernel, out_shape=out, grid_spec=pltpu.PrefetchScalarGridS...  75.3 us
    ppermute x1, starting transfers between devices, attention(): next1 = lax.ppermute(out, 'seq', on_core(0, UP1) + on_core(1, DOWN1))  7.08 us
    pallas_call x2, Pallas kernels, call(): pl.pallas_call(kernel, out_shape=out_shape, grid_spec=pltpu.PrefetchScala...  6.68 us
    all_gather x2, blocking collectives, join(): lax.all_gather(jnp.concatenate([first, second]), 'seq', axis=0, tiled=Tru...  4.52 us
    all_gather x1, blocking collectives, chip_states(): lax.all_gather(mine, 'seq', axis=0, tiled=True, axis_index_groups=PAIRS)  4.36 us
    pallas_call x2, Pallas kernels, chained(): pl.pallas_call(kernel, out_shape=shape(SENT, HD, dtype=bf16), name=name)  3.69 us
    all_gather x1, blocking collectives, attention(): lax.all_gather(far, 'seq', axis=0, tiled=True, axis_index_groups=PAIRS)  2.84 us
    ppermute x1, starting transfers between devices, attention(): mate = lax.ppermute(query, 'head', MATES)  2.83 us
  transfers between devices with their start and end apart: 10, of which 1 were waited for; matrix products, arithmetic and copies ran while one was open for 0% of the time, Pallas kernels for 65%

profile of v5, /device:TPU:501, one launch (start us, length us, event | category | flops | bytes accessed | tf_op | source)
XLA Modules:
  0.0 136.4 jit_solution(2344100816299019172)
XLA Ops:
  0.6 1.6 %pick.1 = (bf16[256,256]{1,0:T(8,128)(2,1)}, bf16[128,256]{1,0:T(8,128)(2,1)}) custom-call(bf16[256,1024]{1,0:T(8,128)(2,1)} %keys_ref.2, bf16[256,1024]{1,0:T(8,128)(2,1)} %values_ref.3), custom_call_target="tpu_custom_call" | custom-call | tf_op jit(solution)/shard_map/pick/pallas_call | solution.py:112
  2.2 2.6 %all_gather.21 = bf16[256,256]{1,0:T(8,128)(2,1)S(1)} all-gather(bf16[128,256]{1,0:T(8,128)(2,1)} %get-tuple-element.17), channel_id=1, replica_groups={{0,16},{32,48},{64,80},{96,112},{128,144},{160,176},{192,208},{224,240}..., dimensions={0}, use_global_device_ids=true | all-gather | bytes 196608 | tf_op jit(solution)/shard_map/all_gather | solution.py:472
  5.5 1.3 collective-permute-start.1
  6.8 2.6 %block_state.1 = bf16[528,128]{1,0:T(8,128)(2,1)} custom-call(bf16[256,512]{1,0:T(8,128)(2,1)} %keys_ref.4, bf16[256,512]{1,0:T(8,128)(2,1)} %values_ref.5, f32[4,256]{1,0:T(4,128)} %decay_ref.3), custom_call_target="tpu_custom_call" | custom-call | tf_op jit(solution)/shard_map/block_state/pallas_call | solution.py:233
  9.3 4.4 %all_gather.22.refs_0_.both_ref = bf16[1056,128]{1,0:T(8,128)(2,1)} all-gather(bf16[528,128]{1,0:T(8,128)(2,1)} %block_state.1), channel_id=1, replica_groups={{0,16},{32,48},{64,80},{96,112},{128,144},{160,176},{192,208},{224,240}..., dimensions={0}, use_global_device_ids=true | all-gather | bytes 405504 | tf_op jit(solution)/shard_map/all_gather | solution.py:236
  13.7 1.7 %chip_state.1.refs_0_ = bf16[528,128]{1,0:T(8,128)(2,1)} custom-call(bf16[1056,128]{1,0:T(8,128)(2,1)} %all_gather.22.refs_0_.both_ref), custom_call_target="tpu_custom_call" | custom-call | tf_op jit(solution)/shard_map/chip_state/pallas_call | solution.py:182
  15.4 1.3 collective-permute-start.2
  17.5 2.0 %collective-permute-done.1 = bf16[256,256]{1,0:T(8,128)(2,1)S(1)} collective-permute-done((bf16[256,256]{1,0:T(8,128)(2,1)S(1)}, bf16[256,256]{1,0:T(8,128)(2,1)S(1)}, u32[]{:S(2)}, u32[]{:S(2)}) %collective-permute-start.1) | collective-permute-done | bytes 131104 | tf_op jit(solution)/shard_map/ppermute | solution.py:406
  19.6 2.8 %all_gather.23.far_ref.refs_6_ = bf16[1024,256]{1,0:T(8,128)(2,1)S(1)} all-gather(bf16[512,256]{1,0:T(8,128)(2,1)S(1)} %maximum_select_fusion), channel_id=1, replica_groups={{0,16},{32,48},{64,80},{96,112},{128,144},{160,176},{192,208},{224,240}..., dimensions={0}, use_global_device_ids=true | all-gather | bytes 786432 | tf_op jit(solution)/shard_map/all_gather | solution.py:413
  22.4 2.3 %collective-permute-start.7 = (bf16[768,256]{1,0:T(8,128)(2,1)S(1)}, bf16[768,256]{1,0:T(8,128)(2,1)S(1)}, u32[]{:S(2)}, u32[]{:S(2)}) collective-permute-start(bf16[768,256]{1,0:T(8,128)(2,1)S(1)} %constant_dynamic-slice_fusion), channel_id=1, source_target_pairs={{0,64},{32,96},{64,128},{96,160},{128,192},{160,224},{192,256},{22... | collective-permute-start | bytes 1179656 | tf_op jit(solution)/shard_map/ppermute | solution.py:416
  24.7 7.1 %collective-permute-start.8 = (bf16[768,256]{1,0:T(8,128)(2,1)S(1)}, bf16[768,256]{1,0:T(8,128)(2,1)S(1)}, u32[]{:S(2)}, u32[]{:S(2)}) collective-permute-start(bf16[768,256]{1,0:T(8,128)(2,1)S(1)} %constant_dynamic-slice_fusion), channel_id=1, source_target_pairs={{0,32},{32,64},{64,96},{96,128},{128,160},{160,192},{192,224},{224... | collective-permute-start | bytes 1179656 | tf_op jit(solution)/shard_map/ppermute | solution.py:415
  31.8 2.8 %collective-permute-start.4 = (bf16[256,512]{1,0:T(8,128)(2,1)S(1)}, bf16[256,512]{1,0:T(8,128)(2,1)S(1)}, u32[]{:S(2)}, u32[]{:S(2)}) collective-permute-start(bf16[256,512]{1,0:T(8,128)(2,1)S(1)} %copy-done.9), channel_id=1, source_target_pairs={{0,1},{1,0},{2,3},{3,2},{4,5},{5,4},{6,7},{7,6},{8,9},{9,8},{10,11... | collective-permute-start | bytes 786440 | tf_op jit(solution)/shard_map/ppermute | solution.py:411
  34.7 2.3 %all_gather.24.refs_1_.near_ref = bf16[2112,128]{1,0:T(8,128)(2,1)} all-gather(bf16[1056,128]{1,0:T(8,128)(2,1)S(1)} %pad_maximum_fusion), channel_id=1, replica_groups={{0,16},{32,48},{64,80},{96,112},{128,144},{160,176},{192,208},{224,240}..., dimensions={0}, use_global_device_ids=true | all-gather | bytes 811008 | tf_op jit(solution)/shard_map/all_gather | solution.py:189
  37.0 2.0 %window_state.1 = bf16[528,128]{1,0:T(8,128)(2,1)} custom-call(bf16[528,128]{1,0:T(8,128)(2,1)} %chip_state.1.refs_0_, bf16[2112,128]{1,0:T(8,128)(2,1)} %all_gather.24.refs_1_.near_ref), custom_call_target="tpu_custom_call" | custom-call | tf_op jit(solution)/shard_map/window_state/pallas_call | solution.py:182
  39.0 1.3 collective-permute-start.5
  40.9 4.1 %attend_near.1 = (bf16[2048,256]{1,0:T(8,128)(2,1)S(1)}, f32[2048,256]{1,0:T(8,128)S(1)}) custom-call(s32[2]{0:T(128)S(1)} %pad_add_fusion.place_ref.refs_0_, bf16[256,512]{1,0:T(8,128)(2,1)S(1)} %copy-done.9, bf16[256,512]{1,0:T(8,128)(2,1)S(1)} %collective-permute-done.4.mate_ref, bf16[256,256]{1,0:T(8,128)(2,1)S(1)} %copy-done.5, ...), custom_call_target="tpu_custom_call" | custom-call | flops 2147483648 | bytes 1179648 | tf_op jit(solution)/shard_map/attend_near/pallas_call | solution.py:78
  45.1 2.8 %all_gather.25.refs_3_ = bf16[1536,256]{1,0:T(8,128)(2,1)S(1)} all-gather(bf16[768,256]{1,0:T(8,128)(2,1)S(1)} %collective-permute-done.7), channel_id=1, replica_groups={{0,16},{32,48},{64,80},{96,112},{128,144},{160,176},{192,208},{224,240}..., dimensions={0}, use_global_device_ids=true | all-gather | bytes 1179648 | tf_op jit(solution)/shard_map/all_gather | solution.py:435
  47.8 2.4 %all_gather.26.refs_4_ = bf16[1536,256]{1,0:T(8,128)(2,1)S(1)} all-gather(bf16[768,256]{1,0:T(8,128)(2,1)S(1)} %collective-permute-done.8), channel_id=1, replica_groups={{0,16},{32,48},{64,80},{96,112},{128,144},{160,176},{192,208},{224,240}..., dimensions={0}, use_global_device_ids=true | all-gather | bytes 1179648 | tf_op jit(solution)/shard_map/all_gather | solution.py:434
  50.2 4.6 %attend_rest.2 = bf16[256,640]{1,0:T(8,128)(2,1)S(1)} custom-call(s32[2]{0:T(128)S(1)} %pad_add_fusion.place_ref.refs_0_, bf16[2048,256]{1,0:T(8,128)(2,1)S(1)} %get-tuple-element.30.refs_1_, f32[2048,256]{1,0:T(8,128)S(1)} %get-tuple-element.27.refs_2_, bf16[1536,256]{1,0:T(8,128)(2,1)S(1)} %all_gather.25.refs_3_, ...), custom_call_target="tpu_custom_call" | custom-call | tf_op jit(solution)/shard_map/attend_rest/pallas_call | solution.py:442
  54.8 2.8 %collective-permute-start.9 = (bf16[256,640]{1,0:T(8,128)(2,1)S(1)}, bf16[256,640]{1,0:T(8,128)(2,1)S(1)}, u32[]{:S(2)}, u32[]{:S(2)}) collective-permute-start(bf16[256,640]{1,0:T(8,128)(2,1)S(1)} %attend_rest.2), channel_id=1, source_target_pairs={{0,1},{1,0},{2,3},{3,2},{4,5},{5,4},{6,7},{7,6},{8,9},{9,8},{10,11... | collective-permute-start | bytes 983048 | tf_op jit(solution)/shard_map/ppermute | solution.py:464
  57.6 70.7 %attend_rest.3.mine_ref = f32[256,640]{1,0:T(8,128)S(1)} custom-call(s32[2]{0:T(128)S(1)} %pad_add_fusion.place_ref.refs_0_, bf16[2048,256]{1,0:T(8,128)(2,1)S(1)} %get-tuple-element.30.refs_1_, f32[2048,256]{1,0:T(8,128)S(1)} %get-tuple-element.27.refs_2_, bf16[1536,256]{1,0:T(8,128)(2,1)S(1)} %all_gather.25.refs_3_, ...), custom_call_target="tpu_custom_call" | custom-call | tf_op jit(solution)/shard_map/attend_rest/pallas_call | solution.py:442
  128.4 2.2 %all_gather.27.far_ref = bf16[2112,128]{1,0:T(8,128)(2,1)S(1)} all-gather(bf16[1056,128]{1,0:T(8,128)(2,1)S(1)} %pad_maximum_fusion.1), channel_id=1, replica_groups={{0,16},{32,48},{64,80},{96,112},{128,144},{160,176},{192,208},{224,240}..., dimensions={0}, use_global_device_ids=true | all-gather | bytes 811008 | tf_op jit(solution)/shard_map/all_gather | solution.py:189
  130.7 2.6 %mix.1 = bf16[256,512]{1,0:T(8,128)(2,1)} custom-call(s32[2]{0:T(128)S(1)} %pad_add_fusion.place_ref.refs_0_, bf16[256,512]{1,0:T(8,128)(2,1)S(1)} %copy-done.6, bf16[256,512]{1,0:T(8,128)(2,1)S(1)} %copy-done.3, bf16[256,512]{1,0:T(8,128)(2,1)S(1)} %copy-done.4, f32[4,256]{1,0:T(4,128)S(1)} %copy-done.7, f32[1,512]{1,0:T(1,128)S(1)} %bitcast.3, ...), custom_call_target="tpu_custom_call" | custom-call | bytes 2144256 | tf_op jit(solution)/shard_map/mix/pallas_call | solution.py:78
  134.0 2.4 %add_sums.1 = bf16[256,512]{1,0:T(8,128)(2,1)} custom-call(f32[256,640]{1,0:T(8,128)} %copy-done.1, bf16[256,640]{1,0:T(8,128)(2,1)} %copy-done.10), custom_call_target="tpu_custom_call" | custom-call | tf_op jit(solution)/shard_map/add_sums/pallas_call | solution.py:492
  (39 shorter events, 3.0 us)
Async XLA Ops:
  2.2 29.6 %copy-start.9 = (bf16[256,512]{1,0:T(8,128)(2,1)S(1)}, bf16[256,512]{1,0:T(8,128)(2,1)}, u32[]{:S(2)}) copy-start(bf16[256,512]{1,0:T(8,128)(2,1)} %query_ref.1) | copy-start | bytes 786436
  4.8 12.7 %collective-permute-start = (bf16[256,256]{1,0:T(8,128)(2,1)S(1)}, bf16[256,256]{1,0:T(8,128)(2,1)S(1)}, u32[]{:S(2)}, u32[]{:S(2)}) collective-permute-start(bf16[256,256]{1,0:T(8,128)(2,1)S(1)} %all_gather.21), channel_id=1, source_target_pairs={{0,480},{32,0},{64,32},{1,481},{33,1},{65,33},{2,482},{34,2},{66,3... | collective-permute-start | bytes 393224 | tf_op jit(solution)/shard_map/ppermute | solution.py:407
  5.5 14.0 %collective-permute-start.1 = (bf16[256,256]{1,0:T(8,128)(2,1)S(1)}, bf16[256,256]{1,0:T(8,128)(2,1)S(1)}, u32[]{:S(2)}, u32[]{:S(2)}) collective-permute-start(bf16[256,256]{1,0:T(8,128)(2,1)S(1)} %all_gather.21), channel_id=1, source_target_pairs={{0,320},{32,352},{64,384},{96,416},{128,448},{160,480},{192,0},{22... | collective-permute-start | bytes 393224 | tf_op jit(solution)/shard_map/ppermute | solution.py:406
  15.4 19.2 %collective-permute-start.2 = (bf16[528,128]{1,0:T(8,128)(2,1)}, bf16[528,128]{1,0:T(8,128)(2,1)S(1)}, u32[]{:S(2)}, u32[]{:S(2)}) collective-permute-start(bf16[528,128]{1,0:T(8,128)(2,1)} %chip_state.1.refs_0_), channel_id=1, source_target_pairs={{0,32},{32,64},{64,96},{96,128},{128,160},{160,192},{192,224},{224... | collective-permute-start | bytes 405512 | tf_op jit(solution)/shard_map/ppermute | solution.py:243
  16.7 17.9 %collective-permute-start.3 = (bf16[528,128]{1,0:T(8,128)(2,1)}, bf16[528,128]{1,0:T(8,128)(2,1)S(1)}, u32[]{:S(2)}, u32[]{:S(2)}) collective-permute-start(bf16[528,128]{1,0:T(8,128)(2,1)} %chip_state.1.refs_0_), channel_id=1, source_target_pairs={{0,96},{32,128},{64,160},{96,192},{128,224},{160,256},{192,288},{2... | collective-permute-start | bytes 405512 | tf_op jit(solution)/shard_map/ppermute | solution.py:244
  17.5 23.4 %copy-start.5 = (bf16[256,256]{1,0:T(8,128)(2,1)S(1)}, bf16[256,256]{1,0:T(8,128)(2,1)}, u32[]{:S(2)}) copy-start(bf16[256,256]{1,0:T(8,128)(2,1)} %get-tuple-element.24.kv_ref.refs_5_) | copy-start | bytes 393220
  22.4 22.6 %collective-permute-start.7 = (bf16[768,256]{1,0:T(8,128)(2,1)S(1)}, bf16[768,256]{1,0:T(8,128)(2,1)S(1)}, u32[]{:S(2)}, u32[]{:S(2)}) collective-permute-start(bf16[768,256]{1,0:T(8,128)(2,1)S(1)} %constant_dynamic-slice_fusion), channel_id=1, source_target_pairs={{0,64},{32,96},{64,128},{96,160},{128,192},{160,224},{192,256},{22... | collective-permute-start | bytes 1179656 | tf_op jit(solution)/shard_map/ppermute | solution.py:416
  24.7 23.1 %collective-permute-start.8 = (bf16[768,256]{1,0:T(8,128)(2,1)S(1)}, bf16[768,256]{1,0:T(8,128)(2,1)S(1)}, u32[]{:S(2)}, u32[]{:S(2)}) collective-permute-start(bf16[768,256]{1,0:T(8,128)(2,1)S(1)} %constant_dynamic-slice_fusion), channel_id=1, source_target_pairs={{0,32},{32,64},{64,96},{96,128},{128,160},{160,192},{192,224},{224... | collective-permute-start | bytes 1179656 | tf_op jit(solution)/shard_map/ppermute | solution.py:415
  31.8 9.1 %collective-permute-start.4 = (bf16[256,512]{1,0:T(8,128)(2,1)S(1)}, bf16[256,512]{1,0:T(8,128)(2,1)S(1)}, u32[]{:S(2)}, u32[]{:S(2)}) collective-permute-start(bf16[256,512]{1,0:T(8,128)(2,1)S(1)} %copy-done.9), channel_id=1, source_target_pairs={{0,1},{1,0},{2,3},{3,2},{4,5},{5,4},{6,7},{7,6},{8,9},{9,8},{10,11... | collective-permute-start | bytes 786440 | tf_op jit(solution)/shard_map/ppermute | solution.py:411
  39.0 18.7 %collective-permute-start.5 = (bf16[528,128]{1,0:T(8,128)(2,1)}, bf16[528,128]{1,0:T(8,128)(2,1)S(1)}, u32[]{:S(2)}, u32[]{:S(2)}) collective-permute-start(bf16[528,128]{1,0:T(8,128)(2,1)} %window_state.1), channel_id=1, source_target_pairs={{0,128},{32,160},{64,192},{96,224},{128,256},{160,288},{192,320},{... | collective-permute-start | bytes 405512 | tf_op jit(solution)/shard_map/ppermute | solution.py:243
  40.2 17.4 %collective-permute-start.6 = (bf16[528,128]{1,0:T(8,128)(2,1)}, bf16[528,128]{1,0:T(8,128)(2,1)S(1)}, u32[]{:S(2)}, u32[]{:S(2)}) collective-permute-start(bf16[528,128]{1,0:T(8,128)(2,1)} %window_state.1), channel_id=1, source_target_pairs={{0,384},{32,416},{64,448},{96,480},{1,385},{33,417},{65,449},{97,4... | collective-permute-start | bytes 405512 | tf_op jit(solution)/shard_map/ppermute | solution.py:244
  54.8 75.9 %copy-start = (bf16[2112,128]{1,0:T(8,128)(2,1)S(1)}, bf16[2112,128]{1,0:T(8,128)(2,1)}, u32[]{:S(2)}) copy-start(bf16[2112,128]{1,0:T(8,128)(2,1)} %all_gather.24.refs_1_.near_ref) | copy-start | bytes 1622020
  54.8 75.9 %copy-start.2 = (bf16[1056,128]{1,0:T(8,128)(2,1)S(1)}, bf16[1056,128]{1,0:T(8,128)(2,1)}, u32[]{:S(2)}) copy-start(bf16[1056,128]{1,0:T(8,128)(2,1)} %all_gather.22.refs_0_.both_ref) | copy-start | bytes 811012
  54.8 75.9 %copy-start.3 = (bf16[256,512]{1,0:T(8,128)(2,1)S(1)}, bf16[256,512]{1,0:T(8,128)(2,1)}, u32[]{:S(2)}) copy-start(bf16[256,512]{1,0:T(8,128)(2,1)} %keys_ref.4) | copy-start | bytes 786436
  54.8 75.8 %copy-start.4 = (bf16[256,512]{1,0:T(8,128)(2,1)S(1)}, bf16[256,512]{1,0:T(8,128)(2,1)}, u32[]{:S(2)}) copy-start(bf16[256,512]{1,0:T(8,128)(2,1)} %values_ref.5) | copy-start | bytes 786436
  54.8 75.8 %copy-start.6 = (bf16[256,512]{1,0:T(8,128)(2,1)S(1)}, bf16[256,512]{1,0:T(8,128)(2,1)}, u32[]{:S(2)}) copy-start(bf16[256,512]{1,0:T(8,128)(2,1)} %query_ref.2) | copy-start | bytes 786436
  54.8 75.8 %copy-start.7 = (f32[4,256]{1,0:T(4,128)S(1)}, f32[4,256]{1,0:T(4,128)}, u32[]{:S(2)}) copy-start(f32[4,256]{1,0:T(4,128)} %decay_ref.3) | copy-start | bytes 12292
  54.8 75.8 %copy-start.8 = (f32[512]{0:T(512)S(1)}, f32[512]{0:T(512)}, u32[]{:S(2)}) copy-start(f32[512]{0:T(512)} %param.12) | copy-start | bytes 6148
  54.8 78.4 %collective-permute-start.9 = (bf16[256,640]{1,0:T(8,128)(2,1)S(1)}, bf16[256,640]{1,0:T(8,128)(2,1)S(1)}, u32[]{:S(2)}, u32[]{:S(2)}) collective-permute-start(bf16[256,640]{1,0:T(8,128)(2,1)S(1)} %attend_rest.2), channel_id=1, source_target_pairs={{0,1},{1,0},{2,3},{3,2},{4,5},{5,4},{6,7},{7,6},{8,9},{9,8},{10,11... | collective-permute-start | bytes 983048 | tf_op jit(solution)/shard_map/ppermute | solution.py:464
  128.4 4.9 %copy-start.1 = (f32[256,640]{1,0:T(8,128)}, f32[256,640]{1,0:T(8,128)S(1)}, u32[]{:S(2)}) copy-start(f32[256,640]{1,0:T(8,128)S(1)} %attend_rest.3.mine_ref) | copy-start | bytes 1966084
  133.3 0.7 copy-start.10
